TPU v7x, 32 devices: a whole 2x2x4 slice. The times are simulated.
32 devices in a mesh: view: 2 (over x), fx: 4 (over y, core), fy: 4 (over z).
Axes of the slice: x: 2, y: 2, z: 4, core: 2. Of those that a mesh axis runs over, the one named last changes fastest.
Arguments:
- estimate: float32 [128, 128, 128], P('fx', 'fy'), may hold values from 0.25 to 30
- images: bfloat16 [6, 128, 128, 128], P('view', 'fx', 'fy'), may hold values from 0.1 to 30
- psf: float32 [6, 3, 31], P('view'), may hold values from 0.05 to 1
- cover_lo: int32 [6, 4, 4], P('view'), may hold values from 0 to 63
- cover_len: int32 [6, 4, 4], P('view'), may hold values from 32 to 64
Outputs:
- joined: float32 [128, 128, 128], P('fx', 'fy')
All inputs are finite; a program needn't handle non-finite values.
Results may differ from a plain program's by a relative error of at most 0.0003.
Values may be sent and summed in bfloat16 or wider, within the bound.
No kernel may reach another device: no remote copies, remote signals or barrier semaphores. Data moves between devices by JAX's collectives and lax.ppermute only.
A program may use at most 64 MiB of HBM per device.

v0:
```python
import jax
import jax.numpy as jnp
from jax import lax
from jax.sharding import PartitionSpec as P

ITERS = 2


def shift_pairs(peers):
    up = [(i, i + 1) for i in range(peers - 1)]
    return up, [(j, i) for i, j in up]


def gather_halo(array, axis, dim, width):
    up, down = shift_pairs(lax.axis_size(axis))
    length = array.shape[dim]
    last = lax.slice_in_dim(array, length - width, length, axis=dim)
    first = lax.slice_in_dim(array, 0, width, axis=dim)
    before = lax.ppermute(last, axis, up)
    after = lax.ppermute(first, axis, down)
    return jnp.concatenate([before, array, after], axis=dim)


def scatter_halo(array, axis, dim, width):
    up, down = shift_pairs(lax.axis_size(axis))
    length = array.shape[dim]
    head = lax.ppermute(lax.slice_in_dim(array, 0, width, axis=dim), axis, down)
    tail = lax.ppermute(lax.slice_in_dim(array, length - width, length, axis=dim), axis, up)
    centre = lax.slice_in_dim(array, width, length - width, axis=dim)
    inner = [(0, 0, 0)] * array.ndim
    inner[dim] = (0, length - 3 * width, 0)
    outer = [(0, 0, 0)] * array.ndim
    outer[dim] = (length - 3 * width, 0, 0)
    zero = jnp.zeros((), array.dtype)
    return centre + lax.pad(tail, zero, inner) + lax.pad(head, zero, outer)


def band(weights, rows, cols, shift):
    taps = weights.shape[-1]
    gap = (
        jnp.arange(cols, dtype=jnp.int32)[None, :]
        - jnp.arange(rows, dtype=jnp.int32)[:, None]
        + shift
    )
    picks = (gap[:, :, None] == jnp.arange(taps, dtype=jnp.int32)).astype(jnp.float32)
    return jnp.einsum("oit,gt->goi", picks, weights, precision=lax.Precision.HIGHEST)


def block_sums(weights, axis, cells):
    blocks = lax.axis_size(axis)
    taps = weights.shape[-1]
    place = lax.axis_index(axis) * cells + jnp.arange(cells, dtype=jnp.int32)
    source = place[:, None] - jnp.arange(taps, dtype=jnp.int32)[None, :] + (taps - 1) // 2
    first = jnp.arange(blocks, dtype=jnp.int32)[:, None, None] * cells
    picks = ((source[None] >= first) & (source[None] < first + cells)).astype(jnp.float32)
    return jnp.einsum("bot,gt->ogb", picks, weights, precision=lax.Precision.HIGHEST)


def weight_of(kern, low, span, cells_x, cells_y, depth):
    views = kern.shape[0]
    taps = kern.shape[-1]
    sums_x = block_sums(kern[:, 0], "fx", cells_x)
    sums_y = block_sums(kern[:, 1], "fy", cells_y)
    levels = jnp.arange(depth, dtype=jnp.int32)
    inside = (levels >= low[..., None]) & (levels < (low + span)[..., None])
    table_z = band(kern[:, 2], depth, depth, (taps - 1) // 2)
    sums_z = jnp.einsum(
        "gxyi,gio->gxyo", inside.astype(jnp.float32), table_z, precision=lax.Precision.HIGHEST
    )
    plane = sums_x[:, None, :, :, None] * sums_y[None, :, :, None, :]
    plane = plane.reshape(cells_x, cells_y, -1)
    return jnp.einsum(
        "xym,mz->xyz", plane, sums_z.reshape(-1, depth), precision=lax.Precision.HIGHEST
    )


def body(estimate, images, psf, cover_lo, cover_len):
    group, cells_x, cells_y, depth = images.shape
    taps = psf.shape[-1]
    radius = (taps - 1) // 2
    halo = min(-(-radius // 16) * 16, cells_x, cells_y)
    exact = lax.Precision.HIGH
    groups = lax.axis_size("view")
    swap = [(i, (i + 1) % groups) for i in range(groups)]

    kern = psf / jnp.sum(psf, axis=-1, keepdims=True)
    pack = jnp.concatenate(
        [kern.reshape(-1), cover_lo.reshape(-1).astype(jnp.float32), cover_len.reshape(-1).astype(jnp.float32)]
    )
    packs = [pack]
    for _ in range(groups - 1):
        packs.append(lax.ppermute(packs[-1], "view", swap))
    packs = jnp.stack(packs)
    all_kern = packs[:, : kern.size].reshape((-1,) + kern.shape[1:])
    cells = cover_lo.size
    all_low = packs[:, kern.size : kern.size + cells].astype(jnp.int32).reshape((-1,) + cover_lo.shape[1:])
    all_span = packs[:, kern.size + cells :].astype(jnp.int32).reshape((-1,) + cover_len.shape[1:])
    lower_part = weight_of(all_kern, all_low, all_span, cells_x, cells_y, depth) + 0.5

    block_x, block_y = lax.axis_index("fx"), lax.axis_index("fy")
    low = lax.dynamic_slice(cover_lo, (0, block_x, block_y), (group, 1, 1))[..., None]
    span = lax.dynamic_slice(cover_len, (0, block_x, block_y), (group, 1, 1))[..., None]
    levels = jnp.arange(depth, dtype=jnp.int32)
    own = (levels >= low) & (levels < low + span)
    masked = jnp.where(own, images, jnp.zeros_like(images)).astype(jnp.float32)

    table_x = band(kern[:, 0], cells_x, cells_x + 2 * halo, radius - halo)
    table_y = band(kern[:, 1], cells_y, cells_y + 2 * halo, radius - halo)
    table_z = band(kern[:, 2], depth, depth, radius)

    joined = estimate
    for step in range(ITERS):
        wide = gather_halo(joined.astype(jnp.bfloat16), "fy", 1, halo)
        wide = gather_halo(wide, "fx", 0, halo).astype(jnp.float32)
        field = jnp.einsum("gox,xyz->goyz", table_x, wide, precision=exact)
        field = jnp.einsum("goy,gxyz->gxoz", table_y, field, precision=exact)
        blurred = jnp.einsum("goz,gxyz->gxyo", table_z, field, precision=exact)
        ratio = masked / blurred
        field = jnp.einsum("goz,gxyo->gxyz", table_z, ratio, precision=exact)
        field = jnp.einsum("goy,gxoz->gxyz", table_y, field, precision=exact)
        field = jnp.einsum("gox,goyz->xyz", table_x, field, precision=exact)
        field = scatter_halo(field, "fx", 0, halo)
        field = scatter_halo(field, "fy", 1, halo)
        correction = field
        moving = field
        for _ in range(groups - 1):
            moving = lax.ppermute(moving, "view", swap)
            correction = correction + moving
        joined = joined * (correction + 0.5) / lower_part
    return joined


def solution(mesh):
    return jax.shard_map(
        body,
        mesh=mesh,
        in_specs=(
            P("fx", "fy", None),
            P("view", "fx", "fy", None),
            P("view", None, None),
            P("view", None, None),
            P("view", None, None),
        ),
        out_specs=P("fx", "fy", None),
        check_vma=False,
    )
```

profile of v0, /device:TPU:1, one launch (start us, length us, event | category | flops | bytes accessed | tf_op | source)
XLA Modules:
  0.0 140.5 jit_solution(11320959746817942028)
XLA Ops:
  6.7 3.2 %collective-permute-start = (bf16[32,16,128]{2,0,1:T(8,128)(2,1)S(1)}, bf16[32,16,128]{2,0,1:T(8,128)(2,1)S(1)}, u32[]{:S(2)}, u32[]{:S(2)}) collective-permute-start(bf16[32,16,128]{2,0,1:T(8,128)(2,1)S(1)} %get-tuple-element.21), channel_id=1, source_target_pairs={{0,1},{1,2},{2,3},{4,5},{5,6},{6,7},{8,9},{9,10},{10,11},{12,13},{... | collective-permute-start | bytes 393224 | tf_op jit(solution)/shard_map/ppermute | solution.py:19
  15.8 5.4 %collective-permute-start.2 = (bf16[16,64,128]{2,0,1:T(8,128)(2,1)S(1)}, bf16[16,64,128]{2,0,1:T(8,128)(2,1)S(1)}, u32[]{:S(2)}, u32[]{:S(2)}) collective-permute-start(bf16[16,64,128]{2,0,1:T(8,128)(2,1)S(1)} %get-tuple-element.17), channel_id=1, source_target_pairs={{0,4},{4,8},{8,12},{1,5},{5,9},{9,13},{2,6},{6,10},{10,14},{3,7},{... | collective-permute-start | bytes 786440 | tf_op jit(solution)/shard_map/ppermute | solution.py:19
  24.5 4.4 %collective-permute-done.3 = bf16[16,64,128]{2,0,1:T(8,128)(2,1)S(1)} collective-permute-done((bf16[16,64,128]{2,0,1:T(8,128)(2,1)S(1)}, bf16[16,64,128]{2,0,1:T(8,128)(2,1)S(1)}, u32[]{:S(2)}, u32[]{:S(2)}) %collective-permute-start.3) | collective-permute-done | bytes 262176 | tf_op jit(solution)/shard_map/ppermute | solution.py:20
  29.9 2.7 %fusion.6 = f32[3,32,128,32]{2,3,1,0:T(8,128)S(1)} fusion(f32[3,32,64,128]{3,1,2,0:T(8,128)S(1)} %fusion.31, f32[3,32,64,1]{2,0,1,3:T(4,128)S(1)} %convolution_bitcast_fusion.2), kind=kOutput, calls=%fused_computation.6 | convolution fusion | flops 150994944 | bytes 4743168 | tf_op jit(solution)/shard_map/goy,gxyz->gxoz/dot_general | solution.py:116
  36.1 2.8 %fusion.12 = f32[64,64,128]{2,0,1:T(8,128)S(1)} fusion(f32[3,32,64,128]{3,2,1,0:T(8,128)S(1)} %convolution_bitcast_fusion.1, f32[3,32,64]{2,0,1:T(4,128)S(1)} %fusion.55), kind=kOutput, calls=%fused_computation.17 | convolution fusion | flops 301989888 | bytes 5267456 | tf_op jit(solution)/shard_map/gox,goyz->xyz/dot_general | solution.py:121
  41.7 2.4 %collective-permute-start.5 = (f32[16,64,128]{2,0,1:T(8,128)S(1)}, f32[16,64,128]{2,0,1:T(8,128)}, u32[]{:S(2)}, u32[]{:S(2)}) collective-permute-start(f32[16,64,128]{2,0,1:T(8,128)S(1)} %get-tuple-element.10), channel_id=1, source_target_pairs={{4,0},{8,4},{12,8},{5,1},{9,5},{13,9},{6,2},{10,6},{14,10},{7,3},{... | collective-permute-start | bytes 1572872 | tf_op jit(solution)/shard_map/ppermute | solution.py:27
  49.2 3.1 %collective-permute-done.5 = f32[16,64,128]{2,0,1:T(8,128)} collective-permute-done((f32[16,64,128]{2,0,1:T(8,128)S(1)}, f32[16,64,128]{2,0,1:T(8,128)}, u32[]{:S(2)}, u32[]{:S(2)}) %collective-permute-start.5) | collective-permute-done | bytes 524320 | tf_op jit(solution)/shard_map/ppermute | solution.py:27
  53.8 3.2 %collective-permute-start.6 = (f32[32,16,128]{2,0,1:T(8,128)S(1)}, f32[32,16,128]{2,0,1:T(8,128)S(1)}, u32[]{:S(2)}, u32[]{:S(2)}) collective-permute-start(f32[32,16,128]{2,0,1:T(8,128)S(1)} %get-tuple-element.13), channel_id=1, source_target_pairs={{0,1},{1,2},{2,3},{4,5},{5,6},{6,7},{8,9},{9,10},{10,11},{12,13},{... | collective-permute-start | bytes 786440 | tf_op jit(solution)/shard_map/ppermute | solution.py:28
  60.4 3.7 %collective-permute-done.7 = f32[32,16,128]{2,0,1:T(8,128)S(1)} collective-permute-done((f32[32,16,128]{2,0,1:T(8,128)S(1)}, f32[32,16,128]{2,0,1:T(8,128)S(1)}, u32[]{:S(2)}, u32[]{:S(2)}) %collective-permute-start.7) | collective-permute-done | bytes 262176 | tf_op jit(solution)/shard_map/ppermute | solution.py:27
  65.2 2.8 %fusion.25 = f32[32,32,128]{2,1,0:T(8,128)S(1)} fusion(f32[32,6,4]{0,1,2:T(8,128)S(1)} %convolution_bitcast_fusion.4, f32[32,6,4]{1,0,2:T(8,128)S(1)} %copy.50, f32[6,4,4,128,1]{3,2,1,0,4:T(4,128)S(1)} %convolution_bitcast_fusion.3), kind=kOutput, calls=%fused_computation.26 | convolution fusion | flops 151093248 | bytes 579584 | tf_op jit(solution)/shard_map/xym,mz->xyz/dot_general | solution.py:72
  68.1 8.1 %collective-permute-done.8 = f32[32,32,128]{2,0,1:T(8,128)S(1)} collective-permute-done((f32[32,32,128]{2,0,1:T(8,128)S(1)}, f32[32,32,128]{2,0,1:T(8,128)S(1)}, u32[]{:S(2)}, u32[]{:S(2)}) %collective-permute-start.8) | collective-permute-done | bytes 524320 | tf_op jit(solution)/shard_map/ppermute | solution.py:127
  76.8 3.2 %collective-permute-start.10 = (bf16[32,16,128]{2,0,1:T(8,128)(2,1)S(1)}, bf16[32,16,128]{2,0,1:T(8,128)(2,1)S(1)}, u32[]{:S(2)}, u32[]{:S(2)}) collective-permute-start(bf16[32,16,128]{2,0,1:T(8,128)(2,1)S(1)} %get-tuple-element.19), channel_id=1, source_target_pairs={{0,1},{1,2},{2,3},{4,5},{5,6},{6,7},{8,9},{9,10},{10,11},{12,13},{... | collective-permute-start | bytes 393224 | tf_op jit(solution)/shard_map/ppermute | solution.py:19
  82.6 4.1 %collective-permute-done.11 = bf16[32,16,128]{2,0,1:T(8,128)(2,1)S(1)} collective-permute-done((bf16[32,16,128]{2,0,1:T(8,128)(2,1)S(1)}, bf16[32,16,128]{2,0,1:T(8,128)(2,1)S(1)}, u32[]{:S(2)}, u32[]{:S(2)}) %collective-permute-start.11) | collective-permute-done | bytes 131104 | tf_op jit(solution)/shard_map/ppermute | solution.py:20
  86.8 2.2 %collective-permute-start.12 = (bf16[16,64,128]{2,0,1:T(8,128)(2,1)S(1)}, bf16[16,64,128]{2,0,1:T(8,128)(2,1)S(1)}, u32[]{:S(2)}, u32[]{:S(2)}) collective-permute-start(bf16[16,64,128]{2,0,1:T(8,128)(2,1)S(1)} %get-tuple-element.15), channel_id=1, source_target_pairs={{0,4},{4,8},{8,12},{1,5},{5,9},{9,13},{2,6},{6,10},{10,14},{3,7},{... | collective-permute-start | bytes 786440 | tf_op jit(solution)/shard_map/ppermute | solution.py:19
  89.0 2.1 %collective-permute-start.13 = (bf16[16,64,128]{2,0,1:T(8,128)(2,1)S(1)}, bf16[16,64,128]{2,0,1:T(8,128)(2,1)S(1)}, u32[]{:S(2)}, u32[]{:S(2)}) collective-permute-start(bf16[16,64,128]{2,0,1:T(8,128)(2,1)S(1)} %get-tuple-element.16), channel_id=1, source_target_pairs={{4,0},{8,4},{12,8},{5,1},{9,5},{13,9},{6,2},{10,6},{14,10},{7,3},{... | collective-permute-start | bytes 786440 | tf_op jit(solution)/shard_map/ppermute | solution.py:20
  92.3 4.4 %collective-permute-done.13 = bf16[16,64,128]{2,0,1:T(8,128)(2,1)S(1)} collective-permute-done((bf16[16,64,128]{2,0,1:T(8,128)(2,1)S(1)}, bf16[16,64,128]{2,0,1:T(8,128)(2,1)S(1)}, u32[]{:S(2)}, u32[]{:S(2)}) %collective-permute-start.13) | collective-permute-done | bytes 262176 | tf_op jit(solution)/shard_map/ppermute | solution.py:20
  97.7 2.7 %fusion.2 = f32[3,32,128,32]{2,3,1,0:T(8,128)S(1)} fusion(f32[3,32,64,128]{3,1,2,0:T(8,128)S(1)} %fusion.40, f32[3,32,64,1]{2,0,1,3:T(4,128)S(1)} %convolution_bitcast_fusion.2), kind=kOutput, calls=%fused_computation.2 | convolution fusion | flops 150994944 | bytes 4743168 | tf_op jit(solution)/shard_map/goy,gxyz->gxoz/dot_general | solution.py:116
  103.9 2.8 %fusion.15 = f32[64,64,128]{2,0,1:T(8,128)S(1)} fusion(f32[3,32,64,128]{3,2,1,0:T(8,128)S(1)} %convolution_bitcast_fusion, f32[3,32,64]{2,0,1:T(4,128)S(1)} %copy-done.3), kind=kOutput, calls=%fused_computation.18 | convolution fusion | flops 301989888 | bytes 5267456 | tf_op jit(solution)/shard_map/gox,goyz->xyz/dot_general | solution.py:121
  108.8 2.4 %collective-permute-start.15 = (f32[16,64,128]{2,0,1:T(8,128)S(1)}, f32[16,64,128]{2,0,1:T(8,128)S(1)}, u32[]{:S(2)}, u32[]{:S(2)}) collective-permute-start(f32[16,64,128]{2,0,1:T(8,128)S(1)} %get-tuple-element.8), channel_id=1, source_target_pairs={{4,0},{8,4},{12,8},{5,1},{9,5},{13,9},{6,2},{10,6},{14,10},{7,3},{... | collective-permute-start | bytes 1572872 | tf_op jit(solution)/shard_map/ppermute | solution.py:27
  111.2 3.7 %collective-permute-done.14 = f32[16,64,128]{2,0,1:T(8,128)S(1)} collective-permute-done((f32[16,64,128]{2,0,1:T(8,128)S(1)}, f32[16,64,128]{2,0,1:T(8,128)S(1)}, u32[]{:S(2)}, u32[]{:S(2)}) %collective-permute-start.14) | collective-permute-done | bytes 524320 | tf_op jit(solution)/shard_map/ppermute | solution.py:28
  114.9 4.4 %collective-permute-done.15 = f32[16,64,128]{2,0,1:T(8,128)S(1)} collective-permute-done((f32[16,64,128]{2,0,1:T(8,128)S(1)}, f32[16,64,128]{2,0,1:T(8,128)S(1)}, u32[]{:S(2)}, u32[]{:S(2)}) %collective-permute-start.15) | collective-permute-done | bytes 524320 | tf_op jit(solution)/shard_map/ppermute | solution.py:27
  119.5 3.2 %collective-permute-start.16 = (f32[32,16,128]{2,0,1:T(8,128)S(1)}, f32[32,16,128]{2,0,1:T(8,128)S(1)}, u32[]{:S(2)}, u32[]{:S(2)}) collective-permute-start(f32[32,16,128]{2,0,1:T(8,128)S(1)} %get-tuple-element.11), channel_id=1, source_target_pairs={{0,1},{1,2},{2,3},{4,5},{5,6},{6,7},{8,9},{9,10},{10,11},{12,13},{... | collective-permute-start | bytes 786440 | tf_op jit(solution)/shard_map/ppermute | solution.py:28
  125.9 4.1 %collective-permute-done.17 = f32[32,16,128]{2,0,1:T(8,128)S(1)} collective-permute-done((f32[32,16,128]{2,0,1:T(8,128)S(1)}, f32[32,16,128]{2,0,1:T(8,128)S(1)}, u32[]{:S(2)}, u32[]{:S(2)}) %collective-permute-start.17) | collective-permute-done | bytes 262176 | tf_op jit(solution)/shard_map/ppermute | solution.py:27
  130.5 8.5 %collective-permute-done.18 = f32[32,32,128]{2,0,1:T(8,128)S(1)} collective-permute-done((f32[32,32,128]{2,0,1:T(8,128)S(1)}, f32[32,32,128]{2,0,1:T(8,128)S(1)}, u32[]{:S(2)}, u32[]{:S(2)}) %collective-permute-start.18) | collective-permute-done | bytes 524320 | tf_op jit(solution)/shard_map/ppermute | solution.py:127
  (112 shorter events, 50.1 us)
Async XLA Ops:
  3.3 41.5 %collective-permute-start.9 = (f32[375]{0:T(512)S(1)}, f32[375]{0:T(512)}, u32[]{:S(2)}, u32[]{:S(2)}) collective-permute-start(f32[375]{0:T(512)S(1)} %pad_maximum_fusion.2), channel_id=1, source_target_pairs={{0,16},{16,0},{1,17},{17,1},{2,18},{18,2},{3,19},{19,3},{4,20},{20... | collective-permute-start | bytes 4508 | tf_op jit(solution)/shard_map/ppermute | solution.py:92
  6.7 8.6 %collective-permute-start = (bf16[32,16,128]{2,0,1:T(8,128)(2,1)S(1)}, bf16[32,16,128]{2,0,1:T(8,128)(2,1)S(1)}, u32[]{:S(2)}, u32[]{:S(2)}) collective-permute-start(bf16[32,16,128]{2,0,1:T(8,128)(2,1)S(1)} %get-tuple-element.21), channel_id=1, source_target_pairs={{0,1},{1,2},{2,3},{4,5},{5,6},{6,7},{8,9},{9,10},{10,11},{12,13},{... | collective-permute-start | bytes 393224 | tf_op jit(solution)/shard_map/ppermute | solution.py:19
  9.9 5.7 %collective-permute-start.1 = (bf16[32,16,128]{2,0,1:T(8,128)(2,1)S(1)}, bf16[32,16,128]{2,0,1:T(8,128)(2,1)S(1)}, u32[]{:S(2)}, u32[]{:S(2)}) collective-permute-start(bf16[32,16,128]{2,0,1:T(8,128)(2,1)S(1)} %get-tuple-element.22), channel_id=1, source_target_pairs={{1,0},{2,1},{3,2},{5,4},{6,5},{7,6},{9,8},{10,9},{11,10},{13,12},{... | collective-permute-start | bytes 393224 | tf_op jit(solution)/shard_map/ppermute | solution.py:20
  13.2 20.2 %copy-start.9 = (pred[3,128]{1,0:T(4,128)(4,1)}, pred[3,128]{1,0:T(4,128)(4,1)S(1)}, u32[]{:S(2)}) copy-start(pred[3,128]{1,0:T(4,128)(4,1)S(1)} %fusion.99) | copy-start | bytes 1156
  15.8 8.7 %collective-permute-start.2 = (bf16[16,64,128]{2,0,1:T(8,128)(2,1)S(1)}, bf16[16,64,128]{2,0,1:T(8,128)(2,1)S(1)}, u32[]{:S(2)}, u32[]{:S(2)}) collective-permute-start(bf16[16,64,128]{2,0,1:T(8,128)(2,1)S(1)} %get-tuple-element.17), channel_id=1, source_target_pairs={{0,4},{4,8},{8,12},{1,5},{5,9},{9,13},{2,6},{6,10},{10,14},{3,7},{... | collective-permute-start | bytes 786440 | tf_op jit(solution)/shard_map/ppermute | solution.py:19
  21.2 7.7 %collective-permute-start.3 = (bf16[16,64,128]{2,0,1:T(8,128)(2,1)S(1)}, bf16[16,64,128]{2,0,1:T(8,128)(2,1)S(1)}, u32[]{:S(2)}, u32[]{:S(2)}) collective-permute-start(bf16[16,64,128]{2,0,1:T(8,128)(2,1)S(1)} %get-tuple-element.18), channel_id=1, source_target_pairs={{4,0},{8,4},{12,8},{5,1},{9,5},{13,9},{6,2},{10,6},{14,10},{7,3},{... | collective-permute-start | bytes 786440 | tf_op jit(solution)/shard_map/ppermute | solution.py:20
  23.7 12.4 %copy-start.2 = (f32[3,32,64]{2,0,1:T(4,128)}, f32[3,32,64]{2,0,1:T(4,128)S(1)}, u32[]{:S(2)}) copy-start(f32[3,32,64]{2,0,1:T(4,128)S(1)} %fusion.55) | copy-start | bytes 73732
  39.8 8.6 %collective-permute-start.4 = (f32[16,64,128]{2,0,1:T(8,128)}, f32[16,64,128]{2,0,1:T(8,128)S(1)}, u32[]{:S(2)}, u32[]{:S(2)}) collective-permute-start(f32[16,64,128]{2,0,1:T(8,128)} %get-tuple-element.9), channel_id=1, source_target_pairs={{0,4},{4,8},{8,12},{1,5},{5,9},{9,13},{2,6},{6,10},{10,14},{3,7},{... | collective-permute-start | bytes 1572872 | tf_op jit(solution)/shard_map/ppermute | solution.py:28
  41.7 10.6 %collective-permute-start.5 = (f32[16,64,128]{2,0,1:T(8,128)S(1)}, f32[16,64,128]{2,0,1:T(8,128)}, u32[]{:S(2)}, u32[]{:S(2)}) collective-permute-start(f32[16,64,128]{2,0,1:T(8,128)S(1)} %get-tuple-element.10), channel_id=1, source_target_pairs={{4,0},{8,4},{12,8},{5,1},{9,5},{13,9},{6,2},{10,6},{14,10},{7,3},{... | collective-permute-start | bytes 1572872 | tf_op jit(solution)/shard_map/ppermute | solution.py:27
  53.7 11.2 %copy-start.4 = (s32[32,31]{1,0:T(8,128)S(1)}, s32[32,31]{1,0:T(8,128)}, u32[]{:S(2)}) copy-start(s32[32,31]{1,0:T(8,128)} %subtract_add_fusion.1) | copy-start | bytes 11908
  53.8 6.6 %collective-permute-start.6 = (f32[32,16,128]{2,0,1:T(8,128)S(1)}, f32[32,16,128]{2,0,1:T(8,128)S(1)}, u32[]{:S(2)}, u32[]{:S(2)}) collective-permute-start(f32[32,16,128]{2,0,1:T(8,128)S(1)} %get-tuple-element.13), channel_id=1, source_target_pairs={{0,1},{1,2},{2,3},{4,5},{5,6},{6,7},{8,9},{9,10},{10,11},{12,13},{... | collective-permute-start | bytes 786440 | tf_op jit(solution)/shard_map/ppermute | solution.py:28
  57.0 7.1 %collective-permute-start.7 = (f32[32,16,128]{2,0,1:T(8,128)S(1)}, f32[32,16,128]{2,0,1:T(8,128)S(1)}, u32[]{:S(2)}, u32[]{:S(2)}) collective-permute-start(f32[32,16,128]{2,0,1:T(8,128)S(1)} %get-tuple-element.14), channel_id=1, source_target_pairs={{1,0},{2,1},{3,2},{5,4},{6,5},{7,6},{9,8},{10,9},{11,10},{13,12},{... | collective-permute-start | bytes 786440 | tf_op jit(solution)/shard_map/ppermute | solution.py:27
  64.2 11.9 %copy-start = (f32[32,32,128]{2,1,0:T(8,128)S(1)}, f32[32,32,128]{2,1,0:T(8,128)}, u32[]{:S(2)}) copy-start(f32[32,32,128]{2,1,0:T(8,128)} %param.5) | copy-start | bytes 1572868
  64.2 11.9 %collective-permute-start.8 = (f32[32,32,128]{2,0,1:T(8,128)S(1)}, f32[32,32,128]{2,0,1:T(8,128)S(1)}, u32[]{:S(2)}, u32[]{:S(2)}) collective-permute-start(f32[32,32,128]{2,0,1:T(8,128)S(1)} %fusion.54), channel_id=1, source_target_pairs={{0,16},{16,0},{1,17},{17,1},{2,18},{18,2},{3,19},{19,3},{4,20},{20... | collective-permute-start | bytes 1572872 | tf_op jit(solution)/shard_map/ppermute | solution.py:127
  68.0 28.7 %copy-start.3 = (f32[3,32,64]{2,0,1:T(4,128)S(1)}, f32[3,32,64]{2,0,1:T(4,128)}, u32[]{:S(2)}) copy-start(f32[3,32,64]{2,0,1:T(4,128)} %copy-done.2) | copy-start | bytes 73732
  76.8 5.7 %collective-permute-start.10 = (bf16[32,16,128]{2,0,1:T(8,128)(2,1)S(1)}, bf16[32,16,128]{2,0,1:T(8,128)(2,1)S(1)}, u32[]{:S(2)}, u32[]{:S(2)}) collective-permute-start(bf16[32,16,128]{2,0,1:T(8,128)(2,1)S(1)} %get-tuple-element.19), channel_id=1, source_target_pairs={{0,1},{1,2},{2,3},{4,5},{5,6},{6,7},{8,9},{9,10},{10,11},{12,13},{... | collective-permute-start | bytes 393224 | tf_op jit(solution)/shard_map/ppermute | solution.py:19
  80.1 6.6 %collective-permute-start.11 = (bf16[32,16,128]{2,0,1:T(8,128)(2,1)S(1)}, bf16[32,16,128]{2,0,1:T(8,128)(2,1)S(1)}, u32[]{:S(2)}, u32[]{:S(2)}) collective-permute-start(bf16[32,16,128]{2,0,1:T(8,128)(2,1)S(1)} %get-tuple-element.20), channel_id=1, source_target_pairs={{1,0},{2,1},{3,2},{5,4},{6,5},{7,6},{9,8},{10,9},{11,10},{13,12},{... | collective-permute-start | bytes 393224 | tf_op jit(solution)/shard_map/ppermute | solution.py:20
  86.8 5.5 %collective-permute-start.12 = (bf16[16,64,128]{2,0,1:T(8,128)(2,1)S(1)}, bf16[16,64,128]{2,0,1:T(8,128)(2,1)S(1)}, u32[]{:S(2)}, u32[]{:S(2)}) collective-permute-start(bf16[16,64,128]{2,0,1:T(8,128)(2,1)S(1)} %get-tuple-element.15), channel_id=1, source_target_pairs={{0,4},{4,8},{8,12},{1,5},{5,9},{9,13},{2,6},{6,10},{10,14},{3,7},{... | collective-permute-start | bytes 786440 | tf_op jit(solution)/shard_map/ppermute | solution.py:19
  89.0 7.7 %collective-permute-start.13 = (bf16[16,64,128]{2,0,1:T(8,128)(2,1)S(1)}, bf16[16,64,128]{2,0,1:T(8,128)(2,1)S(1)}, u32[]{:S(2)}, u32[]{:S(2)}) collective-permute-start(bf16[16,64,128]{2,0,1:T(8,128)(2,1)S(1)} %get-tuple-element.16), channel_id=1, source_target_pairs={{4,0},{8,4},{12,8},{5,1},{9,5},{13,9},{6,2},{10,6},{14,10},{7,3},{... | collective-permute-start | bytes 786440 | tf_op jit(solution)/shard_map/ppermute | solution.py:20
  106.8 8.0 %collective-permute-start.14 = (f32[16,64,128]{2,0,1:T(8,128)S(1)}, f32[16,64,128]{2,0,1:T(8,128)S(1)}, u32[]{:S(2)}, u32[]{:S(2)}) collective-permute-start(f32[16,64,128]{2,0,1:T(8,128)S(1)} %get-tuple-element.7), channel_id=1, source_target_pairs={{0,4},{4,8},{8,12},{1,5},{5,9},{9,13},{2,6},{6,10},{10,14},{3,7},{... | collective-permute-start | bytes 1572872 | tf_op jit(solution)/shard_map/ppermute | solution.py:28
  108.8 10.5 %collective-permute-start.15 = (f32[16,64,128]{2,0,1:T(8,128)S(1)}, f32[16,64,128]{2,0,1:T(8,128)S(1)}, u32[]{:S(2)}, u32[]{:S(2)}) collective-permute-start(f32[16,64,128]{2,0,1:T(8,128)S(1)} %get-tuple-element.8), channel_id=1, source_target_pairs={{4,0},{8,4},{12,8},{5,1},{9,5},{13,9},{6,2},{10,6},{14,10},{7,3},{... | collective-permute-start | bytes 1572872 | tf_op jit(solution)/shard_map/ppermute | solution.py:27
  119.5 6.5 %collective-permute-start.16 = (f32[32,16,128]{2,0,1:T(8,128)S(1)}, f32[32,16,128]{2,0,1:T(8,128)S(1)}, u32[]{:S(2)}, u32[]{:S(2)}) collective-permute-start(f32[32,16,128]{2,0,1:T(8,128)S(1)} %get-tuple-element.11), channel_id=1, source_target_pairs={{0,1},{1,2},{2,3},{4,5},{5,6},{6,7},{8,9},{9,10},{10,11},{12,13},{... | collective-permute-start | bytes 786440 | tf_op jit(solution)/shard_map/ppermute | solution.py:28
  122.7 7.4 %collective-permute-start.17 = (f32[32,16,128]{2,0,1:T(8,128)S(1)}, f32[32,16,128]{2,0,1:T(8,128)S(1)}, u32[]{:S(2)}, u32[]{:S(2)}) collective-permute-start(f32[32,16,128]{2,0,1:T(8,128)S(1)} %get-tuple-element.12), channel_id=1, source_target_pairs={{1,0},{2,1},{3,2},{5,4},{6,5},{7,6},{9,8},{10,9},{11,10},{13,12},{... | collective-permute-start | bytes 786440 | tf_op jit(solution)/shard_map/ppermute | solution.py:27
  130.2 8.8 %collective-permute-start.18 = (f32[32,32,128]{2,0,1:T(8,128)S(1)}, f32[32,32,128]{2,0,1:T(8,128)S(1)}, u32[]{:S(2)}, u32[]{:S(2)}) collective-permute-start(f32[32,32,128]{2,0,1:T(8,128)S(1)} %fusion.53), channel_id=1, source_target_pairs={{0,16},{16,0},{1,17},{17,1},{2,18},{18,2},{3,19},{19,3},{4,20},{20... | collective-permute-start | bytes 1572872 | tf_op jit(solution)/shard_map/ppermute | solution.py:127
  (10 other events, 68.1 us)
where the time goes:
time: 142 us; the launch traced here: 141 us
  waiting for transfers between devices  53.9 us (38%)
  starting transfers between devices  41.2 us (29%)
  matrix products  25.2 us (18%)
  local copies, waits for them, and re-layouts  10.8 us (8%)
  other arithmetic  8.81 us (6%)
    ppermute x2, waiting for transfers between devices, body(): moving = lax.ppermute(moving, 'view', swap)  16.6 us
    ppermute x4, waiting for transfers between devices, scatter_halo(): head = lax.ppermute(lax.slice_in_dim(array, 0, width, axis=dim), axis, down)  15.3 us
    ppermute x4, starting transfers between devices, gather_halo(): before = lax.ppermute(last, axis, up)  14 us
    ppermute x4, waiting for transfers between devices, gather_halo(): after = lax.ppermute(first, axis, down)  13.2 us
    ppermute x4, starting transfers between devices, scatter_halo(): lax.ppermute(lax.slice_in_dim(array, length - width, length, axis=dim), a...  10.2 us
    ppermute x4, starting transfers between devices, scatter_halo(): head = lax.ppermute(lax.slice_in_dim(array, 0, width, axis=dim), axis, down)  7.64 us
    ppermute x4, starting transfers between devices, gather_halo(): after = lax.ppermute(first, axis, down)  6.65 us
    dot_general x2, matrix products, body(): field = jnp.einsum('gox,goyz->xyz', table_x, field, precision=exact)  5.66 us
  transfers between devices with their start and end apart: 19, of which 15 were waited for; matrix products, arithmetic and copies ran while one was open for 19% of the time, Pallas kernels for 0%

commit v1 on v0

--- a/solution.py
+++ b/solution.py
@@ -6,33 +6,39 @@
 ITERS = 2
 
 
-def shift_pairs(peers):
-    up = [(i, i + 1) for i in range(peers - 1)]
-    return up, [(j, i) for i, j in up]
+def swap_edges(to_below, to_above, axis):
+    peers = lax.axis_size(axis)
+    even = lax.axis_index(axis) % 2 == 0
+
+    def pairs(start):
+        out = []
+        for i in range(start, peers - 1, 2):
+            out += [(i, i + 1), (i + 1, i)]
+        return out
+
+    first = lax.ppermute(jnp.where(even, to_above, to_below), axis, pairs(0))
+    second = lax.ppermute(jnp.where(even, to_below, to_above), axis, pairs(1))
+    return jnp.where(even, second, first), jnp.where(even, first, second)
 
 
 def gather_halo(array, axis, dim, width):
-    up, down = shift_pairs(lax.axis_size(axis))
     length = array.shape[dim]
-    last = lax.slice_in_dim(array, length - width, length, axis=dim)
-    first = lax.slice_in_dim(array, 0, width, axis=dim)
-    before = lax.ppermute(last, axis, up)
-    after = lax.ppermute(first, axis, down)
+    before, after = swap_edges(
+        lax.slice_in_dim(array, 0, width, axis=dim),
+        lax.slice_in_dim(array, length - width, length, axis=dim),
+        axis,
+    )
     return jnp.concatenate([before, array, after], axis=dim)
 
 
-def scatter_halo(array, axis, dim, width):
-    up, down = shift_pairs(lax.axis_size(axis))
-    length = array.shape[dim]
-    head = lax.ppermute(lax.slice_in_dim(array, 0, width, axis=dim), axis, down)
-    tail = lax.ppermute(lax.slice_in_dim(array, length - width, length, axis=dim), axis, up)
-    centre = lax.slice_in_dim(array, width, length - width, axis=dim)
-    inner = [(0, 0, 0)] * array.ndim
-    inner[dim] = (0, length - 3 * width, 0)
-    outer = [(0, 0, 0)] * array.ndim
-    outer[dim] = (length - 3 * width, 0, 0)
-    zero = jnp.zeros((), array.dtype)
-    return centre + lax.pad(tail, zero, inner) + lax.pad(head, zero, outer)
+def add_edges(centre, below, above, dim):
+    length, width = centre.shape[dim], below.shape[dim]
+    zero = jnp.zeros((), centre.dtype)
+    low = [(0, 0, 0)] * centre.ndim
+    low[dim] = (0, length - width, 0)
+    high = [(0, 0, 0)] * centre.ndim
+    high[dim] = (length - width, 0, 0)
+    return centre + lax.pad(below, zero, low) + lax.pad(above, zero, high)
 
 
 def band(weights, rows, cols, shift):
@@ -84,6 +90,8 @@
     swap = [(i, (i + 1) % groups) for i in range(groups)]
 
     kern = psf / jnp.sum(psf, axis=-1, keepdims=True)
+    start = gather_halo(estimate.astype(jnp.bfloat16), "fy", 1, halo)
+    start, psf, cover_lo, cover_len = lax.optimization_barrier((start, psf, cover_lo, cover_len))
     pack = jnp.concatenate(
         [kern.reshape(-1), cover_lo.reshape(-1).astype(jnp.float32), cover_len.reshape(-1).astype(jnp.float32)]
     )
@@ -105,12 +113,14 @@
     masked = jnp.where(own, images, jnp.zeros_like(images)).astype(jnp.float32)
 
     table_x = band(kern[:, 0], cells_x, cells_x + 2 * halo, radius - halo)
+    table_centre = table_x[:, :, halo : halo + cells_x]
+    table_edges = jnp.concatenate([table_x[:, :, :halo], table_x[:, :, halo + cells_x :]], axis=2)
     table_y = band(kern[:, 1], cells_y, cells_y + 2 * halo, radius - halo)
     table_z = band(kern[:, 2], depth, depth, radius)
 
     joined = estimate
     for step in range(ITERS):
-        wide = gather_halo(joined.astype(jnp.bfloat16), "fy", 1, halo)
+        wide = start if step == 0 else gather_halo(joined.astype(jnp.bfloat16), "fy", 1, halo)
         wide = gather_halo(wide, "fx", 0, halo).astype(jnp.float32)
         field = jnp.einsum("gox,xyz->goyz", table_x, wide, precision=exact)
         field = jnp.einsum("goy,gxyz->gxoz", table_y, field, precision=exact)
@@ -118,9 +128,12 @@
         ratio = masked / blurred
         field = jnp.einsum("goz,gxyo->gxyz", table_z, ratio, precision=exact)
         field = jnp.einsum("goy,gxoz->gxyz", table_y, field, precision=exact)
-        field = jnp.einsum("gox,goyz->xyz", table_x, field, precision=exact)
-        field = scatter_halo(field, "fx", 0, halo)
-        field = scatter_halo(field, "fy", 1, halo)
+        edges = jnp.einsum("gox,goyz->xyz", table_edges, field, precision=exact)
+        below, above = swap_edges(edges[:halo], edges[halo:], "fx")
+        centre = jnp.einsum("gox,goyz->xyz", table_centre, field, precision=exact)
+        field = add_edges(centre, below, above, 0)
+        below, above = swap_edges(field[:, :halo], field[:, cells_y + halo :], "fy")
+        field = add_edges(field[:, halo : cells_y + halo], below, above, 1)
         correction = field
         moving = field
         for _ in range(groups - 1):

time: 142 us -> 128 us (0.901)
  the two profiles are of different devices: /device:TPU:1 before, /device:TPU:20 now
where the time goes in v1:
time: 128 us; the launch traced here: 127 us
  waiting for transfers between devices  44.6 us (35%)
  matrix products  31.6 us (25%)
  starting transfers between devices  30.1 us (24%)
  local copies, waits for them, and re-layouts  10.7 us (8%)
  other arithmetic  8.87 us (7%)
    ppermute x8, waiting for transfers between devices, swap_edges(): second = lax.ppermute(jnp.where(even, to_below, to_above), axis, pairs(1))  27.5 us
    ppermute x8, starting transfers between devices, swap_edges(): second = lax.ppermute(jnp.where(even, to_below, to_above), axis, pairs(1))  24.9 us
    ppermute x2, waiting for transfers between devices, body(): moving = lax.ppermute(moving, 'view', swap)  13.2 us
    dot_general x2, matrix products, body(): centre = jnp.einsum('gox,goyz->xyz', table_centre, field, precision=exact)  5.67 us
    dot_general x2, matrix products, body(): edges = jnp.einsum('gox,goyz->xyz', table_edges, field, precision=exact)  5.63 us
    dot_general x2, matrix products, body(): field = jnp.einsum('goy,gxyz->gxoz', table_y, field, precision=exact)  5.48 us
    ppermute x8, waiting for transfers between devices, swap_edges(): first = lax.ppermute(jnp.where(even, to_above, to_below), axis, pairs(0))  3.87 us
    ppermute x2, starting transfers between devices, body(): moving = lax.ppermute(moving, 'view', swap)  3.11 us
  transfers between devices with their start and end apart: 19, of which 12 were waited for; matrix products, arithmetic and copies ran while one was open for 22% of the time, Pallas kernels for 0%

profile of v1, /device:TPU:20, one launch (start us, length us, event | category | flops | bytes accessed | tf_op | source)
XLA Modules:
  0.0 126.7 jit_solution(1051770381642538554)
XLA Ops:
  1.4 2.4 %collective-permute-start = (bf16[32,16,128]{2,0,1:T(8,128)(2,1)S(1)}, bf16[32,16,128]{2,0,1:T(8,128)(2,1)S(1)}, u32[]{:S(2)}, u32[]{:S(2)}) collective-permute-start(bf16[32,16,128]{2,0,1:T(8,128)(2,1)S(1)} %get-tuple-element.43), channel_id=1, source_target_pairs={{1,2},{2,1},{5,6},{6,5},{9,10},{10,9},{13,14},{14,13},{17,18},{18,... | collective-permute-start | bytes 393224 | tf_op jit(solution)/shard_map/ppermute | solution.py:20
  9.6 2.1 %collective-permute-start.2 = (bf16[16,64,128]{2,0,1:T(8,128)(2,1)S(1)}, bf16[16,64,128]{2,0,1:T(8,128)(2,1)S(1)}, u32[]{:S(2)}, u32[]{:S(2)}) collective-permute-start(bf16[16,64,128]{2,0,1:T(8,128)(2,1)S(1)} %get-tuple-element.35), channel_id=1, source_target_pairs={{4,8},{8,4},{5,9},{9,5},{6,10},{10,6},{7,11},{11,7},{20,24},{24,20... | collective-permute-start | bytes 786440 | tf_op jit(solution)/shard_map/ppermute | solution.py:20
  13.7 3.6 %collective-permute-done.2 = bf16[16,64,128]{2,0,1:T(8,128)(2,1)S(1)} collective-permute-done((bf16[16,64,128]{2,0,1:T(8,128)(2,1)S(1)}, bf16[16,64,128]{2,0,1:T(8,128)(2,1)S(1)}, u32[]{:S(2)}, u32[]{:S(2)}) %collective-permute-start.2) | collective-permute-done | bytes 262176 | tf_op jit(solution)/shard_map/ppermute | solution.py:20
  18.3 2.7 %fusion.2 = f32[3,32,128,32]{2,3,1,0:T(8,128)S(1)} fusion(f32[3,32,64,128]{3,1,2,0:T(8,128)S(1)} %fusion.39, f32[3,32,64,1]{2,0,1,3:T(4,128)S(1)} %convolution_bitcast_fusion.2), kind=kOutput, calls=%fused_computation.2 | convolution fusion | flops 150994944 | bytes 4743168 | tf_op jit(solution)/shard_map/goy,gxyz->gxoz/dot_general | solution.py:126
  24.5 2.8 %fusion.25 = f32[32,64,128]{2,0,1:T(8,128)S(1)} fusion(f32[3,32,64,128]{3,2,1,0:T(8,128)S(1)} %convolution_bitcast_fusion.1, f32[3,32,32]{1,2,0:T(8,128)S(1)} %copy-done.3), kind=kOutput, calls=%fused_computation.28 | convolution fusion | flops 150994944 | bytes 4206592 | tf_op jit(solution)/shard_map/gox,goyz->xyz/dot_general | solution.py:131
  28.4 2.1 %collective-permute-start.4 = (f32[16,64,128]{2,0,1:T(8,128)}, f32[16,64,128]{2,0,1:T(8,128)}, u32[]{:S(2)}, u32[]{:S(2)}) collective-permute-start(f32[16,64,128]{2,0,1:T(8,128)} %get-tuple-element.23), channel_id=1, source_target_pairs={{4,8},{8,4},{5,9},{9,5},{6,10},{10,6},{7,11},{11,7},{20,24},{24,20... | collective-permute-start | bytes 1572872 | tf_op jit(solution)/shard_map/ppermute | solution.py:20
  36.5 2.7 %collective-permute-done.4 = f32[16,64,128]{2,0,1:T(8,128)} collective-permute-done((f32[16,64,128]{2,0,1:T(8,128)}, f32[16,64,128]{2,0,1:T(8,128)}, u32[]{:S(2)}, u32[]{:S(2)}) %collective-permute-start.4) | collective-permute-done | bytes 524320 | tf_op jit(solution)/shard_map/ppermute | solution.py:20
  40.5 2.8 %pad_add_fusion.1 = f32[32,64,128]{2,0,1:T(8,128)S(1)} fusion(f32[16,64,128]{2,0,1:T(8,128)S(1)} %get-tuple-element.22, f32[16,64,128]{2,0,1:T(8,128)S(1)} %get-tuple-element.21, f32[3,32,64,128]{3,2,1,0:T(8,128)S(1)} %convolution_bitcast_fusion.1, f32[3,32,32]{1,2,0:T(8,128)S(1)} %copy-done.5), kind=kOutput, calls=%fused_computation.57 | convolution fusion | flops 151519232 | bytes 5255168 | tf_op jit(solution)/shard_map/gox,goyz->xyz/dot_general | solution.py:133
  44.4 3.6 %collective-permute-start.6 = (f32[32,16,128]{2,0,1:T(8,128)S(1)}, f32[32,16,128]{2,0,1:T(8,128)S(1)}, u32[]{:S(2)}, u32[]{:S(2)}) collective-permute-start(f32[32,16,128]{2,0,1:T(8,128)S(1)} %get-tuple-element.19), channel_id=1, source_target_pairs={{1,2},{2,1},{5,6},{6,5},{9,10},{10,9},{13,14},{14,13},{17,18},{18,... | collective-permute-start | bytes 786440 | tf_op jit(solution)/shard_map/ppermute | solution.py:20
  56.9 2.8 %fusion.35 = f32[32,32,128]{2,1,0:T(8,128)S(1)} fusion(f32[32,6,4]{0,1,2:T(8,128)S(1)} %convolution_bitcast_fusion.4, f32[32,6,4]{1,0,2:T(8,128)S(1)} %copy.74, f32[6,4,4,128,1]{3,2,1,0,4:T(4,128)S(1)} %convolution_bitcast_fusion.3), kind=kOutput, calls=%fused_computation.32 | convolution fusion | flops 151093248 | bytes 579584 | tf_op jit(solution)/shard_map/xym,mz->xyz/dot_general | solution.py:78
  59.7 5.5 %collective-permute-done.8 = f32[32,32,128]{2,0,1:T(8,128)S(1)} collective-permute-done((f32[32,32,128]{2,0,1:T(8,128)S(1)}, f32[32,32,128]{2,0,1:T(8,128)S(1)}, u32[]{:S(2)}, u32[]{:S(2)}) %collective-permute-start.8) | collective-permute-done | bytes 524320 | tf_op jit(solution)/shard_map/ppermute | solution.py:140
  65.9 2.1 %collective-permute-start.10 = (bf16[32,16,128]{2,0,1:T(8,128)(2,1)S(1)}, bf16[32,16,128]{2,0,1:T(8,128)(2,1)S(1)}, u32[]{:S(2)}, u32[]{:S(2)}) collective-permute-start(bf16[32,16,128]{2,0,1:T(8,128)(2,1)S(1)} %get-tuple-element.39), channel_id=1, source_target_pairs={{1,2},{2,1},{5,6},{6,5},{9,10},{10,9},{13,14},{14,13},{17,18},{18,... | collective-permute-start | bytes 393224 | tf_op jit(solution)/shard_map/ppermute | solution.py:20
  68.1 4.7 %collective-permute-done.10 = bf16[32,16,128]{2,0,1:T(8,128)(2,1)S(1)} collective-permute-done((bf16[32,16,128]{2,0,1:T(8,128)(2,1)S(1)}, bf16[32,16,128]{2,0,1:T(8,128)(2,1)S(1)}, u32[]{:S(2)}, u32[]{:S(2)}) %collective-permute-start.10) | collective-permute-done | bytes 131104 | tf_op jit(solution)/shard_map/ppermute | solution.py:20
  73.2 4.9 %collective-permute-start.12 = (bf16[16,64,128]{2,0,1:T(8,128)(2,1)S(1)}, bf16[16,64,128]{2,0,1:T(8,128)(2,1)S(1)}, u32[]{:S(2)}, u32[]{:S(2)}) collective-permute-start(bf16[16,64,128]{2,0,1:T(8,128)(2,1)S(1)} %get-tuple-element.29), channel_id=1, source_target_pairs={{4,8},{8,4},{5,9},{9,5},{6,10},{10,6},{7,11},{11,7},{20,24},{24,20... | collective-permute-start | bytes 786440 | tf_op jit(solution)/shard_map/ppermute | solution.py:20
  78.2 3.7 %collective-permute-done.12 = bf16[16,64,128]{2,0,1:T(8,128)(2,1)S(1)} collective-permute-done((bf16[16,64,128]{2,0,1:T(8,128)(2,1)S(1)}, bf16[16,64,128]{2,0,1:T(8,128)(2,1)S(1)}, u32[]{:S(2)}, u32[]{:S(2)}) %collective-permute-start.12) | collective-permute-done | bytes 262176 | tf_op jit(solution)/shard_map/ppermute | solution.py:20
  82.9 2.7 %fusion = f32[3,32,128,32]{2,3,1,0:T(8,128)S(1)} fusion(f32[3,32,64,128]{3,1,2,0:T(8,128)S(1)} %fusion.44, f32[3,32,64,1]{2,0,1,3:T(4,128)S(1)} %convolution_bitcast_fusion.2), kind=kOutput, calls=%fused_computation | convolution fusion | flops 150994944 | bytes 4743168 | tf_op jit(solution)/shard_map/goy,gxyz->gxoz/dot_general | solution.py:126
  89.2 2.8 %fusion.31 = f32[32,64,128]{2,0,1:T(8,128)S(1)} fusion(f32[3,32,64,128]{3,2,1,0:T(8,128)S(1)} %convolution_bitcast_fusion, f32[3,32,32]{1,2,0:T(8,128)S(1)} %copy-done.4), kind=kOutput, calls=%fused_computation.30 | convolution fusion | flops 150994944 | bytes 4206592 | tf_op jit(solution)/shard_map/gox,goyz->xyz/dot_general | solution.py:131
  92.1 3.9 %collective-permute-start.14 = (f32[16,64,128]{2,0,1:T(8,128)S(1)}, f32[16,64,128]{2,0,1:T(8,128)S(1)}, u32[]{:S(2)}, u32[]{:S(2)}) collective-permute-start(f32[16,64,128]{2,0,1:T(8,128)S(1)} %get-tuple-element.17), channel_id=1, source_target_pairs={{4,8},{8,4},{5,9},{9,5},{6,10},{10,6},{7,11},{11,7},{20,24},{24,20... | collective-permute-start | bytes 1572872 | tf_op jit(solution)/shard_map/ppermute | solution.py:20
  96.1 6.5 %collective-permute-done.14 = f32[16,64,128]{2,0,1:T(8,128)S(1)} collective-permute-done((f32[16,64,128]{2,0,1:T(8,128)S(1)}, f32[16,64,128]{2,0,1:T(8,128)S(1)}, u32[]{:S(2)}, u32[]{:S(2)}) %collective-permute-start.14) | collective-permute-done | bytes 524320 | tf_op jit(solution)/shard_map/ppermute | solution.py:20
  102.7 2.8 %pad_add_fusion = f32[32,64,128]{2,0,1:T(8,128)S(1)} fusion(f32[16,64,128]{2,0,1:T(8,128)S(1)} %get-tuple-element.16, f32[16,64,128]{2,0,1:T(8,128)S(1)} %get-tuple-element.15, f32[3,32,64,128]{3,2,1,0:T(8,128)S(1)} %convolution_bitcast_fusion, f32[3,32,32]{1,2,0:T(8,128)S(1)} %copy-done.6), kind=kOutput, calls=%fused_computation.54 | convolution fusion | flops 151519232 | bytes 5255168 | tf_op jit(solution)/shard_map/gox,goyz->xyz/dot_general | solution.py:133
  105.5 3.8 %collective-permute-start.16 = (f32[32,16,128]{2,0,1:T(8,128)S(1)}, f32[32,16,128]{2,0,1:T(8,128)S(1)}, u32[]{:S(2)}, u32[]{:S(2)}) collective-permute-start(f32[32,16,128]{2,0,1:T(8,128)S(1)} %get-tuple-element.13), channel_id=1, source_target_pairs={{1,2},{2,1},{5,6},{6,5},{9,10},{10,9},{13,14},{14,13},{17,18},{18,... | collective-permute-start | bytes 786440 | tf_op jit(solution)/shard_map/ppermute | solution.py:20
  109.4 4.4 %collective-permute-done.16 = f32[32,16,128]{2,0,1:T(8,128)S(1)} collective-permute-done((f32[32,16,128]{2,0,1:T(8,128)S(1)}, f32[32,16,128]{2,0,1:T(8,128)S(1)}, u32[]{:S(2)}, u32[]{:S(2)}) %collective-permute-start.16) | collective-permute-done | bytes 262176 | tf_op jit(solution)/shard_map/ppermute | solution.py:20
  113.8 2.0 %collective-permute-done.17 = f32[32,16,128]{2,0,1:T(8,128)S(1)} collective-permute-done((f32[32,16,128]{2,0,1:T(8,128)S(1)}, f32[32,16,128]{2,0,1:T(8,128)S(1)}, u32[]{:S(2)}, u32[]{:S(2)}) %collective-permute-start.17) | collective-permute-done | bytes 262176 | tf_op jit(solution)/shard_map/ppermute | solution.py:19
  117.5 7.7 %collective-permute-done.18 = f32[32,32,128]{2,0,1:T(8,128)S(1)} collective-permute-done((f32[32,32,128]{2,0,1:T(8,128)S(1)}, f32[32,32,128]{2,0,1:T(8,128)S(1)}, u32[]{:S(2)}, u32[]{:S(2)}) %collective-permute-start.18) | collective-permute-done | bytes 524320 | tf_op jit(solution)/shard_map/ppermute | solution.py:140
  (136 shorter events, 40.7 us)
Async XLA Ops:
  1.4 7.7 %collective-permute-start = (bf16[32,16,128]{2,0,1:T(8,128)(2,1)S(1)}, bf16[32,16,128]{2,0,1:T(8,128)(2,1)S(1)}, u32[]{:S(2)}, u32[]{:S(2)}) collective-permute-start(bf16[32,16,128]{2,0,1:T(8,128)(2,1)S(1)} %get-tuple-element.43), channel_id=1, source_target_pairs={{1,2},{2,1},{5,6},{6,5},{9,10},{10,9},{13,14},{14,13},{17,18},{18,... | collective-permute-start | bytes 393224 | tf_op jit(solution)/shard_map/ppermute | solution.py:20
  3.8 5.4 %collective-permute-start.1 = (bf16[32,16,128]{2,0,1:T(8,128)(2,1)S(1)}, bf16[32,16,128]{2,0,1:T(8,128)(2,1)S(1)}, u32[]{:S(2)}, u32[]{:S(2)}) collective-permute-start(bf16[32,16,128]{2,0,1:T(8,128)(2,1)S(1)} %get-tuple-element.44), channel_id=1, source_target_pairs={{0,1},{1,0},{2,3},{3,2},{4,5},{5,4},{6,7},{7,6},{8,9},{9,8},{10,11... | collective-permute-start | bytes 393224 | tf_op jit(solution)/shard_map/ppermute | solution.py:19
  9.6 7.7 %collective-permute-start.2 = (bf16[16,64,128]{2,0,1:T(8,128)(2,1)S(1)}, bf16[16,64,128]{2,0,1:T(8,128)(2,1)S(1)}, u32[]{:S(2)}, u32[]{:S(2)}) collective-permute-start(bf16[16,64,128]{2,0,1:T(8,128)(2,1)S(1)} %get-tuple-element.35), channel_id=1, source_target_pairs={{4,8},{8,4},{5,9},{9,5},{6,10},{10,6},{7,11},{11,7},{20,24},{24,20... | collective-permute-start | bytes 786440 | tf_op jit(solution)/shard_map/ppermute | solution.py:20
  11.7 5.6 %collective-permute-start.3 = (bf16[16,64,128]{2,0,1:T(8,128)(2,1)S(1)}, bf16[16,64,128]{2,0,1:T(8,128)(2,1)S(1)}, u32[]{:S(2)}, u32[]{:S(2)}) collective-permute-start(bf16[16,64,128]{2,0,1:T(8,128)(2,1)S(1)} %get-tuple-element.36), channel_id=1, source_target_pairs={{0,4},{4,0},{8,12},{12,8},{1,5},{5,1},{9,13},{13,9},{2,6},{6,2},{1... | collective-permute-start | bytes 786440 | tf_op jit(solution)/shard_map/ppermute | solution.py:19
  11.8 21.6 %collective-permute-start.9 = (f32[375]{0:T(512)S(1)}, f32[375]{0:T(512)S(1)}, u32[]{:S(2)}, u32[]{:S(2)}) collective-permute-start(f32[375]{0:T(512)S(1)} %pad_maximum_fusion.3), channel_id=1, source_target_pairs={{0,16},{16,0},{1,17},{17,1},{2,18},{18,2},{3,19},{19,3},{4,20},{20... | collective-permute-start | bytes 4508 | tf_op jit(solution)/shard_map/ppermute | solution.py:100
  28.4 10.8 %collective-permute-start.4 = (f32[16,64,128]{2,0,1:T(8,128)}, f32[16,64,128]{2,0,1:T(8,128)}, u32[]{:S(2)}, u32[]{:S(2)}) collective-permute-start(f32[16,64,128]{2,0,1:T(8,128)} %get-tuple-element.23), channel_id=1, source_target_pairs={{4,8},{8,4},{5,9},{9,5},{6,10},{10,6},{7,11},{11,7},{20,24},{24,20... | collective-permute-start | bytes 1572872 | tf_op jit(solution)/shard_map/ppermute | solution.py:20
  30.5 8.7 %collective-permute-start.5 = (f32[16,64,128]{2,0,1:T(8,128)}, f32[16,64,128]{2,0,1:T(8,128)}, u32[]{:S(2)}, u32[]{:S(2)}) collective-permute-start(f32[16,64,128]{2,0,1:T(8,128)} %get-tuple-element.24), channel_id=1, source_target_pairs={{0,4},{4,0},{8,12},{12,8},{1,5},{5,1},{9,13},{13,9},{2,6},{6,2},{1... | collective-permute-start | bytes 1572872 | tf_op jit(solution)/shard_map/ppermute | solution.py:19
  44.4 12.2 %copy-start.8 = (s32[32,31]{1,0:T(8,128)S(1)}, s32[32,31]{1,0:T(8,128)}, u32[]{:S(2)}) copy-start(s32[32,31]{1,0:T(8,128)} %subtract_add_fusion.1) | copy-start | bytes 11908
  44.4 12.2 %copy-start.12 = (f32[6,1,31]{2,1,0:T(1,128)S(1)}, f32[6,1,31]{2,1,0:T(1,128)}, u32[]{:S(2)}) copy-start(f32[6,1,31]{2,1,0:T(1,128)} %get-tuple-element.48) | copy-start | bytes 2236
  44.4 12.2 %copy-start.18 = (s32[4]{0:T(128)S(1)}, s32[4]{0:T(128)}, u32[]{:S(2)}) copy-start(s32[4]{0:T(128)} %get-tuple-element.57) | copy-start | bytes 52
  44.4 12.2 %copy-start.20 = (s32[4]{0:T(128)S(1)}, s32[4]{0:T(128)}, u32[]{:S(2)}) copy-start(s32[4]{0:T(128)} %get-tuple-element.58) | copy-start | bytes 52
  44.4 8.4 %collective-permute-start.6 = (f32[32,16,128]{2,0,1:T(8,128)S(1)}, f32[32,16,128]{2,0,1:T(8,128)S(1)}, u32[]{:S(2)}, u32[]{:S(2)}) collective-permute-start(f32[32,16,128]{2,0,1:T(8,128)S(1)} %get-tuple-element.19), channel_id=1, source_target_pairs={{1,2},{2,1},{5,6},{6,5},{9,10},{10,9},{13,14},{14,13},{17,18},{18,... | collective-permute-start | bytes 786440 | tf_op jit(solution)/shard_map/ppermute | solution.py:20
  48.1 6.4 %collective-permute-start.7 = (f32[32,16,128]{2,0,1:T(8,128)S(1)}, f32[32,16,128]{2,0,1:T(8,128)S(1)}, u32[]{:S(2)}, u32[]{:S(2)}) collective-permute-start(f32[32,16,128]{2,0,1:T(8,128)S(1)} %get-tuple-element.20), channel_id=1, source_target_pairs={{0,1},{1,0},{2,3},{3,2},{4,5},{5,4},{6,7},{7,6},{8,9},{9,8},{10,11... | collective-permute-start | bytes 786440 | tf_op jit(solution)/shard_map/ppermute | solution.py:19
  54.7 10.5 %collective-permute-start.8 = (f32[32,32,128]{2,0,1:T(8,128)S(1)}, f32[32,32,128]{2,0,1:T(8,128)S(1)}, u32[]{:S(2)}, u32[]{:S(2)}) collective-permute-start(f32[32,32,128]{2,0,1:T(8,128)S(1)} %fusion.58), channel_id=1, source_target_pairs={{0,16},{16,0},{1,17},{17,1},{2,18},{18,2},{3,19},{19,3},{4,20},{20... | collective-permute-start | bytes 1572872 | tf_op jit(solution)/shard_map/ppermute | solution.py:140
  65.9 6.9 %collective-permute-start.10 = (bf16[32,16,128]{2,0,1:T(8,128)(2,1)S(1)}, bf16[32,16,128]{2,0,1:T(8,128)(2,1)S(1)}, u32[]{:S(2)}, u32[]{:S(2)}) collective-permute-start(bf16[32,16,128]{2,0,1:T(8,128)(2,1)S(1)} %get-tuple-element.39), channel_id=1, source_target_pairs={{1,2},{2,1},{5,6},{6,5},{9,10},{10,9},{13,14},{14,13},{17,18},{18,... | collective-permute-start | bytes 393224 | tf_op jit(solution)/shard_map/ppermute | solution.py:20
  68.0 5.0 %collective-permute-start.11 = (bf16[32,16,128]{2,0,1:T(8,128)(2,1)S(1)}, bf16[32,16,128]{2,0,1:T(8,128)(2,1)S(1)}, u32[]{:S(2)}, u32[]{:S(2)}) collective-permute-start(bf16[32,16,128]{2,0,1:T(8,128)(2,1)S(1)} %get-tuple-element.40), channel_id=1, source_target_pairs={{0,1},{1,0},{2,3},{3,2},{4,5},{5,4},{6,7},{7,6},{8,9},{9,8},{10,11... | collective-permute-start | bytes 393224 | tf_op jit(solution)/shard_map/ppermute | solution.py:19
  73.2 8.7 %collective-permute-start.12 = (bf16[16,64,128]{2,0,1:T(8,128)(2,1)S(1)}, bf16[16,64,128]{2,0,1:T(8,128)(2,1)S(1)}, u32[]{:S(2)}, u32[]{:S(2)}) collective-permute-start(bf16[16,64,128]{2,0,1:T(8,128)(2,1)S(1)} %get-tuple-element.29), channel_id=1, source_target_pairs={{4,8},{8,4},{5,9},{9,5},{6,10},{10,6},{7,11},{11,7},{20,24},{24,20... | collective-permute-start | bytes 786440 | tf_op jit(solution)/shard_map/ppermute | solution.py:20
  78.1 3.8 %collective-permute-start.13 = (bf16[16,64,128]{2,0,1:T(8,128)(2,1)S(1)}, bf16[16,64,128]{2,0,1:T(8,128)(2,1)S(1)}, u32[]{:S(2)}, u32[]{:S(2)}) collective-permute-start(bf16[16,64,128]{2,0,1:T(8,128)(2,1)S(1)} %get-tuple-element.30), channel_id=1, source_target_pairs={{0,4},{4,0},{8,12},{12,8},{1,5},{5,1},{9,13},{13,9},{2,6},{6,2},{1... | collective-permute-start | bytes 786440 | tf_op jit(solution)/shard_map/ppermute | solution.py:19
  92.0 10.7 %copy-start.6 = (f32[3,32,32]{1,2,0:T(8,128)S(1)}, f32[3,32,32]{1,2,0:T(8,128)}, u32[]{:S(2)}) copy-start(f32[3,32,32]{1,2,0:T(8,128)} %copy.68) | copy-start | bytes 36868
  92.1 10.5 %collective-permute-start.14 = (f32[16,64,128]{2,0,1:T(8,128)S(1)}, f32[16,64,128]{2,0,1:T(8,128)S(1)}, u32[]{:S(2)}, u32[]{:S(2)}) collective-permute-start(f32[16,64,128]{2,0,1:T(8,128)S(1)} %get-tuple-element.17), channel_id=1, source_target_pairs={{4,8},{8,4},{5,9},{9,5},{6,10},{10,6},{7,11},{11,7},{20,24},{24,20... | collective-permute-start | bytes 1572872 | tf_op jit(solution)/shard_map/ppermute | solution.py:20
  96.0 6.6 %collective-permute-start.15 = (f32[16,64,128]{2,0,1:T(8,128)S(1)}, f32[16,64,128]{2,0,1:T(8,128)S(1)}, u32[]{:S(2)}, u32[]{:S(2)}) collective-permute-start(f32[16,64,128]{2,0,1:T(8,128)S(1)} %get-tuple-element.18), channel_id=1, source_target_pairs={{0,4},{4,0},{8,12},{12,8},{1,5},{5,1},{9,13},{13,9},{2,6},{6,2},{1... | collective-permute-start | bytes 1572872 | tf_op jit(solution)/shard_map/ppermute | solution.py:19
  105.5 8.3 %collective-permute-start.16 = (f32[32,16,128]{2,0,1:T(8,128)S(1)}, f32[32,16,128]{2,0,1:T(8,128)S(1)}, u32[]{:S(2)}, u32[]{:S(2)}) collective-permute-start(f32[32,16,128]{2,0,1:T(8,128)S(1)} %get-tuple-element.13), channel_id=1, source_target_pairs={{1,2},{2,1},{5,6},{6,5},{9,10},{10,9},{13,14},{14,13},{17,18},{18,... | collective-permute-start | bytes 786440 | tf_op jit(solution)/shard_map/ppermute | solution.py:20
  109.3 6.4 %collective-permute-start.17 = (f32[32,16,128]{2,0,1:T(8,128)S(1)}, f32[32,16,128]{2,0,1:T(8,128)S(1)}, u32[]{:S(2)}, u32[]{:S(2)}) collective-permute-start(f32[32,16,128]{2,0,1:T(8,128)S(1)} %get-tuple-element.14), channel_id=1, source_target_pairs={{0,1},{1,0},{2,3},{3,2},{4,5},{5,4},{6,7},{7,6},{8,9},{9,8},{10,11... | collective-permute-start | bytes 786440 | tf_op jit(solution)/shard_map/ppermute | solution.py:19
  115.9 9.2 %collective-permute-start.18 = (f32[32,32,128]{2,0,1:T(8,128)S(1)}, f32[32,32,128]{2,0,1:T(8,128)S(1)}, u32[]{:S(2)}, u32[]{:S(2)}) collective-permute-start(f32[32,32,128]{2,0,1:T(8,128)S(1)} %fusion.57), channel_id=1, source_target_pairs={{0,16},{16,0},{1,17},{17,1},{2,18},{18,2},{3,19},{19,3},{4,20},{20... | collective-permute-start | bytes 1572872 | tf_op jit(solution)/shard_map/ppermute | solution.py:140
  (16 other events, 88.7 us)

commit v2 on v0

v2 whole, which is shorter than its diff:
```python
import functools

import jax
import jax.numpy as jnp
from jax import lax
from jax.experimental import pallas as pl
from jax.experimental.pallas import tpu as pltpu
from jax.sharding import PartitionSpec as P

ITERS = 2
LANES = 128
VMEM = pl.BlockSpec(memory_space=pltpu.VMEM)
SMEM = pl.BlockSpec(memory_space=pltpu.SMEM)
PARAMS = pltpu.CompilerParams(vmem_limit_bytes=40 * 2**20)
ROUNDS = ((None, 0), (None, 1), (0, 0), (0, 1), (1, 0), (1, 1), (0, None), (1, None))


def side(flags, axis, turn):
    return 1 - lax.rem(flags[axis] + turn, 2)


def span(flags, axis, turn, low, high, width):
    start = low + side(flags, axis, turn) * (high - low)
    return pl.ds(pl.multiple_of(start, 16), width)


def piece(flags, turns, full, lows, highs, halo):
    out = []
    for axis in range(2):
        if turns[axis] is None:
            out.append(full[axis])
        else:
            out.append(span(flags, axis, turns[axis], lows[axis], highs[axis], halo))
    return tuple(out)


def pairs_of(peers, turn):
    out = list(range(peers))
    for i in range(turn, peers - 1, 2):
        out[i], out[i + 1] = i + 1, i
    return out


def exchange(parts):
    size_x, size_y = lax.axis_size("fx"), lax.axis_size("fy")
    out = []
    for (turn_x, turn_y), part in zip(ROUNDS, parts):
        partner_x = list(range(size_x)) if turn_x is None else pairs_of(size_x, turn_x)
        partner_y = list(range(size_y)) if turn_y is None else pairs_of(size_y, turn_y)
        pairs = []
        for i in range(size_x):
            for j in range(size_y):
                if (turn_x is not None and partner_x[i] == i) or (turn_y is not None and partner_y[j] == j):
                    continue
                pairs.append((i * size_y + j, partner_x[i] * size_y + partner_y[j]))
        out.append(lax.ppermute(part, ("fx", "fy"), pairs))
    return out


def part_shapes(cells_x, cells_y, depth, halo, dtype):
    return [
        jax.ShapeDtypeStruct(
            (cells_x if tx is None else halo, cells_y if ty is None else halo, depth), dtype
        )
        for tx, ty in ROUNDS
    ]


def split(value):
    high = value.astype(jnp.bfloat16)
    low = (value - high.astype(jnp.float32)).astype(jnp.bfloat16)
    return high, low


def place(blocks, width):
    per = LANES // width
    tiles = []
    for first in range(0, len(blocks), per):
        tile = blocks[first]
        for at, block in enumerate(blocks[first + 1 : first + per]):
            tile = tile + pltpu.roll(block, (at + 1) * width, 1)
        tiles.append(tile)
    whole = tiles[0] if len(tiles) == 1 else jnp.concatenate(tiles, axis=1)
    return whole[:, : len(blocks) * width].astype(jnp.bfloat16)


def table_kernel(taps, halo, cells_x, cells_y, psf, tyf, txf, tzf, tzb, txb, tyb):
    group = psf.shape[0]
    radius = (taps - 1) // 2
    depth = tzb.shape[2]

    def parts(value):
        high = value.astype(jnp.bfloat16).astype(jnp.float32)
        return high, value - high

    y_blocks, y_low = [], []
    for k in range(group):
        rows = psf[k]
        rows = rows / jnp.sum(rows, axis=1, keepdims=True)
        bands = []
        for axis, cells in ((0, cells_x), (1, cells_y)):
            base = jnp.broadcast_to(pltpu.roll(rows[axis : axis + 1], halo - radius, 1), (cells, LANES))
            bands.append(pltpu.roll(base, 0, 1, stride=1, stride_axis=0))
        base = jnp.broadcast_to(pltpu.roll(rows[2:3], depth - radius, 1), (depth, depth))
        band_z = pltpu.roll(base, 0, 1, stride=1, stride_axis=0)
        gap = lax.broadcasted_iota(jnp.int32, (depth, depth), 1) - lax.broadcasted_iota(
            jnp.int32, (depth, depth), 0
        )
        band_z = jnp.where((gap >= -radius) & (gap <= radius), band_z, 0.0)
        wide_x, wide_y = cells_x + 2 * halo, cells_y + 2 * halo

        high, low = parts(bands[1])
        tyf[k * cells_y : (k + 1) * cells_y, :] = place([high, low], wide_y)
        high, low = parts(bands[0])
        txf[k] = place([high, low, high], wide_x)
        high, low = parts(band_z)
        tzb[k, 0:depth, :] = high.astype(jnp.bfloat16)
        tzb[k, depth : 2 * depth, :] = low.astype(jnp.bfloat16)
        tzb[k, 2 * depth :, :] = high.astype(jnp.bfloat16)
        high, low = high.T, low.T
        tzf[k, 0:depth, :] = high.astype(jnp.bfloat16)
        tzf[k, depth : 2 * depth, :] = low.astype(jnp.bfloat16)
        tzf[k, 2 * depth :, :] = high.astype(jnp.bfloat16)

        def turned(value, cells, wide):
            square = jnp.concatenate([value, jnp.zeros((LANES - cells, LANES), jnp.float32)], axis=0)
            return square.T[:wide]

        high, low = parts(turned(bands[0], cells_x, wide_x))
        txb[k] = place([high, low, high], cells_x)
        high, low = parts(turned(bands[1], cells_y, wide_y))
        y_blocks.append(high)
        y_low.append(low)
    tyb[...] = place(y_blocks + y_low + y_blocks, cells_y)


def blur_kernel(halo, chunk, flags, centre, *refs):
    received, refs = refs[:8], refs[8:]
    images, tyf, txf, tzf, tzb, txb, tyb = refs[:7]
    out_centre, sent = refs[7], refs[8:16]
    field, turned, back, result = refs[16:]
    cells_x, cells_y, depth = centre.shape
    group = images.shape[0]
    wide_x, wide_y = cells_x + 2 * halo, cells_y + 2 * halo
    inner = (pl.ds(halo, cells_x), pl.ds(halo, cells_y))
    zeros, tops = (0, 0), (cells_x + halo, cells_y + halo)

    field[inner] = centre[...]
    for turns, part in zip(ROUNDS, received):
        field[piece(flags, turns, inner, zeros, tops, halo)] = part[...]

    dot = functools.partial(jnp.dot, preferred_element_type=jnp.float32)
    pair = functools.partial(jnp.concatenate, axis=1)
    stack = functools.partial(jnp.concatenate, axis=0)

    def forward_y(i, carry):
        x = 2 * i
        both = pair([field[x], field[x + 1]])
        got = dot(tyf[...], stack([both, both]))
        turned[pl.ds(x, group * cells_y, stride=wide_x), :] = got[:, :depth]
        turned[pl.ds(x + 1, group * cells_y, stride=wide_x), :] = got[:, depth:]
        return carry

    lax.fori_loop(0, wide_x // 2, forward_y, 0, unroll=4)

    per = cells_y // chunk

    def middle(i, carry):
        k = i // per
        first = (i - k * per) * chunk
        rows = []
        for j in range(0, chunk, 2):
            at = pl.multiple_of((k * cells_y + first + j) * wide_x, 16)
            both = pair([turned[pl.ds(at, wide_x), :], turned[pl.ds(at + wide_x, wide_x), :]])
            high, low = split(both)
            got = dot(txf[k], stack([high, high, low]))
            rows += [got[:, :depth], got[:, depth:]]
        high, low = split(stack(rows))
        blurred = dot(pair([high, high, low]), tzf[k])
        seen = images[k, pl.ds(first, chunk)].astype(jnp.float32).reshape(chunk * cells_x, depth)
        high, low = split(seen / blurred)
        spread = dot(pair([high, high, low]), tzb[k])
        for j in range(0, chunk, 2):
            both = pair([spread[j * cells_x : (j + 1) * cells_x], spread[(j + 1) * cells_x : (j + 2) * cells_x]])
            high, low = split(both)
            got = dot(txb[k], stack([high, high, low]))
            at = k * cells_y + first + j
            back[pl.ds(at, wide_x, stride=group * cells_y), :] = got[:, :depth]
            back[pl.ds(at + 1, wide_x, stride=group * cells_y), :] = got[:, depth:]
        return carry

    lax.fori_loop(0, group * per, middle, 0, unroll=1)

    def backward_y(i, carry):
        rows = group * cells_y
        at = pl.multiple_of(2 * i * rows, 16)
        high, low = split(pair([back[pl.ds(at, rows), :], back[pl.ds(at + rows, rows), :]]))
        got = dot(tyb[...], stack([high, high, low]))
        result[2 * i] = got[:, :depth]
        result[2 * i + 1] = got[:, depth:]
        return carry

    lax.fori_loop(0, wide_x // 2, backward_y, 0, unroll=4)
    out_centre[...] = result[inner]
    for turns, part in zip(ROUNDS, sent):
        part[...] = result[piece(flags, turns, inner, zeros, tops, halo)]


def join_kernel(halo, flags, centre, *refs):
    received, out = refs[:8], refs[8]
    cells_x, cells_y, _ = centre.shape
    full = (pl.ds(0, cells_x), pl.ds(0, cells_y))
    out[...] = centre[...]
    for turns, part in zip(ROUNDS, received):
        at = piece(flags, turns, full, (0, 0), (cells_x - halo, cells_y - halo), halo)
        out[at] = out[at] + part[...]


def send_parts(flags, source, halo, out_centre, outs):
    cells_x, cells_y, _ = source.shape
    full = (pl.ds(0, cells_x), pl.ds(0, cells_y))
    out_centre[...] = source[...].astype(out_centre.dtype)
    for turns, part in zip(ROUNDS, outs):
        at = piece(flags, turns, full, (0, 0), (cells_x - halo, cells_y - halo), halo)
        part[...] = source[at].astype(part.dtype)


def start_kernel(halo, flags, source, out_centre, *outs):
    send_parts(flags, source, halo, out_centre, outs)


def update_kernel(halo, flags, joined, own, moved, lower, out, *outs):
    out[...] = joined[...] * (own[...] + moved[...] + 0.5) / lower[...]
    if outs:
        send_parts(flags, out, halo, outs[0], outs[1:])


def call(kernel, inputs, outs, scratch=(), flagged=True):
    return pl.pallas_call(
        kernel,
        out_shape=outs,
        in_specs=[SMEM if flagged and i == 0 else VMEM for i in range(len(inputs))],
        out_specs=[VMEM] * len(outs),
        scratch_shapes=list(scratch),
        compiler_params=PARAMS,
    )(*inputs)


def band(weights, rows, cols, shift):
    taps = weights.shape[-1]
    gap = (
        jnp.arange(cols, dtype=jnp.int32)[None, :]
        - jnp.arange(rows, dtype=jnp.int32)[:, None]
        + shift
    )
    picks = (gap[:, :, None] == jnp.arange(taps, dtype=jnp.int32)).astype(jnp.float32)
    return jnp.einsum("oit,gt->goi", picks, weights, precision=lax.Precision.HIGHEST)


def block_sums(weights, axis, cells):
    blocks = lax.axis_size(axis)
    taps = weights.shape[-1]
    at = lax.axis_index(axis) * cells + jnp.arange(cells, dtype=jnp.int32)
    source = at[:, None] - jnp.arange(taps, dtype=jnp.int32)[None, :] + (taps - 1) // 2
    first = jnp.arange(blocks, dtype=jnp.int32)[:, None, None] * cells
    picks = ((source[None] >= first) & (source[None] < first + cells)).astype(jnp.float32)
    return jnp.einsum("bot,gt->ogb", picks, weights, precision=lax.Precision.HIGHEST)


def weight_of(kern, low, length, cells_x, cells_y, depth):
    taps = kern.shape[-1]
    sums_x = block_sums(kern[:, 0], "fx", cells_x)
    sums_y = block_sums(kern[:, 1], "fy", cells_y)
    levels = jnp.arange(depth, dtype=jnp.int32)
    inside = (levels >= low[..., None]) & (levels < (low + length)[..., None])
    table_z = band(kern[:, 2], depth, depth, (taps - 1) // 2)
    sums_z = jnp.einsum(
        "gxyi,gio->gxyo", inside.astype(jnp.float32), table_z, precision=lax.Precision.HIGHEST
    )
    plane = sums_x[:, None, :, :, None] * sums_y[None, :, :, None, :]
    plane = plane.reshape(cells_x, cells_y, -1)
    return jnp.einsum(
        "xym,mz->xyz", plane, sums_z.reshape(-1, depth), precision=lax.Precision.HIGHEST
    )


def body(estimate, images, psf, cover_lo, cover_len):
    group, cells_x, cells_y, depth = images.shape
    taps = psf.shape[-1]
    halo = -(-((taps - 1) // 2) // 16) * 16
    wide_x, wide_y = cells_x + 2 * halo, cells_y + 2 * halo
    groups = lax.axis_size("view")
    swap = [(i, (i + 1) % groups) for i in range(groups)]
    bf16, f32 = jnp.bfloat16, jnp.float32
    block = lambda dtype: jax.ShapeDtypeStruct((cells_x, cells_y, depth), dtype)
    parts_of = functools.partial(part_shapes, cells_x, cells_y, depth, halo)

    block_x, block_y = lax.axis_index("fx"), lax.axis_index("fy")
    flags = jnp.stack([block_x % 2, block_y % 2]).astype(jnp.int32)

    centre, *parts = call(
        functools.partial(start_kernel, halo), (flags, estimate), [block(bf16)] + parts_of(bf16)
    )
    parts = exchange(parts)

    padded = jnp.pad(psf, ((0, 0), (0, 0), (0, LANES - taps)))
    tables = call(
        functools.partial(table_kernel, taps, halo, cells_x, cells_y),
        (padded,),
        [
            jax.ShapeDtypeStruct((group * cells_y, 2 * wide_y), bf16),
            jax.ShapeDtypeStruct((group, cells_x, 3 * wide_x), bf16),
            jax.ShapeDtypeStruct((group, 3 * depth, depth), bf16),
            jax.ShapeDtypeStruct((group, 3 * depth, depth), bf16),
            jax.ShapeDtypeStruct((group, wide_x, 3 * cells_x), bf16),
            jax.ShapeDtypeStruct((wide_y, 3 * group * cells_y), bf16),
        ],
        flagged=False,
    )

    low = lax.dynamic_slice(cover_lo, (0, block_x, block_y), (group, 1, 1))[..., None]
    length = lax.dynamic_slice(cover_len, (0, block_x, block_y), (group, 1, 1))[..., None]
    levels = jnp.arange(depth, dtype=jnp.int32)
    own = (levels >= low) & (levels < low + length)
    masked = jnp.where(own, images, jnp.zeros_like(images)).transpose(0, 2, 1, 3)

    psf_late, lo_late, len_late, _ = lax.optimization_barrier((psf, cover_lo, cover_len, parts[0]))
    kern = psf_late / jnp.sum(psf_late, axis=-1, keepdims=True)
    pack = jnp.concatenate(
        [kern.reshape(-1), lo_late.reshape(-1).astype(f32), len_late.reshape(-1).astype(f32)]
    )
    packs = [pack]
    for _ in range(groups - 1):
        packs.append(lax.ppermute(packs[-1], "view", swap))
    packs = jnp.stack(packs)
    cells = cover_lo.size
    all_kern = packs[:, : kern.size].reshape((-1,) + kern.shape[1:])
    all_low = packs[:, kern.size : kern.size + cells].astype(jnp.int32).reshape((-1,) + cover_lo.shape[1:])
    all_len = packs[:, kern.size + cells :].astype(jnp.int32).reshape((-1,) + cover_len.shape[1:])
    lower_part = weight_of(all_kern, all_low, all_len, cells_x, cells_y, depth) + 0.5

    joined = estimate
    for step in range(ITERS):
        total, *sums = call(
            functools.partial(blur_kernel, halo, 8),
            (flags, centre, *parts, masked, *tables),
            [block(f32)] + parts_of(f32),
            [
                pltpu.VMEM((wide_x, wide_y, depth), bf16),
                pltpu.VMEM((group * cells_y * wide_x, depth), f32),
                pltpu.VMEM((wide_x * group * cells_y, depth), f32),
                pltpu.VMEM((wide_x, wide_y, depth), f32),
            ],
        )
        sums = exchange(sums)
        (own_sum,) = call(functools.partial(join_kernel, halo), (flags, total, *sums), [block(f32)])
        moving, moved = own_sum, None
        for _ in range(groups - 1):
            moving = lax.ppermute(moving, "view", swap)
            moved = moving if moved is None else moved + moving
        if moved is None:
            moved = jnp.zeros_like(own_sum)
        last = step == ITERS - 1
        joined, *rest = call(
            functools.partial(update_kernel, halo),
            (flags, joined, own_sum, moved, lower_part),
            [block(f32)] + ([] if last else [block(bf16)] + parts_of(bf16)),
        )
        if not last:
            centre, parts = rest[0], exchange(rest[1:])
    return joined


def solution(mesh):
    return jax.shard_map(
        body,
        mesh=mesh,
        in_specs=(
            P("fx", "fy", None),
            P("view", "fx", "fy", None),
            P("view", None, None),
            P("view", None, None),
            P("view", None, None),
        ),
        out_specs=P("fx", "fy", None),
        check_vma=False,
    )
```

time: 142 us -> 144 us (1.014)
  the two profiles are of different devices: /device:TPU:1 before, /device:TPU:20 now
where the time goes in v2:
time: 144 us; the launch traced here: 141 us
  starting transfers between devices  65.5 us (45%)
  Pallas kernels  35.8 us (25%)
  waiting for transfers between devices  20.7 us (14%)
  local copies, waits for them, and re-layouts  8.59 us (6%)
  matrix products  6.29 us (4%)
  other arithmetic  3.72 us (3%)
    ppermute x32, starting transfers between devices, exchange(): out.append(lax.ppermute(part, ('fx', 'fy'), pairs))  60.9 us
    pallas_call x8, Pallas kernels, call(): pl.pallas_call(kernel, out_shape=outs, in_specs=[SMEM if flagged and i ==...  35.8 us
    ppermute x2, waiting for transfers between devices, body(): moving = lax.ppermute(moving, 'view', swap)  11 us
    ppermute x32, waiting for transfers between devices, exchange(): out.append(lax.ppermute(part, ('fx', 'fy'), pairs))  9.64 us
    unnamed x52, local copies, waits for them, and re-layouts  5.66 us
    ppermute x2, starting transfers between devices, body(): moving = lax.ppermute(moving, 'view', swap)  3.11 us
  transfers between devices with their start and end apart: 35, of which 6 were waited for; matrix products, arithmetic and copies ran while one was open for 9% of the time, Pallas kernels for 12%

profile of v2, /device:TPU:20, one launch (start us, length us, event | category | flops | bytes accessed | tf_op | source)
XLA Modules:
  0.0 141.3 jit_solution(65682580099955842)
XLA Ops:
  6.7 2.3 %collective-permute-start = (bf16[32,16,128]{2,1,0:T(8,128)(2,1)S(1)}, bf16[32,16,128]{2,1,0:T(8,128)(2,1)S(1)}, u32[]{:S(2)}, u32[]{:S(2)}) collective-permute-start(bf16[32,16,128]{2,1,0:T(8,128)(2,1)S(1)} %get-tuple-element.52), channel_id=1, source_target_pairs={{0,1},{1,0},{2,3},{3,2},{4,5},{5,4},{6,7},{7,6},{8,9},{9,8},{10,11... | collective-permute-start | bytes 393224 | tf_op jit(solution)/shard_map/ppermute | solution.py:56
  9.0 3.3 %collective-permute-start.1 = (bf16[32,16,128]{2,1,0:T(8,128)(2,1)S(1)}, bf16[32,16,128]{2,1,0:T(8,128)(2,1)S(1)}, u32[]{:S(2)}, u32[]{:S(2)}) collective-permute-start(bf16[32,16,128]{2,1,0:T(8,128)(2,1)S(1)} %get-tuple-element.53), channel_id=1, source_target_pairs={{1,2},{2,1},{5,6},{6,5},{9,10},{10,9},{13,14},{14,13},{17,18},{18,... | collective-permute-start | bytes 393224 | tf_op jit(solution)/shard_map/ppermute | solution.py:56
  17.2 3.1 %collective-permute-start.7 = (bf16[16,32,128]{2,1,0:T(8,128)(2,1)S(1)}, bf16[16,32,128]{2,1,0:T(8,128)(2,1)S(1)}, u32[]{:S(2)}, u32[]{:S(2)}) collective-permute-start(bf16[16,32,128]{2,1,0:T(8,128)(2,1)S(1)} %get-tuple-element.59), channel_id=1, source_target_pairs={{4,8},{5,9},{6,10},{7,11},{8,4},{9,5},{10,6},{11,7},{20,24},{21,25... | collective-permute-start | bytes 393224 | tf_op jit(solution)/shard_map/ppermute | solution.py:56
  20.4 2.4 %collective-permute-start.5 = (bf16[16,16,128]{2,1,0:T(8,128)(2,1)S(1)}, bf16[16,16,128]{2,1,0:T(8,128)(2,1)S(1)}, u32[]{:S(2)}, u32[]{:S(2)}) collective-permute-start(bf16[16,16,128]{2,1,0:T(8,128)(2,1)S(1)} %get-tuple-element.57), channel_id=1, source_target_pairs={{5,10},{6,9},{9,6},{10,5},{21,26},{22,25},{25,22},{26,21}} | collective-permute-start | bytes 196616 | tf_op jit(solution)/shard_map/ppermute | solution.py:56
  26.9 15.5 %shard_map.57 = (f32[32,32,128]{2,1,0:T(8,128)S(1)}, f32[32,16,128]{2,1,0:T(8,128)}, f32[32,16,128]{2,1,0:T(8,128)}, f32[16,16,128]{2,1,0:T(8,128)S(1)}, f32[16,...) custom-call(s32[2]{0:T(128)S(1)} %pad_add_fusion.flags, ...), custom_call_target="tpu_custom_call" | custom-call | tf_op jit(solution)/shard_map/pallas_call | solution.py:239
  48.3 2.0 %collective-permute-start.8 = (f32[32,16,128]{2,1,0:T(8,128)}, f32[32,16,128]{2,1,0:T(8,128)S(1)}, u32[]{:S(2)}, u32[]{:S(2)}) collective-permute-start(f32[32,16,128]{2,1,0:T(8,128)} %get-tuple-element.67), channel_id=1, source_target_pairs={{0,1},{1,0},{2,3},{3,2},{4,5},{5,4},{6,7},{7,6},{8,9},{9,8},{10,11... | collective-permute-start | bytes 786440 | tf_op jit(solution)/shard_map/ppermute | solution.py:56
  50.3 2.5 %collective-permute-start.9 = (f32[32,16,128]{2,1,0:T(8,128)}, f32[32,16,128]{2,1,0:T(8,128)S(1)}, u32[]{:S(2)}, u32[]{:S(2)}) collective-permute-start(f32[32,16,128]{2,1,0:T(8,128)} %get-tuple-element.68), channel_id=1, source_target_pairs={{1,2},{2,1},{5,6},{6,5},{9,10},{10,9},{13,14},{14,13},{17,18},{18,... | collective-permute-start | bytes 786440 | tf_op jit(solution)/shard_map/ppermute | solution.py:56
  55.2 2.3 %collective-permute-start.15 = (f32[16,32,128]{2,1,0:T(8,128)}, f32[16,32,128]{2,1,0:T(8,128)S(1)}, u32[]{:S(2)}, u32[]{:S(2)}) collective-permute-start(f32[16,32,128]{2,1,0:T(8,128)} %copy-done.12), channel_id=1, source_target_pairs={{4,8},{5,9},{6,10},{7,11},{8,4},{9,5},{10,6},{11,7},{20,24},{21,25... | collective-permute-start | bytes 786440 | tf_op jit(solution)/shard_map/ppermute | solution.py:56
  57.8 4.3 %collective-permute-start.13 = (f32[16,16,128]{2,1,0:T(8,128)}, f32[16,16,128]{2,1,0:T(8,128)S(1)}, u32[]{:S(2)}, u32[]{:S(2)}) collective-permute-start(f32[16,16,128]{2,1,0:T(8,128)} %copy-done.14), channel_id=1, source_target_pairs={{5,10},{6,9},{9,6},{10,5},{21,26},{22,25},{25,22},{26,21}} | collective-permute-start | bytes 393224 | tf_op jit(solution)/shard_map/ppermute | solution.py:56
  62.1 1.9 %fusion.8 = f32[6,128,128,1]{2,0,1,3:T(8,128)S(1)} fusion(pred[128,128,31]{1,0,2:T(32,128)(4,1)} %iota_compare_fusion, f32[6,1,31]{2,1,0:T(1,128)S(1)} %get-tuple-element.97), kind=kOutput, calls=%fused_computation.7 | convolution fusion | flops 36569088 | bytes 901864 | tf_op jit(solution)/shard_map/oit,gt->goi/dot_general | solution.py:257
  71.0 2.8 %fusion.11.lower = f32[32,32,128]{2,1,0:T(8,128)S(1)} fusion(f32[32,6,4]{0,1,2:T(8,128)S(1)} %convolution_bitcast_fusion.1, f32[32,6,4]{1,0,2:T(8,128)S(1)} %copy.15, f32[6,4,4,128,1]{3,2,1,0,4:T(4,128)S(1)} %convolution_bitcast_fusion), kind=kOutput, calls=%fused_computation.8 | convolution fusion | flops 151224320 | bytes 579584 | tf_op jit(solution)/shard_map/xym,mz->xyz/dot_general | solution.py:282
  73.9 3.3 %collective-permute-done.16.moved = f32[32,32,128]{2,1,0:T(8,128)S(1)} collective-permute-done((f32[32,32,128]{2,1,0:T(8,128)S(1)}, f32[32,32,128]{2,1,0:T(8,128)S(1)}, u32[]{:S(2)}, u32[]{:S(2)}) %collective-permute-start.16) | collective-permute-done | bytes 524320 | tf_op jit(solution)/shard_map/ppermute | solution.py:359
  82.1 2.0 %collective-permute-start.18 = (bf16[32,16,128]{2,1,0:T(8,128)(2,1)S(1)}, bf16[32,16,128]{2,1,0:T(8,128)(2,1)S(1)}, u32[]{:S(2)}, u32[]{:S(2)}) collective-permute-start(bf16[32,16,128]{2,1,0:T(8,128)(2,1)S(1)} %get-tuple-element.80), channel_id=1, source_target_pairs={{0,1},{1,0},{2,3},{3,2},{4,5},{5,4},{6,7},{7,6},{8,9},{9,8},{10,11... | collective-permute-start | bytes 393224 | tf_op jit(solution)/shard_map/ppermute | solution.py:56
  84.2 3.1 %collective-permute-start.19 = (bf16[32,16,128]{2,1,0:T(8,128)(2,1)S(1)}, bf16[32,16,128]{2,1,0:T(8,128)(2,1)S(1)}, u32[]{:S(2)}, u32[]{:S(2)}) collective-permute-start(bf16[32,16,128]{2,1,0:T(8,128)(2,1)S(1)} %get-tuple-element.81), channel_id=1, source_target_pairs={{1,2},{2,1},{5,6},{6,5},{9,10},{10,9},{13,14},{14,13},{17,18},{18,... | collective-permute-start | bytes 393224 | tf_op jit(solution)/shard_map/ppermute | solution.py:56
  87.3 3.2 %collective-permute-start.25 = (bf16[16,32,128]{2,1,0:T(8,128)(2,1)S(1)}, bf16[16,32,128]{2,1,0:T(8,128)(2,1)S(1)}, u32[]{:S(2)}, u32[]{:S(2)}) collective-permute-start(bf16[16,32,128]{2,1,0:T(8,128)(2,1)S(1)} %get-tuple-element.87), channel_id=1, source_target_pairs={{4,8},{5,9},{6,10},{7,11},{8,4},{9,5},{10,6},{11,7},{20,24},{21,25... | collective-permute-start | bytes 393224 | tf_op jit(solution)/shard_map/ppermute | solution.py:56
  90.5 2.7 %collective-permute-start.23 = (bf16[16,16,128]{2,1,0:T(8,128)(2,1)S(1)}, bf16[16,16,128]{2,1,0:T(8,128)(2,1)S(1)}, u32[]{:S(2)}, u32[]{:S(2)}) collective-permute-start(bf16[16,16,128]{2,1,0:T(8,128)(2,1)S(1)} %get-tuple-element.85), channel_id=1, source_target_pairs={{5,10},{6,9},{9,6},{10,5},{21,26},{22,25},{25,22},{26,21}} | collective-permute-start | bytes 196616 | tf_op jit(solution)/shard_map/ppermute | solution.py:56
  93.2 3.8 %collective-permute-done.23.refs_5_ = bf16[16,16,128]{2,1,0:T(8,128)(2,1)S(1)} collective-permute-done((bf16[16,16,128]{2,1,0:T(8,128)(2,1)S(1)}, bf16[16,16,128]{2,1,0:T(8,128)(2,1)S(1)}, u32[]{:S(2)}, u32[]{:S(2)}) %collective-permute-start.23) | collective-permute-done | bytes 65568 | tf_op jit(solution)/shard_map/ppermute | solution.py:56
  97.0 14.7 %shard_map.60 = (f32[32,32,128]{2,1,0:T(8,128)S(1)}, f32[32,16,128]{2,1,0:T(8,128)S(1)}, f32[32,16,128]{2,1,0:T(8,128)S(1)}, f32[16,16,128]{2,1,0:T(8,128)S(1)},...) custom-call(s32[2]{0:T(128)S(1)} %pad_add_fusion.flags, ...), custom_call_target="tpu_custom_call" | custom-call | tf_op jit(solution)/shard_map/pallas_call | solution.py:239
  115.7 2.0 %collective-permute-start.26 = (f32[32,16,128]{2,1,0:T(8,128)S(1)}, f32[32,16,128]{2,1,0:T(8,128)S(1)}, u32[]{:S(2)}, u32[]{:S(2)}) collective-permute-start(f32[32,16,128]{2,1,0:T(8,128)S(1)} %get-tuple-element.89), channel_id=1, source_target_pairs={{0,1},{1,0},{2,3},{3,2},{4,5},{5,4},{6,7},{7,6},{8,9},{9,8},{10,11... | collective-permute-start | bytes 786440 | tf_op jit(solution)/shard_map/ppermute | solution.py:56
  117.7 2.8 %collective-permute-start.27 = (f32[32,16,128]{2,1,0:T(8,128)S(1)}, f32[32,16,128]{2,1,0:T(8,128)S(1)}, u32[]{:S(2)}, u32[]{:S(2)}) collective-permute-start(f32[32,16,128]{2,1,0:T(8,128)S(1)} %get-tuple-element.90), channel_id=1, source_target_pairs={{1,2},{2,1},{5,6},{6,5},{9,10},{10,9},{13,14},{14,13},{17,18},{18,... | collective-permute-start | bytes 786440 | tf_op jit(solution)/shard_map/ppermute | solution.py:56
  120.5 2.0 %collective-permute-start.33 = (f32[16,32,128]{2,1,0:T(8,128)S(1)}, f32[16,32,128]{2,1,0:T(8,128)S(1)}, u32[]{:S(2)}, u32[]{:S(2)}) collective-permute-start(f32[16,32,128]{2,1,0:T(8,128)S(1)} %get-tuple-element.96), channel_id=1, source_target_pairs={{4,8},{5,9},{6,10},{7,11},{8,4},{9,5},{10,6},{11,7},{20,24},{21,25... | collective-permute-start | bytes 786440 | tf_op jit(solution)/shard_map/ppermute | solution.py:56
  122.6 4.1 %collective-permute-start.31 = (f32[16,16,128]{2,1,0:T(8,128)S(1)}, f32[16,16,128]{2,1,0:T(8,128)S(1)}, u32[]{:S(2)}, u32[]{:S(2)}) collective-permute-start(f32[16,16,128]{2,1,0:T(8,128)S(1)} %get-tuple-element.94), channel_id=1, source_target_pairs={{5,10},{6,9},{9,6},{10,5},{21,26},{22,25},{25,22},{26,21}} | collective-permute-start | bytes 393224 | tf_op jit(solution)/shard_map/ppermute | solution.py:56
  126.7 3.1 %collective-permute-done.31.refs_5_ = f32[16,16,128]{2,1,0:T(8,128)S(1)} collective-permute-done((f32[16,16,128]{2,1,0:T(8,128)S(1)}, f32[16,16,128]{2,1,0:T(8,128)S(1)}, u32[]{:S(2)}, u32[]{:S(2)}) %collective-permute-start.31) | collective-permute-done | bytes 131104 | tf_op jit(solution)/shard_map/ppermute | solution.py:56
  132.1 7.7 %collective-permute-done.34.moved = f32[32,32,128]{2,1,0:T(8,128)S(1)} collective-permute-done((f32[32,32,128]{2,1,0:T(8,128)S(1)}, f32[32,32,128]{2,1,0:T(8,128)S(1)}, u32[]{:S(2)}, u32[]{:S(2)}) %collective-permute-start.34) | collective-permute-done | bytes 524320 | tf_op jit(solution)/shard_map/ppermute | solution.py:359
  (141 shorter events, 43.7 us)
Async XLA Ops:
  1.8 15.4 %collective-permute-start.2 = (bf16[16,16,128]{2,1,0:T(8,128)(2,1)S(1)}, bf16[16,16,128]{2,1,0:T(8,128)(2,1)S(1)}, u32[]{:S(2)}, u32[]{:S(2)}) collective-permute-start(bf16[16,16,128]{2,1,0:T(8,128)(2,1)S(1)} %get-tuple-element.54), channel_id=1, source_target_pairs={{0,5},{1,4},{2,7},{3,6},{4,1},{5,0},{6,3},{7,2},{8,13},{9,12},{10,... | collective-permute-start | bytes 196616 | tf_op jit(solution)/shard_map/ppermute | solution.py:56
  2.9 17.6 %collective-permute-start.3 = (bf16[16,16,128]{2,1,0:T(8,128)(2,1)S(1)}, bf16[16,16,128]{2,1,0:T(8,128)(2,1)S(1)}, u32[]{:S(2)}, u32[]{:S(2)}) collective-permute-start(bf16[16,16,128]{2,1,0:T(8,128)(2,1)S(1)} %get-tuple-element.55), channel_id=1, source_target_pairs={{1,6},{2,5},{5,2},{6,1},{9,14},{10,13},{13,10},{14,9},{17,22},{18,... | collective-permute-start | bytes 196616 | tf_op jit(solution)/shard_map/ppermute | solution.py:56
  4.8 18.1 %collective-permute-start.4 = (bf16[16,16,128]{2,1,0:T(8,128)(2,1)S(1)}, bf16[16,16,128]{2,1,0:T(8,128)(2,1)S(1)}, u32[]{:S(2)}, u32[]{:S(2)}) collective-permute-start(bf16[16,16,128]{2,1,0:T(8,128)(2,1)S(1)} %get-tuple-element.56), channel_id=1, source_target_pairs={{4,9},{5,8},{6,11},{7,10},{8,5},{9,4},{10,7},{11,6},{20,25},{21,24... | collective-permute-start | bytes 196616 | tf_op jit(solution)/shard_map/ppermute | solution.py:56
  6.7 10.1 %collective-permute-start = (bf16[32,16,128]{2,1,0:T(8,128)(2,1)S(1)}, bf16[32,16,128]{2,1,0:T(8,128)(2,1)S(1)}, u32[]{:S(2)}, u32[]{:S(2)}) collective-permute-start(bf16[32,16,128]{2,1,0:T(8,128)(2,1)S(1)} %get-tuple-element.52), channel_id=1, source_target_pairs={{0,1},{1,0},{2,3},{3,2},{4,5},{5,4},{6,7},{7,6},{8,9},{9,8},{10,11... | collective-permute-start | bytes 393224 | tf_op jit(solution)/shard_map/ppermute | solution.py:56
  9.0 17.9 %collective-permute-start.1 = (bf16[32,16,128]{2,1,0:T(8,128)(2,1)S(1)}, bf16[32,16,128]{2,1,0:T(8,128)(2,1)S(1)}, u32[]{:S(2)}, u32[]{:S(2)}) collective-permute-start(bf16[32,16,128]{2,1,0:T(8,128)(2,1)S(1)} %get-tuple-element.53), channel_id=1, source_target_pairs={{1,2},{2,1},{5,6},{6,5},{9,10},{10,9},{13,14},{14,13},{17,18},{18,... | collective-permute-start | bytes 393224 | tf_op jit(solution)/shard_map/ppermute | solution.py:56
  16.8 10.2 %collective-permute-start.6 = (bf16[16,32,128]{2,1,0:T(8,128)(2,1)S(1)}, bf16[16,32,128]{2,1,0:T(8,128)(2,1)S(1)}, u32[]{:S(2)}, u32[]{:S(2)}) collective-permute-start(bf16[16,32,128]{2,1,0:T(8,128)(2,1)S(1)} %get-tuple-element.58), channel_id=1, source_target_pairs={{0,4},{1,5},{2,6},{3,7},{4,0},{5,1},{6,2},{7,3},{8,12},{9,13},{10,... | collective-permute-start | bytes 393224 | tf_op jit(solution)/shard_map/ppermute | solution.py:56
  17.2 9.7 %collective-permute-start.7 = (bf16[16,32,128]{2,1,0:T(8,128)(2,1)S(1)}, bf16[16,32,128]{2,1,0:T(8,128)(2,1)S(1)}, u32[]{:S(2)}, u32[]{:S(2)}) collective-permute-start(bf16[16,32,128]{2,1,0:T(8,128)(2,1)S(1)} %get-tuple-element.59), channel_id=1, source_target_pairs={{4,8},{5,9},{6,10},{7,11},{8,4},{9,5},{10,6},{11,7},{20,24},{21,25... | collective-permute-start | bytes 393224 | tf_op jit(solution)/shard_map/ppermute | solution.py:56
  22.9 27.5 %collective-permute-start.17 = (f32[375]{0:T(512)S(1)}, f32[375]{0:T(512)S(1)}, u32[]{:S(2)}, u32[]{:S(2)}) collective-permute-start(f32[375]{0:T(512)S(1)} %pad_maximum_fusion), channel_id=1, source_target_pairs={{0,16},{16,0},{1,17},{17,1},{2,18},{18,2},{3,19},{19,3},{4,20},{20... | collective-permute-start | bytes 4508 | tf_op jit(solution)/shard_map/ppermute | solution.py:334
  44.5 10.0 %collective-permute-start.10 = (f32[16,16,128]{2,1,0:T(8,128)S(1)}, f32[16,16,128]{2,1,0:T(8,128)S(1)}, u32[]{:S(2)}, u32[]{:S(2)}) collective-permute-start(f32[16,16,128]{2,1,0:T(8,128)S(1)} %get-tuple-element.69), channel_id=1, source_target_pairs={{0,5},{1,4},{2,7},{3,6},{4,1},{5,0},{6,3},{7,2},{8,13},{9,12},{10,... | collective-permute-start | bytes 393224 | tf_op jit(solution)/shard_map/ppermute | solution.py:56
  44.5 10.0 %collective-permute-start.11 = (f32[16,16,128]{2,1,0:T(8,128)S(1)}, f32[16,16,128]{2,1,0:T(8,128)S(1)}, u32[]{:S(2)}, u32[]{:S(2)}) collective-permute-start(f32[16,16,128]{2,1,0:T(8,128)S(1)} %get-tuple-element.70), channel_id=1, source_target_pairs={{1,6},{2,5},{5,2},{6,1},{9,14},{10,13},{13,10},{14,9},{17,22},{18,... | collective-permute-start | bytes 393224 | tf_op jit(solution)/shard_map/ppermute | solution.py:56
  46.4 11.4 %collective-permute-start.12 = (f32[16,16,128]{2,1,0:T(8,128)}, f32[16,16,128]{2,1,0:T(8,128)S(1)}, u32[]{:S(2)}, u32[]{:S(2)}) collective-permute-start(f32[16,16,128]{2,1,0:T(8,128)} %get-tuple-element.71), channel_id=1, source_target_pairs={{4,9},{5,8},{6,11},{7,10},{8,5},{9,4},{10,7},{11,6},{20,25},{21,24... | collective-permute-start | bytes 393224 | tf_op jit(solution)/shard_map/ppermute | solution.py:56
  48.3 17.0 %collective-permute-start.8 = (f32[32,16,128]{2,1,0:T(8,128)}, f32[32,16,128]{2,1,0:T(8,128)S(1)}, u32[]{:S(2)}, u32[]{:S(2)}) collective-permute-start(f32[32,16,128]{2,1,0:T(8,128)} %get-tuple-element.67), channel_id=1, source_target_pairs={{0,1},{1,0},{2,3},{3,2},{4,5},{5,4},{6,7},{7,6},{8,9},{9,8},{10,11... | collective-permute-start | bytes 786440 | tf_op jit(solution)/shard_map/ppermute | solution.py:56
  50.3 15.0 %collective-permute-start.9 = (f32[32,16,128]{2,1,0:T(8,128)}, f32[32,16,128]{2,1,0:T(8,128)S(1)}, u32[]{:S(2)}, u32[]{:S(2)}) collective-permute-start(f32[32,16,128]{2,1,0:T(8,128)} %get-tuple-element.68), channel_id=1, source_target_pairs={{1,2},{2,1},{5,6},{6,5},{9,10},{10,9},{13,14},{14,13},{17,18},{18,... | collective-permute-start | bytes 786440 | tf_op jit(solution)/shard_map/ppermute | solution.py:56
  54.5 10.9 %collective-permute-start.14 = (f32[16,32,128]{2,1,0:T(8,128)}, f32[16,32,128]{2,1,0:T(8,128)S(1)}, u32[]{:S(2)}, u32[]{:S(2)}) collective-permute-start(f32[16,32,128]{2,1,0:T(8,128)} %copy-done.13), channel_id=1, source_target_pairs={{0,4},{1,5},{2,6},{3,7},{4,0},{5,1},{6,2},{7,3},{8,12},{9,13},{10,... | collective-permute-start | bytes 786440 | tf_op jit(solution)/shard_map/ppermute | solution.py:56
  55.2 10.2 %collective-permute-start.15 = (f32[16,32,128]{2,1,0:T(8,128)}, f32[16,32,128]{2,1,0:T(8,128)S(1)}, u32[]{:S(2)}, u32[]{:S(2)}) collective-permute-start(f32[16,32,128]{2,1,0:T(8,128)} %copy-done.12), channel_id=1, source_target_pairs={{4,8},{5,9},{6,10},{7,11},{8,4},{9,5},{10,6},{11,7},{20,24},{21,25... | collective-permute-start | bytes 786440 | tf_op jit(solution)/shard_map/ppermute | solution.py:56
  80.2 10.3 %collective-permute-start.22 = (bf16[16,16,128]{2,1,0:T(8,128)(2,1)S(1)}, bf16[16,16,128]{2,1,0:T(8,128)(2,1)S(1)}, u32[]{:S(2)}, u32[]{:S(2)}) collective-permute-start(bf16[16,16,128]{2,1,0:T(8,128)(2,1)S(1)} %get-tuple-element.84), channel_id=1, source_target_pairs={{4,9},{5,8},{6,11},{7,10},{8,5},{9,4},{10,7},{11,6},{20,25},{21,24... | collective-permute-start | bytes 196616 | tf_op jit(solution)/shard_map/ppermute | solution.py:56
  82.1 14.9 %collective-permute-start.18 = (bf16[32,16,128]{2,1,0:T(8,128)(2,1)S(1)}, bf16[32,16,128]{2,1,0:T(8,128)(2,1)S(1)}, u32[]{:S(2)}, u32[]{:S(2)}) collective-permute-start(bf16[32,16,128]{2,1,0:T(8,128)(2,1)S(1)} %get-tuple-element.80), channel_id=1, source_target_pairs={{0,1},{1,0},{2,3},{3,2},{4,5},{5,4},{6,7},{7,6},{8,9},{9,8},{10,11... | collective-permute-start | bytes 393224 | tf_op jit(solution)/shard_map/ppermute | solution.py:56
  84.2 12.8 %collective-permute-start.19 = (bf16[32,16,128]{2,1,0:T(8,128)(2,1)S(1)}, bf16[32,16,128]{2,1,0:T(8,128)(2,1)S(1)}, u32[]{:S(2)}, u32[]{:S(2)}) collective-permute-start(bf16[32,16,128]{2,1,0:T(8,128)(2,1)S(1)} %get-tuple-element.81), channel_id=1, source_target_pairs={{1,2},{2,1},{5,6},{6,5},{9,10},{10,9},{13,14},{14,13},{17,18},{18,... | collective-permute-start | bytes 393224 | tf_op jit(solution)/shard_map/ppermute | solution.py:56
  87.2 9.8 %collective-permute-start.24 = (bf16[16,32,128]{2,1,0:T(8,128)(2,1)S(1)}, bf16[16,32,128]{2,1,0:T(8,128)(2,1)S(1)}, u32[]{:S(2)}, u32[]{:S(2)}) collective-permute-start(bf16[16,32,128]{2,1,0:T(8,128)(2,1)S(1)} %get-tuple-element.86), channel_id=1, source_target_pairs={{0,4},{1,5},{2,6},{3,7},{4,0},{5,1},{6,2},{7,3},{8,12},{9,13},{10,... | collective-permute-start | bytes 393224 | tf_op jit(solution)/shard_map/ppermute | solution.py:56
  87.3 9.7 %collective-permute-start.25 = (bf16[16,32,128]{2,1,0:T(8,128)(2,1)S(1)}, bf16[16,32,128]{2,1,0:T(8,128)(2,1)S(1)}, u32[]{:S(2)}, u32[]{:S(2)}) collective-permute-start(bf16[16,32,128]{2,1,0:T(8,128)(2,1)S(1)} %get-tuple-element.87), channel_id=1, source_target_pairs={{4,8},{5,9},{6,10},{7,11},{8,4},{9,5},{10,6},{11,7},{20,24},{21,25... | collective-permute-start | bytes 393224 | tf_op jit(solution)/shard_map/ppermute | solution.py:56
  115.7 14.1 %collective-permute-start.26 = (f32[32,16,128]{2,1,0:T(8,128)S(1)}, f32[32,16,128]{2,1,0:T(8,128)S(1)}, u32[]{:S(2)}, u32[]{:S(2)}) collective-permute-start(f32[32,16,128]{2,1,0:T(8,128)S(1)} %get-tuple-element.89), channel_id=1, source_target_pairs={{0,1},{1,0},{2,3},{3,2},{4,5},{5,4},{6,7},{7,6},{8,9},{9,8},{10,11... | collective-permute-start | bytes 786440 | tf_op jit(solution)/shard_map/ppermute | solution.py:56
  117.7 12.1 %collective-permute-start.27 = (f32[32,16,128]{2,1,0:T(8,128)S(1)}, f32[32,16,128]{2,1,0:T(8,128)S(1)}, u32[]{:S(2)}, u32[]{:S(2)}) collective-permute-start(f32[32,16,128]{2,1,0:T(8,128)S(1)} %get-tuple-element.90), channel_id=1, source_target_pairs={{1,2},{2,1},{5,6},{6,5},{9,10},{10,9},{13,14},{14,13},{17,18},{18,... | collective-permute-start | bytes 786440 | tf_op jit(solution)/shard_map/ppermute | solution.py:56
  120.4 9.3 %collective-permute-start.32 = (f32[16,32,128]{2,1,0:T(8,128)S(1)}, f32[16,32,128]{2,1,0:T(8,128)S(1)}, u32[]{:S(2)}, u32[]{:S(2)}) collective-permute-start(f32[16,32,128]{2,1,0:T(8,128)S(1)} %get-tuple-element.95), channel_id=1, source_target_pairs={{0,4},{1,5},{2,6},{3,7},{4,0},{5,1},{6,2},{7,3},{8,12},{9,13},{10,... | collective-permute-start | bytes 786440 | tf_op jit(solution)/shard_map/ppermute | solution.py:56
  120.5 9.3 %collective-permute-start.33 = (f32[16,32,128]{2,1,0:T(8,128)S(1)}, f32[16,32,128]{2,1,0:T(8,128)S(1)}, u32[]{:S(2)}, u32[]{:S(2)}) collective-permute-start(f32[16,32,128]{2,1,0:T(8,128)S(1)} %get-tuple-element.96), channel_id=1, source_target_pairs={{4,8},{5,9},{6,10},{7,11},{8,4},{9,5},{10,6},{11,7},{20,24},{21,25... | collective-permute-start | bytes 786440 | tf_op jit(solution)/shard_map/ppermute | solution.py:56
  (37 other events, 292.9 us)

commit v3 on v1

--- a/solution.py
+++ b/solution.py
@@ -39,6 +39,30 @@
     high = [(0, 0, 0)] * centre.ndim
     high[dim] = (length - width, 0, 0)
     return centre + lax.pad(below, zero, low) + lax.pad(above, zero, high)
+
+
+def pack_fixed(values, bound):
+    level = jnp.ceil(4.0 * jnp.log2(jnp.maximum(bound, 1e-30)) + 0.01)
+    scale = 32700.0 * jnp.exp2(-0.25 * level)
+    fixed = jnp.round(values * scale).astype(jnp.int16)
+    plane = jnp.broadcast_to(level.astype(jnp.int16), (1,) + values.shape[1:])
+    return jnp.concatenate([fixed, plane], axis=0)
+
+
+def unpack_fixed(packed):
+    level = packed[-1, 0, 0].astype(jnp.float32)
+    step = jnp.exp2(0.25 * level) * (1.0 / 32700.0)
+    return packed[:-1].astype(jnp.float32) * step
+
+
+def bound_of(packed):
+    return jnp.exp2(0.25 * packed[-1, 0, 0].astype(jnp.float32))
+
+
+def swap_fixed(to_below, to_above, bound, axis):
+    below, above = swap_edges(pack_fixed(to_below, bound), pack_fixed(to_above, bound), axis)
+    limit = bound + bound_of(below) + bound_of(above)
+    return unpack_fixed(below), unpack_fixed(above), limit
 
 
 def band(weights, rows, cols, shift):
@@ -113,8 +137,6 @@
     masked = jnp.where(own, images, jnp.zeros_like(images)).astype(jnp.float32)
 
     table_x = band(kern[:, 0], cells_x, cells_x + 2 * halo, radius - halo)
-    table_centre = table_x[:, :, halo : halo + cells_x]
-    table_edges = jnp.concatenate([table_x[:, :, :halo], table_x[:, :, halo + cells_x :]], axis=2)
     table_y = band(kern[:, 1], cells_y, cells_y + 2 * halo, radius - halo)
     table_z = band(kern[:, 2], depth, depth, radius)
 
@@ -128,17 +150,16 @@
         ratio = masked / blurred
         field = jnp.einsum("goz,gxyo->gxyz", table_z, ratio, precision=exact)
         field = jnp.einsum("goy,gxoz->gxyz", table_y, field, precision=exact)
-        edges = jnp.einsum("gox,goyz->xyz", table_edges, field, precision=exact)
-        below, above = swap_edges(edges[:halo], edges[halo:], "fx")
-        centre = jnp.einsum("gox,goyz->xyz", table_centre, field, precision=exact)
-        field = add_edges(centre, below, above, 0)
-        below, above = swap_edges(field[:, :halo], field[:, cells_y + halo :], "fy")
+        field = jnp.einsum("gox,goyz->xyz", table_x, field, precision=exact)
+        below, above, limit = swap_fixed(field[:halo], field[cells_x + halo :], jnp.max(field), "fx")
+        field = add_edges(field[halo : cells_x + halo], below, above, 0)
+        below, above, _ = swap_fixed(field[:, :halo], field[:, cells_y + halo :], limit, "fy")
         field = add_edges(field[:, halo : cells_y + halo], below, above, 1)
-        correction = field
-        moving = field
+        moving = pack_fixed(field, jnp.max(field))
+        correction = unpack_fixed(moving)
         for _ in range(groups - 1):
             moving = lax.ppermute(moving, "view", swap)
-            correction = correction + moving
+            correction = correction + unpack_fixed(moving)
         joined = joined * (correction + 0.5) / lower_part
     return joined
 

time: 128 us -> 131 us (1.023)
  between operations: 0.78 us -> 11.8 us
  starting transfers between devices: 30.1 us -> 23 us
  waiting for transfers between devices: 44.6 us -> 47.8 us
  matrix products: 31.6 us -> 29.6 us
    ppermute x8, waiting for transfers between devices: 27.5 us -> 33.6 us  [swap_edges(): second = lax.ppermute(jnp.where(even, to_below, to_above), axis, pairs(1))]
    ppermute x8, starting transfers between devices: 24.9 us -> 19.8 us  [swap_edges(): second = lax.ppermute(jnp.where(even, to_below, to_above), axis, pairs(1))]
    dot_general x4 -> x2, matrix products: 11.3 us -> 7.27 us  [body(): field = jnp.einsum('gox,goyz->xyz', table_x, field, precision=exact)]
    ppermute x2, waiting for transfers between devices: 13.2 us -> 9.72 us  [body(): moving = lax.ppermute(moving, 'view', swap)]
    slice x3 -> x10, local copies, waits for them, and re-layouts: 2.36 us -> 5.29 us  [unpack_fixed(): level = packed[-1, 0, 0].astype(jnp.float32)]
    ppermute x2, starting transfers between devices: 3.11 us -> 1.19 us  [body(): moving = lax.ppermute(moving, 'view', swap)]
    reduce_max x0 -> x2, other arithmetic: none -> 1.54 us  [body(): moving = pack_fixed(field, jnp.max(field))]
    slice x1, local copies, waits for them, and re-layouts: 1.42 us -> 0.01 us  [weight_of(): table_z = band(kern[:, 2], depth, depth, (taps - 1) // 2)]
  transfers between devices with their start and end apart: 19 -> 19, of which waited for: 12 -> 14; matrix products, arithmetic and copies ran while one was open for 22% -> 9% of each run, Pallas kernels for 0% -> 0%
where the time goes in v3:
time: 131 us
  waiting for transfers between devices  47.8 us (36%)
  matrix products  29.6 us (23%)
  starting transfers between devices  23 us (18%)
  between operations  11.8 us (9%)
  local copies, waits for them, and re-layouts  9.41 us (7%)
  other arithmetic  8.88 us (7%)
    ppermute x8, waiting for transfers between devices, swap_edges(): second = lax.ppermute(jnp.where(even, to_below, to_above), axis, pairs(1))  33.6 us
    ppermute x8, starting transfers between devices, swap_edges(): second = lax.ppermute(jnp.where(even, to_below, to_above), axis, pairs(1))  19.8 us
    ppermute x2, waiting for transfers between devices, body(): moving = lax.ppermute(moving, 'view', swap)  9.72 us
    dot_general x2, matrix products, body(): field = jnp.einsum('gox,goyz->xyz', table_x, field, precision=exact)  7.27 us
    dot_general x2, matrix products, body(): field = jnp.einsum('goy,gxyz->gxoz', table_y, field, precision=exact)  5.48 us
    slice x10, local copies, waits for them, and re-layouts, unpack_fixed(): level = packed[-1, 0, 0].astype(jnp.float32)  5.29 us
    ppermute x8, waiting for transfers between devices, swap_edges(): first = lax.ppermute(jnp.where(even, to_above, to_below), axis, pairs(0))  4.39 us
    dot_general x4, matrix products, band(): jnp.einsum('oit,gt->goi', picks, weights, precision=lax.Precision.HIGHEST)  3.7 us
  transfers between devices with their start and end apart: 19, of which 14 were waited for; matrix products, arithmetic and copies ran while one was open for 9% of the time, Pallas kernels for 0%

profile of v3, /device:TPU:20, one launch (start us, length us, event | category | flops | bytes accessed | tf_op | source)
XLA Modules:
  0.0 130.5 jit_solution(15632394266909845019)
XLA Ops:
  1.4 2.4 %collective-permute-start = (bf16[32,16,128]{2,0,1:T(8,128)(2,1)S(1)}, bf16[32,16,128]{2,0,1:T(8,128)(2,1)S(1)}, u32[]{:S(2)}, u32[]{:S(2)}) collective-permute-start(bf16[32,16,128]{2,0,1:T(8,128)(2,1)S(1)} %get-tuple-element.49), channel_id=1, source_target_pairs={{1,2},{2,1},{5,6},{6,5},{9,10},{10,9},{13,14},{14,13},{17,18},{18,... | collective-permute-start | bytes 393224 | tf_op jit(solution)/shard_map/ppermute | solution.py:20
  11.1 2.1 %collective-permute-start.2 = (bf16[16,64,128]{2,0,1:T(8,128)(2,1)S(1)}, bf16[16,64,128]{2,0,1:T(8,128)(2,1)S(1)}, u32[]{:S(2)}, u32[]{:S(2)}) collective-permute-start(bf16[16,64,128]{2,0,1:T(8,128)(2,1)S(1)} %get-tuple-element.33), channel_id=1, source_target_pairs={{4,8},{8,4},{5,9},{9,5},{6,10},{10,6},{7,11},{11,7},{20,24},{24,20... | collective-permute-start | bytes 786440 | tf_op jit(solution)/shard_map/ppermute | solution.py:20
  13.4 5.4 %collective-permute-done.2 = bf16[16,64,128]{2,0,1:T(8,128)(2,1)S(1)} collective-permute-done((bf16[16,64,128]{2,0,1:T(8,128)(2,1)S(1)}, bf16[16,64,128]{2,0,1:T(8,128)(2,1)S(1)}, u32[]{:S(2)}, u32[]{:S(2)}) %collective-permute-start.2) | collective-permute-done | bytes 262176 | tf_op jit(solution)/shard_map/ppermute | solution.py:20
  19.8 2.7 %fusion.6 = f32[3,32,128,32]{2,3,1,0:T(8,128)S(1)} fusion(f32[3,32,64,128]{3,1,2,0:T(8,128)S(1)} %fusion.31, f32[3,32,64,1]{2,0,1,3:T(4,128)S(1)} %convolution_bitcast_fusion.2), kind=kOutput, calls=%fused_computation.6 | convolution fusion | flops 150994944 | bytes 4743168 | tf_op jit(solution)/shard_map/goy,gxyz->gxoz/dot_general | solution.py:148
  26.1 3.6 %fusion.124 = (f32[]{:T(128)}, f32[64,64,128]{2,0,1:T(8,128)S(1)}) fusion(f32[3,32,64,128]{3,2,1,0:T(8,128)S(1)} %convolution_bitcast_fusion.1, f32[3,32,64]{2,0,1:T(4,128)S(1)} %fusion.59), kind=kOutput, calls=%fused_computation.214 | convolution fusion | flops 302514176 | bytes 5267460 | tf_op jit(solution)/shard_map/gox,goyz->xyz/dot_general | solution.py:153
  30.7 1.9 %collective-permute-start.4 = (s16[17,64,128]{2,0,1:T(8,128)(2,1)S(1)}, s16[17,64,128]{2,0,1:T(8,128)(2,1)S(1)}, u32[]{:S(2)}, u32[]{:S(2)}) collective-permute-start(s16[17,64,128]{2,0,1:T(8,128)(2,1)S(1)} %get-tuple-element.29), channel_id=1, source_target_pairs={{4,8},{8,4},{5,9},{9,5},{6,10},{10,6},{7,11},{11,7},{20,24},{24,20... | collective-permute-start | bytes 835592 | tf_op jit(solution)/shard_map/ppermute | solution.py:20
  34.6 5.3 %collective-permute-done.4 = s16[17,64,128]{2,0,1:T(8,128)(2,1)S(1)} collective-permute-done((s16[17,64,128]{2,0,1:T(8,128)(2,1)S(1)}, s16[17,64,128]{2,0,1:T(8,128)(2,1)S(1)}, u32[]{:S(2)}, u32[]{:S(2)}) %collective-permute-start.4) | collective-permute-done | bytes 278560 | tf_op jit(solution)/shard_map/ppermute | solution.py:20
  43.8 3.7 %collective-permute-start.6 = (s16[33,16,128]{2,0,1:T(8,128)(2,1)S(1)}, s16[33,16,128]{2,0,1:T(8,128)(2,1)S(1)}, u32[]{:S(2)}, u32[]{:S(2)}) collective-permute-start(s16[33,16,128]{2,0,1:T(8,128)(2,1)S(1)} %get-tuple-element.45), channel_id=1, source_target_pairs={{1,2},{2,1},{5,6},{6,5},{9,10},{10,9},{13,14},{14,13},{17,18},{18,... | collective-permute-start | bytes 405512 | tf_op jit(solution)/shard_map/ppermute | solution.py:20
  47.8 2.4 %fusion.24 = f32[6,128,128,1]{2,0,1,3:T(8,128)} fusion(s32[128,128]{1,0:T(8,128)} %copy-done.6, f32[6,1,31]{2,1,0:T(1,128)S(1)} %get-tuple-element.51), kind=kOutput, calls=%fused_computation.25 | convolution fusion | flops 37076992 | bytes 459496 | tf_op jit(solution)/shard_map/oit,gt->goi/dot_general | solution.py:76
  51.0 1.9 %collective-permute-done.7 = s16[33,16,128]{2,0,1:T(8,128)(2,1)S(1)} collective-permute-done((s16[33,16,128]{2,0,1:T(8,128)(2,1)S(1)}, s16[33,16,128]{2,0,1:T(8,128)(2,1)S(1)}, u32[]{:S(2)}, u32[]{:S(2)}) %collective-permute-start.7) | collective-permute-done | bytes 135200 | tf_op jit(solution)/shard_map/ppermute | solution.py:19
  58.0 2.8 %fusion.25 = f32[32,32,128]{2,1,0:T(8,128)S(1)} fusion(f32[32,6,4]{0,1,2:T(8,128)S(1)} %copy-done.12, f32[32,6,4]{1,0,2:T(8,128)S(1)} %copy.52, f32[6,4,4,128,1]{3,2,1,0,4:T(4,128)S(1)} %convolution_bitcast_fusion.3), kind=kOutput, calls=%fused_computation.26 | convolution fusion | flops 151093248 | bytes 579584 | tf_op jit(solution)/shard_map/xym,mz->xyz/dot_general | solution.py:102
  60.8 3.2 %collective-permute-done.8 = s16[33,32,128]{2,0,1:T(8,128)(2,1)S(1)} collective-permute-done((s16[33,32,128]{2,0,1:T(8,128)(2,1)S(1)}, s16[33,32,128]{2,0,1:T(8,128)(2,1)S(1)}, u32[]{:S(2)}, u32[]{:S(2)}) %collective-permute-start.8) | collective-permute-done | bytes 270368 | tf_op jit(solution)/shard_map/ppermute | solution.py:161
  66.0 2.4 %collective-permute-start.10 = (bf16[32,16,128]{2,0,1:T(8,128)(2,1)S(1)}, bf16[32,16,128]{2,0,1:T(8,128)(2,1)S(1)}, u32[]{:S(2)}, u32[]{:S(2)}) collective-permute-start(bf16[32,16,128]{2,0,1:T(8,128)(2,1)S(1)} %get-tuple-element.43), channel_id=1, source_target_pairs={{1,2},{2,1},{5,6},{6,5},{9,10},{10,9},{13,14},{14,13},{17,18},{18,... | collective-permute-start | bytes 393224 | tf_op jit(solution)/shard_map/ppermute | solution.py:20
  68.4 4.4 %collective-permute-done.10 = bf16[32,16,128]{2,0,1:T(8,128)(2,1)S(1)} collective-permute-done((bf16[32,16,128]{2,0,1:T(8,128)(2,1)S(1)}, bf16[32,16,128]{2,0,1:T(8,128)(2,1)S(1)}, u32[]{:S(2)}, u32[]{:S(2)}) %collective-permute-start.10) | collective-permute-done | bytes 131104 | tf_op jit(solution)/shard_map/ppermute | solution.py:20
  73.6 1.9 %collective-permute-start.12 = (bf16[16,64,128]{2,0,1:T(8,128)(2,1)S(1)}, bf16[16,64,128]{2,0,1:T(8,128)(2,1)S(1)}, u32[]{:S(2)}, u32[]{:S(2)}) collective-permute-start(bf16[16,64,128]{2,0,1:T(8,128)(2,1)S(1)} %get-tuple-element.27), channel_id=1, source_target_pairs={{4,8},{8,4},{5,9},{9,5},{6,10},{10,6},{7,11},{11,7},{20,24},{24,20... | collective-permute-start | bytes 786440 | tf_op jit(solution)/shard_map/ppermute | solution.py:20
  75.6 5.7 %collective-permute-done.12 = bf16[16,64,128]{2,0,1:T(8,128)(2,1)S(1)} collective-permute-done((bf16[16,64,128]{2,0,1:T(8,128)(2,1)S(1)}, bf16[16,64,128]{2,0,1:T(8,128)(2,1)S(1)}, u32[]{:S(2)}, u32[]{:S(2)}) %collective-permute-start.12) | collective-permute-done | bytes 262176 | tf_op jit(solution)/shard_map/ppermute | solution.py:20
  82.3 2.7 %fusion.2 = f32[3,32,128,32]{2,3,1,0:T(8,128)S(1)} fusion(f32[3,32,64,128]{3,1,2,0:T(8,128)S(1)} %fusion.36, f32[3,32,64,1]{2,0,1,3:T(4,128)S(1)} %convolution_bitcast_fusion.2), kind=kOutput, calls=%fused_computation.2 | convolution fusion | flops 150994944 | bytes 4743168 | tf_op jit(solution)/shard_map/goy,gxyz->gxoz/dot_general | solution.py:148
  88.5 3.7 %fusion.125 = (f32[]{:T(128)}, f32[64,64,128]{2,0,1:T(8,128)S(1)}) fusion(f32[3,32,64,128]{3,2,1,0:T(8,128)S(1)} %convolution_bitcast_fusion, f32[3,32,64]{2,0,1:T(4,128)S(1)} %fusion.59), kind=kOutput, calls=%fused_computation.215 | convolution fusion | flops 302514176 | bytes 5267460 | tf_op jit(solution)/shard_map/gox,goyz->xyz/dot_general | solution.py:153
  93.3 1.9 %collective-permute-start.14 = (s16[17,64,128]{2,0,1:T(8,128)(2,1)S(1)}, s16[17,64,128]{2,0,1:T(8,128)(2,1)S(1)}, u32[]{:S(2)}, u32[]{:S(2)}) collective-permute-start(s16[17,64,128]{2,0,1:T(8,128)(2,1)S(1)} %get-tuple-element.23), channel_id=1, source_target_pairs={{4,8},{8,4},{5,9},{9,5},{6,10},{10,6},{7,11},{11,7},{20,24},{24,20... | collective-permute-start | bytes 835592 | tf_op jit(solution)/shard_map/ppermute | solution.py:20
  95.3 7.1 %collective-permute-done.14 = s16[17,64,128]{2,0,1:T(8,128)(2,1)S(1)} collective-permute-done((s16[17,64,128]{2,0,1:T(8,128)(2,1)S(1)}, s16[17,64,128]{2,0,1:T(8,128)(2,1)S(1)}, u32[]{:S(2)}, u32[]{:S(2)}) %collective-permute-start.14) | collective-permute-done | bytes 278560 | tf_op jit(solution)/shard_map/ppermute | solution.py:20
  106.0 3.5 %collective-permute-start.16 = (s16[33,16,128]{2,0,1:T(8,128)(2,1)S(1)}, s16[33,16,128]{2,0,1:T(8,128)(2,1)S(1)}, u32[]{:S(2)}, u32[]{:S(2)}) collective-permute-start(s16[33,16,128]{2,0,1:T(8,128)(2,1)S(1)} %get-tuple-element.39), channel_id=1, source_target_pairs={{1,2},{2,1},{5,6},{6,5},{9,10},{10,9},{13,14},{14,13},{17,18},{18,... | collective-permute-start | bytes 405512 | tf_op jit(solution)/shard_map/ppermute | solution.py:20
  109.6 3.6 %collective-permute-done.16 = s16[33,16,128]{2,0,1:T(8,128)(2,1)S(1)} collective-permute-done((s16[33,16,128]{2,0,1:T(8,128)(2,1)S(1)}, s16[33,16,128]{2,0,1:T(8,128)(2,1)S(1)}, u32[]{:S(2)}, u32[]{:S(2)}) %collective-permute-start.16) | collective-permute-done | bytes 135200 | tf_op jit(solution)/shard_map/ppermute | solution.py:20
  119.9 6.5 %collective-permute-done.18 = s16[33,32,128]{2,0,1:T(8,128)(2,1)S(1)} collective-permute-done((s16[33,32,128]{2,0,1:T(8,128)(2,1)S(1)}, s16[33,32,128]{2,0,1:T(8,128)(2,1)S(1)}, u32[]{:S(2)}, u32[]{:S(2)}) %collective-permute-start.18) | collective-permute-done | bytes 270368 | tf_op jit(solution)/shard_map/ppermute | solution.py:161
  127.7 1.7 %multiply_divide_fusion = f32[32,32,128]{2,0,1:T(8,128)S(1)} fusion(s16[32,32,128]{2,0,1:T(8,128)(2,1)S(1)} %round-nearest-even_convert_fusion, f32[32,32,128]{2,1,0:T(8,128)S(1)} %copy-done.3, s16[33,32,128]{2,0,1:T(8,128)(2,1)S(1)} %collective-permute-done.18, f32[]{:T(128)} %bitcast.43, f32[]{:T(128)S(6)} %mul.361, f32[]{:T(128)} %bitcast.15, ...), kind=kLoop, calls=%fused_computation.76 | loop fusion | flops 2228224 | bytes 2621456 | tf_op jit(solution)/shard_map/div | solution.py:163
  (141 shorter events, 36.3 us)
Async XLA Ops:
  0.0 9.0 %copy-start.8 = (s32[3,4,4]{2,1,0:T(4,128)S(1)}, s32[3,4,4]{2,1,0:T(4,128)}, u32[]{:S(2)}) copy-start(s32[3,4,4]{2,1,0:T(4,128)} %param.9) | copy-start | bytes 580
  1.4 7.1 %collective-permute-start = (bf16[32,16,128]{2,0,1:T(8,128)(2,1)S(1)}, bf16[32,16,128]{2,0,1:T(8,128)(2,1)S(1)}, u32[]{:S(2)}, u32[]{:S(2)}) collective-permute-start(bf16[32,16,128]{2,0,1:T(8,128)(2,1)S(1)} %get-tuple-element.49), channel_id=1, source_target_pairs={{1,2},{2,1},{5,6},{6,5},{9,10},{10,9},{13,14},{14,13},{17,18},{18,... | collective-permute-start | bytes 393224 | tf_op jit(solution)/shard_map/ppermute | solution.py:20
  3.8 5.0 %collective-permute-start.1 = (bf16[32,16,128]{2,0,1:T(8,128)(2,1)S(1)}, bf16[32,16,128]{2,0,1:T(8,128)(2,1)S(1)}, u32[]{:S(2)}, u32[]{:S(2)}) collective-permute-start(bf16[32,16,128]{2,0,1:T(8,128)(2,1)S(1)} %get-tuple-element.50), channel_id=1, source_target_pairs={{0,1},{1,0},{2,3},{3,2},{4,5},{5,4},{6,7},{7,6},{8,9},{9,8},{10,11... | collective-permute-start | bytes 393224 | tf_op jit(solution)/shard_map/ppermute | solution.py:19
  9.2 4.1 %collective-permute-start.9 = (f32[375]{0:T(512)S(1)}, f32[375]{0:T(512)S(1)}, u32[]{:S(2)}, u32[]{:S(2)}) collective-permute-start(f32[375]{0:T(512)S(1)} %pad_maximum_fusion.2), channel_id=1, source_target_pairs={{0,16},{16,0},{1,17},{17,1},{2,18},{18,2},{3,19},{19,3},{4,20},{20... | collective-permute-start | bytes 4508 | tf_op jit(solution)/shard_map/ppermute | solution.py:124
  11.1 7.7 %collective-permute-start.2 = (bf16[16,64,128]{2,0,1:T(8,128)(2,1)S(1)}, bf16[16,64,128]{2,0,1:T(8,128)(2,1)S(1)}, u32[]{:S(2)}, u32[]{:S(2)}) collective-permute-start(bf16[16,64,128]{2,0,1:T(8,128)(2,1)S(1)} %get-tuple-element.33), channel_id=1, source_target_pairs={{4,8},{8,4},{5,9},{9,5},{6,10},{10,6},{7,11},{11,7},{20,24},{24,20... | collective-permute-start | bytes 786440 | tf_op jit(solution)/shard_map/ppermute | solution.py:20
  13.2 5.6 %collective-permute-start.3 = (bf16[16,64,128]{2,0,1:T(8,128)(2,1)S(1)}, bf16[16,64,128]{2,0,1:T(8,128)(2,1)S(1)}, u32[]{:S(2)}, u32[]{:S(2)}) collective-permute-start(bf16[16,64,128]{2,0,1:T(8,128)(2,1)S(1)} %get-tuple-element.34), channel_id=1, source_target_pairs={{0,4},{4,0},{8,12},{12,8},{1,5},{5,1},{9,13},{13,9},{2,6},{6,2},{1... | collective-permute-start | bytes 786440 | tf_op jit(solution)/shard_map/ppermute | solution.py:19
  30.7 9.1 %collective-permute-start.4 = (s16[17,64,128]{2,0,1:T(8,128)(2,1)S(1)}, s16[17,64,128]{2,0,1:T(8,128)(2,1)S(1)}, u32[]{:S(2)}, u32[]{:S(2)}) collective-permute-start(s16[17,64,128]{2,0,1:T(8,128)(2,1)S(1)} %get-tuple-element.29), channel_id=1, source_target_pairs={{4,8},{8,4},{5,9},{9,5},{6,10},{10,6},{7,11},{11,7},{20,24},{24,20... | collective-permute-start | bytes 835592 | tf_op jit(solution)/shard_map/ppermute | solution.py:20
  32.7 7.2 %collective-permute-start.5 = (s16[17,64,128]{2,0,1:T(8,128)(2,1)S(1)}, s16[17,64,128]{2,0,1:T(8,128)(2,1)S(1)}, u32[]{:S(2)}, u32[]{:S(2)}) collective-permute-start(s16[17,64,128]{2,0,1:T(8,128)(2,1)S(1)} %get-tuple-element.30), channel_id=1, source_target_pairs={{0,4},{4,0},{8,12},{12,8},{1,5},{5,1},{9,13},{13,9},{2,6},{6,2},{1... | collective-permute-start | bytes 835592 | tf_op jit(solution)/shard_map/ppermute | solution.py:19
  43.8 7.2 %collective-permute-start.6 = (s16[33,16,128]{2,0,1:T(8,128)(2,1)S(1)}, s16[33,16,128]{2,0,1:T(8,128)(2,1)S(1)}, u32[]{:S(2)}, u32[]{:S(2)}) collective-permute-start(s16[33,16,128]{2,0,1:T(8,128)(2,1)S(1)} %get-tuple-element.45), channel_id=1, source_target_pairs={{1,2},{2,1},{5,6},{6,5},{9,10},{10,9},{13,14},{14,13},{17,18},{18,... | collective-permute-start | bytes 405512 | tf_op jit(solution)/shard_map/ppermute | solution.py:20
  47.5 5.4 %collective-permute-start.7 = (s16[33,16,128]{2,0,1:T(8,128)(2,1)S(1)}, s16[33,16,128]{2,0,1:T(8,128)(2,1)S(1)}, u32[]{:S(2)}, u32[]{:S(2)}) collective-permute-start(s16[33,16,128]{2,0,1:T(8,128)(2,1)S(1)} %get-tuple-element.46), channel_id=1, source_target_pairs={{0,1},{1,0},{2,3},{3,2},{4,5},{5,4},{6,7},{7,6},{8,9},{9,8},{10,11... | collective-permute-start | bytes 405512 | tf_op jit(solution)/shard_map/ppermute | solution.py:19
  56.9 7.1 %collective-permute-start.8 = (s16[33,32,128]{2,0,1:T(8,128)(2,1)S(1)}, s16[33,32,128]{2,0,1:T(8,128)(2,1)S(1)}, u32[]{:S(2)}, u32[]{:S(2)}) collective-permute-start(s16[33,32,128]{2,0,1:T(8,128)(2,1)S(1)} %concatenate.51), channel_id=1, source_target_pairs={{0,16},{16,0},{1,17},{17,1},{2,18},{18,2},{3,19},{19,3},{4,20},{20... | collective-permute-start | bytes 811016 | tf_op jit(solution)/shard_map/ppermute | solution.py:161
  60.7 12.8 %copy-start.2 = (f32[32,32,128]{2,1,0:T(8,128)}, f32[32,32,128]{2,1,0:T(8,128)S(1)}, u32[]{:S(2)}) copy-start(f32[32,32,128]{2,1,0:T(8,128)S(1)} %fusion.25) | copy-start | bytes 1572868
  64.0 9.6 %copy-start.4 = (s16[33,32,128]{2,0,1:T(8,128)(2,1)}, s16[33,32,128]{2,0,1:T(8,128)(2,1)S(1)}, u32[]{:S(2)}) copy-start(s16[33,32,128]{2,0,1:T(8,128)(2,1)S(1)} %collective-permute-done.8) | copy-start | bytes 811012
  66.0 6.9 %collective-permute-start.10 = (bf16[32,16,128]{2,0,1:T(8,128)(2,1)S(1)}, bf16[32,16,128]{2,0,1:T(8,128)(2,1)S(1)}, u32[]{:S(2)}, u32[]{:S(2)}) collective-permute-start(bf16[32,16,128]{2,0,1:T(8,128)(2,1)S(1)} %get-tuple-element.43), channel_id=1, source_target_pairs={{1,2},{2,1},{5,6},{6,5},{9,10},{10,9},{13,14},{14,13},{17,18},{18,... | collective-permute-start | bytes 393224 | tf_op jit(solution)/shard_map/ppermute | solution.py:20
  68.4 5.0 %collective-permute-start.11 = (bf16[32,16,128]{2,0,1:T(8,128)(2,1)S(1)}, bf16[32,16,128]{2,0,1:T(8,128)(2,1)S(1)}, u32[]{:S(2)}, u32[]{:S(2)}) collective-permute-start(bf16[32,16,128]{2,0,1:T(8,128)(2,1)S(1)} %get-tuple-element.44), channel_id=1, source_target_pairs={{0,1},{1,0},{2,3},{3,2},{4,5},{5,4},{6,7},{7,6},{8,9},{9,8},{10,11... | collective-permute-start | bytes 393224 | tf_op jit(solution)/shard_map/ppermute | solution.py:19
  73.6 7.7 %collective-permute-start.12 = (bf16[16,64,128]{2,0,1:T(8,128)(2,1)S(1)}, bf16[16,64,128]{2,0,1:T(8,128)(2,1)S(1)}, u32[]{:S(2)}, u32[]{:S(2)}) collective-permute-start(bf16[16,64,128]{2,0,1:T(8,128)(2,1)S(1)} %get-tuple-element.27), channel_id=1, source_target_pairs={{4,8},{8,4},{5,9},{9,5},{6,10},{10,6},{7,11},{11,7},{20,24},{24,20... | collective-permute-start | bytes 786440 | tf_op jit(solution)/shard_map/ppermute | solution.py:20
  75.5 5.8 %collective-permute-start.13 = (bf16[16,64,128]{2,0,1:T(8,128)(2,1)S(1)}, bf16[16,64,128]{2,0,1:T(8,128)(2,1)S(1)}, u32[]{:S(2)}, u32[]{:S(2)}) collective-permute-start(bf16[16,64,128]{2,0,1:T(8,128)(2,1)S(1)} %get-tuple-element.28), channel_id=1, source_target_pairs={{0,4},{4,0},{8,12},{12,8},{1,5},{5,1},{9,13},{13,9},{2,6},{6,2},{1... | collective-permute-start | bytes 786440 | tf_op jit(solution)/shard_map/ppermute | solution.py:19
  93.3 9.1 %collective-permute-start.14 = (s16[17,64,128]{2,0,1:T(8,128)(2,1)S(1)}, s16[17,64,128]{2,0,1:T(8,128)(2,1)S(1)}, u32[]{:S(2)}, u32[]{:S(2)}) collective-permute-start(s16[17,64,128]{2,0,1:T(8,128)(2,1)S(1)} %get-tuple-element.23), channel_id=1, source_target_pairs={{4,8},{8,4},{5,9},{9,5},{6,10},{10,6},{7,11},{11,7},{20,24},{24,20... | collective-permute-start | bytes 835592 | tf_op jit(solution)/shard_map/ppermute | solution.py:20
  95.2 7.2 %collective-permute-start.15 = (s16[17,64,128]{2,0,1:T(8,128)(2,1)S(1)}, s16[17,64,128]{2,0,1:T(8,128)(2,1)S(1)}, u32[]{:S(2)}, u32[]{:S(2)}) collective-permute-start(s16[17,64,128]{2,0,1:T(8,128)(2,1)S(1)} %get-tuple-element.24), channel_id=1, source_target_pairs={{0,4},{4,0},{8,12},{12,8},{1,5},{5,1},{9,13},{13,9},{2,6},{6,2},{1... | collective-permute-start | bytes 835592 | tf_op jit(solution)/shard_map/ppermute | solution.py:19
  106.0 7.2 %collective-permute-start.16 = (s16[33,16,128]{2,0,1:T(8,128)(2,1)S(1)}, s16[33,16,128]{2,0,1:T(8,128)(2,1)S(1)}, u32[]{:S(2)}, u32[]{:S(2)}) collective-permute-start(s16[33,16,128]{2,0,1:T(8,128)(2,1)S(1)} %get-tuple-element.39), channel_id=1, source_target_pairs={{1,2},{2,1},{5,6},{6,5},{9,10},{10,9},{13,14},{14,13},{17,18},{18,... | collective-permute-start | bytes 405512 | tf_op jit(solution)/shard_map/ppermute | solution.py:20
  109.5 18.2 %copy-start.1 = (f32[32,32,128]{2,1,0:T(8,128)S(1)}, f32[32,32,128]{2,1,0:T(8,128)}, u32[]{:S(2)}) copy-start(f32[32,32,128]{2,1,0:T(8,128)} %param.5) | copy-start | bytes 1572868
  109.5 18.2 %copy-start.3 = (f32[32,32,128]{2,1,0:T(8,128)S(1)}, f32[32,32,128]{2,1,0:T(8,128)}, u32[]{:S(2)}) copy-start(f32[32,32,128]{2,1,0:T(8,128)} %copy-done.2) | copy-start | bytes 1572868
  109.6 5.4 %collective-permute-start.17 = (s16[33,16,128]{2,0,1:T(8,128)(2,1)S(1)}, s16[33,16,128]{2,0,1:T(8,128)(2,1)S(1)}, u32[]{:S(2)}, u32[]{:S(2)}) collective-permute-start(s16[33,16,128]{2,0,1:T(8,128)(2,1)S(1)} %get-tuple-element.40), channel_id=1, source_target_pairs={{0,1},{1,0},{2,3},{3,2},{4,5},{5,4},{6,7},{7,6},{8,9},{9,8},{10,11... | collective-permute-start | bytes 405512 | tf_op jit(solution)/shard_map/ppermute | solution.py:19
  119.2 7.1 %collective-permute-start.18 = (s16[33,32,128]{2,0,1:T(8,128)(2,1)S(1)}, s16[33,32,128]{2,0,1:T(8,128)(2,1)S(1)}, u32[]{:S(2)}, u32[]{:S(2)}) collective-permute-start(s16[33,32,128]{2,0,1:T(8,128)(2,1)S(1)} %concatenate.59), channel_id=1, source_target_pairs={{0,16},{16,0},{1,17},{17,1},{2,18},{18,2},{3,19},{19,3},{4,20},{20... | collective-permute-start | bytes 811016 | tf_op jit(solution)/shard_map/ppermute | solution.py:161
  (8 other events, 31.1 us)

commit v4 on v1

--- a/solution.py
+++ b/solution.py
@@ -1,9 +1,17 @@
+import functools
+
 import jax
 import jax.numpy as jnp
 from jax import lax
+from jax.experimental import pallas as pl
+from jax.experimental.pallas import tpu as pltpu
 from jax.sharding import PartitionSpec as P
 
 ITERS = 2
+LANES = 128
+VMEM = pl.BlockSpec(memory_space=pltpu.VMEM)
+SMEM = pl.BlockSpec(memory_space=pltpu.SMEM)
+PARAMS = pltpu.CompilerParams(vmem_limit_bytes=40 * 2**20)
 
 
 def swap_edges(to_below, to_above, axis):
@@ -39,6 +47,102 @@
     high = [(0, 0, 0)] * centre.ndim
     high[dim] = (length - width, 0, 0)
     return centre + lax.pad(below, zero, low) + lax.pad(above, zero, high)
+
+
+def split(value):
+    high = value.astype(jnp.bfloat16)
+    low = (value - high.astype(jnp.float32)).astype(jnp.bfloat16)
+    return high, low
+
+
+def place(blocks, width):
+    per = LANES // width
+    tiles = []
+    for first in range(0, len(blocks), per):
+        tile = blocks[first]
+        for at, block in enumerate(blocks[first + 1 : first + per]):
+            tile = tile + pltpu.roll(block, (at + 1) * width, 1)
+        tiles.append(tile)
+    whole = tiles[0] if len(tiles) == 1 else jnp.concatenate(tiles, axis=1)
+    return whole[:, : len(blocks) * width].astype(jnp.bfloat16)
+
+
+def table_kernel(taps, halo, cells_x, cells_y, psf, tx, txs, tyf, tzf, tzb, tyb):
+    group = psf.shape[0]
+    radius = (taps - 1) // 2
+    depth = tzb.shape[2]
+    wide_x, wide_y = cells_x + 2 * halo, cells_y + 2 * halo
+
+    def parts(value):
+        high = value.astype(jnp.bfloat16).astype(jnp.float32)
+        return high, value - high
+
+    for k in range(group):
+        rows = psf[k]
+        rows = rows / jnp.sum(rows, axis=1, keepdims=True)
+        bands = []
+        for axis, cells in ((0, cells_x), (1, cells_y)):
+            base = jnp.broadcast_to(pltpu.roll(rows[axis : axis + 1], halo - radius, 1), (cells, LANES))
+            bands.append(pltpu.roll(base, 0, 1, stride=1, stride_axis=0))
+        base = jnp.broadcast_to(pltpu.roll(rows[2:3], depth - radius, 1), (depth, depth))
+        band_z = pltpu.roll(base, 0, 1, stride=1, stride_axis=0)
+        gap = lax.broadcasted_iota(jnp.int32, (depth, depth), 1) - lax.broadcasted_iota(
+            jnp.int32, (depth, depth), 0
+        )
+        band_z = jnp.where((gap >= -radius) & (gap <= radius), band_z, 0.0)
+
+        tx[k] = bands[0][:, :wide_x]
+        high, low = parts(bands[0])
+        txs[0, k] = place([high, low], wide_x)
+        txs[1, k] = place([high, jnp.zeros_like(low)], wide_x)
+        high, low = parts(bands[1])
+        tyf[k] = place([high, low, high], wide_y)
+        high, low = parts(band_z)
+        tzb[k, 0:depth, :] = high.astype(jnp.bfloat16)
+        tzb[k, depth : 2 * depth, :] = low.astype(jnp.bfloat16)
+        tzb[k, 2 * depth :, :] = high.astype(jnp.bfloat16)
+        high, low = high.T, low.T
+        tzf[k, 0:depth, :] = high.astype(jnp.bfloat16)
+        tzf[k, depth : 2 * depth, :] = low.astype(jnp.bfloat16)
+        tzf[k, 2 * depth :, :] = high.astype(jnp.bfloat16)
+        square = jnp.concatenate([bands[1], jnp.zeros((LANES - cells_y, LANES), jnp.float32)], axis=0)
+        high, low = parts(square.T[:wide_y])
+        tyb[k] = place([high, low, high], cells_y)
+
+
+def middle_kernel(chunk, spot, lows, lengths, wide, images, tyf, tzf, tzb, tyb, out):
+    k = pl.program_id(0)
+    _, cells_x, cells_y, depth = images.shape
+    wide_y = wide.shape[2]
+    low = lows[k, spot[0], spot[1]]
+    level = lax.broadcasted_iota(jnp.int32, (chunk * cells_y, depth), 1)
+    inside = (level >= low) & (level < low + lengths[k, spot[0], spot[1]])
+    dot = functools.partial(jnp.dot, preferred_element_type=jnp.float32)
+    pair = functools.partial(jnp.concatenate, axis=1)
+    stack = functools.partial(jnp.concatenate, axis=0)
+
+    def three(left, value):
+        high, low = split(value)
+        return dot(left, stack([high, high, low]))
+
+    def along(value, right):
+        high, low = split(value)
+        return dot(pair([high, high, low]), right)
+
+    for first in range(0, cells_x, chunk):
+        rows = []
+        for x in range(first, first + chunk, 2):
+            got = three(tyf[k], pair([wide[0, x], wide[0, x + 1]]))
+            rows += [got[:, :depth], got[:, depth:]]
+        blurred = along(stack(rows), tzf[k])
+        seen = images[0, first : first + chunk].astype(jnp.float32).reshape(chunk * cells_y, depth)
+        spread = along(jnp.where(inside, seen, 0.0) / blurred, tzb[k])
+        for at in range(0, chunk, 2):
+            two = pair([spread[at * cells_y : (at + 1) * cells_y], spread[(at + 1) * cells_y : (at + 2) * cells_y]])
+            high, low = split(three(tyb[k], two))
+            for j in range(2):
+                out[0, 0, first + at + j] = high[:, j * depth : (j + 1) * depth]
+                out[1, 0, first + at + j] = low[:, j * depth : (j + 1) * depth]
 
 
 def band(weights, rows, cols, shift):
@@ -83,55 +187,69 @@
 def body(estimate, images, psf, cover_lo, cover_len):
     group, cells_x, cells_y, depth = images.shape
     taps = psf.shape[-1]
-    radius = (taps - 1) // 2
-    halo = min(-(-radius // 16) * 16, cells_x, cells_y)
-    exact = lax.Precision.HIGH
+    halo = -(-((taps - 1) // 2) // 16) * 16
+    wide_x, wide_y = cells_x + 2 * halo, cells_y + 2 * halo
     groups = lax.axis_size("view")
     swap = [(i, (i + 1) % groups) for i in range(groups)]
-
-    kern = psf / jnp.sum(psf, axis=-1, keepdims=True)
-    start = gather_halo(estimate.astype(jnp.bfloat16), "fy", 1, halo)
-    start, psf, cover_lo, cover_len = lax.optimization_barrier((start, psf, cover_lo, cover_len))
+    bf16, f32 = jnp.bfloat16, jnp.float32
+    shape = jax.ShapeDtypeStruct
+
+    start = gather_halo(estimate.astype(bf16), "fy", 1, halo)
+    psf_late, lo_late, len_late, _ = lax.optimization_barrier((psf, cover_lo, cover_len, start))
+    kern = psf_late / jnp.sum(psf_late, axis=-1, keepdims=True)
     pack = jnp.concatenate(
-        [kern.reshape(-1), cover_lo.reshape(-1).astype(jnp.float32), cover_len.reshape(-1).astype(jnp.float32)]
+        [kern.reshape(-1), lo_late.reshape(-1).astype(f32), len_late.reshape(-1).astype(f32)]
     )
     packs = [pack]
     for _ in range(groups - 1):
         packs.append(lax.ppermute(packs[-1], "view", swap))
     packs = jnp.stack(packs)
+    cells = cover_lo.size
     all_kern = packs[:, : kern.size].reshape((-1,) + kern.shape[1:])
-    cells = cover_lo.size
     all_low = packs[:, kern.size : kern.size + cells].astype(jnp.int32).reshape((-1,) + cover_lo.shape[1:])
-    all_span = packs[:, kern.size + cells :].astype(jnp.int32).reshape((-1,) + cover_len.shape[1:])
-    lower_part = weight_of(all_kern, all_low, all_span, cells_x, cells_y, depth) + 0.5
-
-    block_x, block_y = lax.axis_index("fx"), lax.axis_index("fy")
-    low = lax.dynamic_slice(cover_lo, (0, block_x, block_y), (group, 1, 1))[..., None]
-    span = lax.dynamic_slice(cover_len, (0, block_x, block_y), (group, 1, 1))[..., None]
-    levels = jnp.arange(depth, dtype=jnp.int32)
-    own = (levels >= low) & (levels < low + span)
-    masked = jnp.where(own, images, jnp.zeros_like(images)).astype(jnp.float32)
-
-    table_x = band(kern[:, 0], cells_x, cells_x + 2 * halo, radius - halo)
-    table_centre = table_x[:, :, halo : halo + cells_x]
-    table_edges = jnp.concatenate([table_x[:, :, :halo], table_x[:, :, halo + cells_x :]], axis=2)
-    table_y = band(kern[:, 1], cells_y, cells_y + 2 * halo, radius - halo)
-    table_z = band(kern[:, 2], depth, depth, radius)
+    all_len = packs[:, kern.size + cells :].astype(jnp.int32).reshape((-1,) + cover_len.shape[1:])
+    lower_part = weight_of(all_kern, all_low, all_len, cells_x, cells_y, depth) + 0.5
+
+    spot = jnp.stack([lax.axis_index("fx"), lax.axis_index("fy")]).astype(jnp.int32)
+    padded = jnp.pad(psf, ((0, 0), (0, 0), (0, LANES - taps)))
+    table_x, table_sum, *tables = pl.pallas_call(
+        functools.partial(table_kernel, taps, halo, cells_x, cells_y),
+        out_shape=[
+            shape((group, cells_x, wide_x), f32),
+            shape((2, group, cells_x, 2 * wide_x), bf16),
+            shape((group, cells_y, 3 * wide_y), bf16),
+            shape((group, 3 * depth, depth), bf16),
+            shape((group, 3 * depth, depth), bf16),
+            shape((group, wide_y, 3 * cells_y), bf16),
+        ],
+        in_specs=[VMEM],
+        out_specs=[VMEM] * 6,
+        compiler_params=PARAMS,
+    )(padded)
+    middle = pl.pallas_call(
+        functools.partial(middle_kernel, 8),
+        grid=(group,),
+        out_shape=shape((2, group, cells_x, wide_y, depth), bf16),
+        in_specs=[SMEM, SMEM, SMEM]
+        + [
+            pl.BlockSpec((1, cells_x, wide_y, depth), lambda k: (k, 0, 0, 0)),
+            pl.BlockSpec((1, cells_x, cells_y, depth), lambda k: (k, 0, 0, 0)),
+        ]
+        + [VMEM] * 4,
+        out_specs=pl.BlockSpec((2, 1, cells_x, wide_y, depth), lambda k: (0, k, 0, 0, 0)),
+        compiler_params=PARAMS,
+    )
 
     joined = estimate
     for step in range(ITERS):
-        wide = start if step == 0 else gather_halo(joined.astype(jnp.bfloat16), "fy", 1, halo)
-        wide = gather_halo(wide, "fx", 0, halo).astype(jnp.float32)
-        field = jnp.einsum("gox,xyz->goyz", table_x, wide, precision=exact)
-        field = jnp.einsum("goy,gxyz->gxoz", table_y, field, precision=exact)
-        blurred = jnp.einsum("goz,gxyz->gxyo", table_z, field, precision=exact)
-        ratio = masked / blurred
-        field = jnp.einsum("goz,gxyo->gxyz", table_z, ratio, precision=exact)
-        field = jnp.einsum("goy,gxoz->gxyz", table_y, field, precision=exact)
-        edges = jnp.einsum("gox,goyz->xyz", table_edges, field, precision=exact)
-        below, above = swap_edges(edges[:halo], edges[halo:], "fx")
-        centre = jnp.einsum("gox,goyz->xyz", table_centre, field, precision=exact)
-        field = add_edges(centre, below, above, 0)
+        wide = start if step == 0 else gather_halo(joined.astype(bf16), "fy", 1, halo)
+        wide = gather_halo(wide, "fx", 0, halo).astype(f32)
+        field = jnp.einsum("gox,xyz->goyz", table_x, wide, precision=lax.Precision.HIGH)
+        field = middle(spot, cover_lo, cover_len, field, images, *tables)
+        field = jnp.einsum("sgox,sgoyz->xyz", table_sum, field, preferred_element_type=f32)
+        field = field[:wide_x] + field[wide_x:]
+        below, above = swap_edges(field[:halo], field[cells_x + halo :], "fx")
+        field = add_edges(field[halo : cells_x + halo], below, above, 0)
         below, above = swap_edges(field[:, :halo], field[:, cells_y + halo :], "fy")
         field = add_edges(field[:, halo : cells_y + halo], below, above, 1)
         correction = field

time: 128 us -> 126 us (0.984)
  matrix products: 31.6 us -> 11.1 us
  Pallas kernels: 0 us -> 15.1 us
  waiting for transfers between devices: 44.6 us -> 57 us
  starting transfers between devices: 30.1 us -> 25.1 us
  local copies, waits for them, and re-layouts: 10.7 us -> 8.14 us
  other arithmetic: 8.87 us -> 7.54 us
    dot_general x14 -> x4, matrix products: 25 us -> 6.31 us  [the longest x2 4.4 us: body(): jnp.einsum('sgox,sgoyz->xyz', table_sum, field, preferred_element_type=f32)]
    pallas_call x0 -> x3, Pallas kernels: none -> 15.1 us  [the longest x2 14.3 us: body(): field = middle(spot, cover_lo, cover_len, field, images, *tables)]
    ppermute x8, waiting for transfers between devices: 27.5 us -> 39.4 us  [swap_edges(): second = lax.ppermute(jnp.where(even, to_below, to_above), axis, pairs(1))]
    ppermute x8, starting transfers between devices: 24.9 us -> 19.9 us  [swap_edges(): second = lax.ppermute(jnp.where(even, to_below, to_above), axis, pairs(1))]
    dot_general x0 -> x2, local copies, waits for them, and re-layouts: none -> 3.65 us  [body(): jnp.einsum('gox,xyz->goyz', table_x, wide, precision=lax.Precision.HIGH)]
    slice x4 -> x0, local copies, waits for them, and re-layouts: 2.37 us -> none  [the longest x2 2.27 us: body(): table_centre = table_x[:, :, halo:halo + cells_x]]
    dot_general x4 -> x1, matrix products: 2.89 us -> 1.04 us  [band(): jnp.einsum('oit,gt->goi', picks, weights, precision=lax.Precision.HIGHEST)]
    slice x1, local copies, waits for them, and re-layouts: 1.42 us -> 0.01 us  [weight_of(): table_z = band(kern[:, 2], depth, depth, (taps - 1) // 2)]
  transfers between devices with their start and end apart: 19 -> 19, of which waited for: 12 -> 15; matrix products, arithmetic and copies ran while one was open for 22% -> 6% of each run, Pallas kernels for 0% -> 1%
where the time goes in v4:
time: 126 us; the launch traced here: 125 us
  waiting for transfers between devices  57 us (45%)
  starting transfers between devices  25.1 us (20%)
  Pallas kernels  15.1 us (12%)
  matrix products  11.1 us (9%)
  local copies, waits for them, and re-layouts  8.14 us (6%)
  other arithmetic  7.54 us (6%)
    ppermute x8, waiting for transfers between devices, swap_edges(): second = lax.ppermute(jnp.where(even, to_below, to_above), axis, pairs(1))  39.4 us
    ppermute x8, starting transfers between devices, swap_edges(): second = lax.ppermute(jnp.where(even, to_below, to_above), axis, pairs(1))  19.9 us
    pallas_call x2, Pallas kernels, body(): field = middle(spot, cover_lo, cover_len, field, images, *tables)  14.3 us
    ppermute x2, waiting for transfers between devices, body(): moving = lax.ppermute(moving, 'view', swap)  11.9 us
    ppermute x8, waiting for transfers between devices, swap_edges(): first = lax.ppermute(jnp.where(even, to_above, to_below), axis, pairs(0))  4.43 us
    dot_general x2, matrix products, body(): jnp.einsum('sgox,sgoyz->xyz', table_sum, field, preferred_element_type=f32)  4.4 us
    dot_general x2, local copies, waits for them, and re-layouts, body(): jnp.einsum('gox,xyz->goyz', table_x, wide, precision=lax.Precision.HIGH)  3.65 us
    ppermute x2, starting transfers between devices, body(): moving = lax.ppermute(moving, 'view', swap)  3.12 us
  transfers between devices with their start and end apart: 19, of which 15 were waited for; matrix products, arithmetic and copies ran while one was open for 6% of the time, Pallas kernels for 1%

profile of v4, /device:TPU:20, one launch (start us, length us, event | category | flops | bytes accessed | tf_op | source)
XLA Modules:
  0.0 124.6 jit_solution(9855484986799848952)
XLA Ops:
  1.4 2.4 %collective-permute-start = (bf16[32,16,128]{2,0,1:T(8,128)(2,1)S(1)}, bf16[32,16,128]{2,0,1:T(8,128)(2,1)S(1)}, u32[]{:S(2)}, u32[]{:S(2)}) collective-permute-start(bf16[32,16,128]{2,0,1:T(8,128)(2,1)S(1)} %get-tuple-element.55), channel_id=1, source_target_pairs={{1,2},{2,1},{5,6},{6,5},{9,10},{10,9},{13,14},{14,13},{17,18},{18,... | collective-permute-start | bytes 393224 | tf_op jit(solution)/shard_map/ppermute | solution.py:28
  5.2 3.4 %collective-permute-done = bf16[32,16,128]{2,0,1:T(8,128)(2,1)S(1)} collective-permute-done((bf16[32,16,128]{2,0,1:T(8,128)(2,1)S(1)}, bf16[32,16,128]{2,0,1:T(8,128)(2,1)S(1)}, u32[]{:S(2)}, u32[]{:S(2)}) %collective-permute-start) | collective-permute-done | bytes 131104 | tf_op jit(solution)/shard_map/ppermute | solution.py:28
  9.0 1.9 %collective-permute-start.2 = (bf16[16,64,128]{2,0,1:T(8,128)(2,1)S(1)}, bf16[16,64,128]{2,0,1:T(8,128)(2,1)S(1)}, u32[]{:S(2)}, u32[]{:S(2)}) collective-permute-start(bf16[16,64,128]{2,0,1:T(8,128)(2,1)S(1)} %get-tuple-element.47), channel_id=1, source_target_pairs={{4,8},{8,4},{5,9},{9,5},{6,10},{10,6},{7,11},{11,7},{20,24},{24,20... | collective-permute-start | bytes 786440 | tf_op jit(solution)/shard_map/ppermute | solution.py:28
  17.7 1.8 %copy.35.wide = f32[3,32,64,128]{3,2,1,0:T(8,128)S(1)} copy(f32[3,32,64,128]{3,1,2,0:T(8,128)S(1)} %fusion.24) | data formatting | bytes 6291456 | tf_op jit(solution)/shard_map/gox,xyz->goyz/dot_general | solution.py:247
  19.5 7.2 %shard_map.56 = bf16[2,3,32,64,128]{4,3,2,1,0:T(8,128)(2,1)S(1)} custom-call(s32[2]{0:T(128)S(1)} %pad_add_fusion.spot, s32[3,4,4]{2,1,0:T(4,128)S(1)} %copy-done.2, s32[3,4,4]{2,1,0:T(4,128)S(1)} %copy-done.1, f32[3,32,64,128]{3,2,1,0:T(8,128)S(1)} %copy.35.wide, bf16[3,32,32,128]{3,2,1,0:T(8,128)(2,1)S(1)} %copy-done, ...), custom_call_target="tpu_custom_call" | custom-call | tf_op jit(solution)/shard_map/pallas_call | solution.py:248
  26.7 2.2 %fusion.5 = f32[128,64,128]{2,0,1:T(8,128)S(1)} fusion(bf16[2,3,32,64,128]{4,3,2,1,0:T(8,128)(2,1)S(1)} %shard_map.56, bf16[2,3,32,128]{3,2,1,0:T(8,128)(2,1)S(1)} %get-tuple-element.14), kind=kOutput, calls=%fused_computation.5 | convolution fusion | flops 402653184 | bytes 7389184 | tf_op jit(solution)/shard_map/sgox,sgoyz->xyz/dot_general | solution.py:249
  31.7 2.1 %collective-permute-start.4 = (f32[16,64,128]{2,0,1:T(8,128)}, f32[16,64,128]{2,0,1:T(8,128)S(1)}, u32[]{:S(2)}, u32[]{:S(2)}) collective-permute-start(f32[16,64,128]{2,0,1:T(8,128)} %get-tuple-element.27), channel_id=1, source_target_pairs={{4,8},{8,4},{5,9},{9,5},{6,10},{10,6},{7,11},{11,7},{20,24},{24,20... | collective-permute-start | bytes 1572872 | tf_op jit(solution)/shard_map/ppermute | solution.py:28
  34.3 8.1 %collective-permute-done.4 = f32[16,64,128]{2,0,1:T(8,128)S(1)} collective-permute-done((f32[16,64,128]{2,0,1:T(8,128)}, f32[16,64,128]{2,0,1:T(8,128)S(1)}, u32[]{:S(2)}, u32[]{:S(2)}) %collective-permute-start.4) | collective-permute-done | bytes 524320 | tf_op jit(solution)/shard_map/ppermute | solution.py:28
  43.5 3.7 %collective-permute-start.6 = (f32[32,16,128]{2,0,1:T(8,128)}, f32[32,16,128]{2,0,1:T(8,128)S(1)}, u32[]{:S(2)}, u32[]{:S(2)}) collective-permute-start(f32[32,16,128]{2,0,1:T(8,128)} %get-tuple-element.33), channel_id=1, source_target_pairs={{1,2},{2,1},{5,6},{6,5},{9,10},{10,9},{13,14},{14,13},{17,18},{18,... | collective-permute-start | bytes 786440 | tf_op jit(solution)/shard_map/ppermute | solution.py:28
  48.7 3.3 %collective-permute-done.6 = f32[32,16,128]{2,0,1:T(8,128)S(1)} collective-permute-done((f32[32,16,128]{2,0,1:T(8,128)}, f32[32,16,128]{2,0,1:T(8,128)S(1)}, u32[]{:S(2)}, u32[]{:S(2)}) %collective-permute-start.6) | collective-permute-done | bytes 262176 | tf_op jit(solution)/shard_map/ppermute | solution.py:28
  52.0 1.9 %collective-permute-done.7 = f32[32,16,128]{2,0,1:T(8,128)} collective-permute-done((f32[32,16,128]{2,0,1:T(8,128)}, f32[32,16,128]{2,0,1:T(8,128)}, u32[]{:S(2)}, u32[]{:S(2)}) %collective-permute-start.7) | collective-permute-done | bytes 262176 | tf_op jit(solution)/shard_map/ppermute | solution.py:27
  57.2 2.8 %fusion.15 = f32[32,32,128]{2,1,0:T(8,128)S(1)} fusion(f32[32,6,4]{0,1,2:T(8,128)S(1)} %convolution_bitcast_fusion.1, f32[32,6,4]{1,0,2:T(8,128)S(1)} %copy.39, f32[6,4,4,128,1]{3,2,1,0,4:T(4,128)S(1)} %convolution_bitcast_fusion), kind=kOutput, calls=%fused_computation.14 | convolution fusion | flops 151093248 | bytes 579584 | tf_op jit(solution)/shard_map/xym,mz->xyz/dot_general | solution.py:182
  60.0 4.2 %collective-permute-done.8 = f32[32,32,128]{2,0,1:T(8,128)S(1)} collective-permute-done((f32[32,32,128]{2,0,1:T(8,128)S(1)}, f32[32,32,128]{2,0,1:T(8,128)S(1)}, u32[]{:S(2)}, u32[]{:S(2)}) %collective-permute-start.8) | collective-permute-done | bytes 524320 | tf_op jit(solution)/shard_map/ppermute | solution.py:258
  65.0 2.4 %collective-permute-start.10 = (bf16[32,16,128]{2,0,1:T(8,128)(2,1)S(1)}, bf16[32,16,128]{2,0,1:T(8,128)(2,1)S(1)}, u32[]{:S(2)}, u32[]{:S(2)}) collective-permute-start(bf16[32,16,128]{2,0,1:T(8,128)(2,1)S(1)} %get-tuple-element.51), channel_id=1, source_target_pairs={{1,2},{2,1},{5,6},{6,5},{9,10},{10,9},{13,14},{14,13},{17,18},{18,... | collective-permute-start | bytes 393224 | tf_op jit(solution)/shard_map/ppermute | solution.py:28
  67.4 4.4 %collective-permute-done.10 = bf16[32,16,128]{2,0,1:T(8,128)(2,1)S(1)} collective-permute-done((bf16[32,16,128]{2,0,1:T(8,128)(2,1)S(1)}, bf16[32,16,128]{2,0,1:T(8,128)(2,1)S(1)}, u32[]{:S(2)}, u32[]{:S(2)}) %collective-permute-start.10) | collective-permute-done | bytes 131104 | tf_op jit(solution)/shard_map/ppermute | solution.py:28
  72.5 2.1 %collective-permute-start.12 = (bf16[16,64,128]{2,0,1:T(8,128)(2,1)S(1)}, bf16[16,64,128]{2,0,1:T(8,128)(2,1)S(1)}, u32[]{:S(2)}, u32[]{:S(2)}) collective-permute-start(bf16[16,64,128]{2,0,1:T(8,128)(2,1)S(1)} %get-tuple-element.41), channel_id=1, source_target_pairs={{4,8},{8,4},{5,9},{9,5},{6,10},{10,6},{7,11},{11,7},{20,24},{24,20... | collective-permute-start | bytes 786440 | tf_op jit(solution)/shard_map/ppermute | solution.py:28
  74.7 5.5 %collective-permute-done.12 = bf16[16,64,128]{2,0,1:T(8,128)(2,1)S(1)} collective-permute-done((bf16[16,64,128]{2,0,1:T(8,128)(2,1)S(1)}, bf16[16,64,128]{2,0,1:T(8,128)(2,1)S(1)}, u32[]{:S(2)}, u32[]{:S(2)}) %collective-permute-start.12) | collective-permute-done | bytes 262176 | tf_op jit(solution)/shard_map/ppermute | solution.py:28
  83.0 7.2 %shard_map.57 = bf16[2,3,32,64,128]{4,3,2,1,0:T(8,128)(2,1)S(1)} custom-call(s32[2]{0:T(128)S(1)} %pad_add_fusion.spot, s32[3,4,4]{2,1,0:T(4,128)S(1)} %copy-done.2, s32[3,4,4]{2,1,0:T(4,128)S(1)} %copy-done.1, f32[3,32,64,128]{3,2,1,0:T(8,128)S(1)} %copy.46.wide, bf16[3,32,32,128]{3,2,1,0:T(8,128)(2,1)S(1)} %copy-done, ...), custom_call_target="tpu_custom_call" | custom-call | tf_op jit(solution)/shard_map/pallas_call | solution.py:248
  90.2 2.2 %fusion.8 = f32[128,64,128]{2,0,1:T(8,128)S(1)} fusion(bf16[2,3,32,64,128]{4,3,2,1,0:T(8,128)(2,1)S(1)} %shard_map.57, bf16[2,3,32,128]{3,2,1,0:T(8,128)(2,1)S(1)} %get-tuple-element.14), kind=kOutput, calls=%fused_computation.6 | convolution fusion | flops 402653184 | bytes 7389184 | tf_op jit(solution)/shard_map/sgox,sgoyz->xyz/dot_general | solution.py:249
  92.9 1.9 %collective-permute-start.14 = (f32[16,64,128]{2,0,1:T(8,128)S(1)}, f32[16,64,128]{2,0,1:T(8,128)S(1)}, u32[]{:S(2)}, u32[]{:S(2)}) collective-permute-start(f32[16,64,128]{2,0,1:T(8,128)S(1)} %get-tuple-element.25), channel_id=1, source_target_pairs={{4,8},{8,4},{5,9},{9,5},{6,10},{10,6},{7,11},{11,7},{20,24},{24,20... | collective-permute-start | bytes 1572872 | tf_op jit(solution)/shard_map/ppermute | solution.py:28
  94.9 8.5 %collective-permute-done.14 = f32[16,64,128]{2,0,1:T(8,128)S(1)} collective-permute-done((f32[16,64,128]{2,0,1:T(8,128)S(1)}, f32[16,64,128]{2,0,1:T(8,128)S(1)}, u32[]{:S(2)}, u32[]{:S(2)}) %collective-permute-start.14) | collective-permute-done | bytes 524320 | tf_op jit(solution)/shard_map/ppermute | solution.py:28
  103.7 3.5 %collective-permute-start.16 = (f32[32,16,128]{2,0,1:T(8,128)S(1)}, f32[32,16,128]{2,0,1:T(8,128)S(1)}, u32[]{:S(2)}, u32[]{:S(2)}) collective-permute-start(f32[32,16,128]{2,0,1:T(8,128)S(1)} %get-tuple-element.29), channel_id=1, source_target_pairs={{1,2},{2,1},{5,6},{6,5},{9,10},{10,9},{13,14},{14,13},{17,18},{18,... | collective-permute-start | bytes 786440 | tf_op jit(solution)/shard_map/ppermute | solution.py:28
  107.3 4.7 %collective-permute-done.16 = f32[32,16,128]{2,0,1:T(8,128)S(1)} collective-permute-done((f32[32,16,128]{2,0,1:T(8,128)S(1)}, f32[32,16,128]{2,0,1:T(8,128)S(1)}, u32[]{:S(2)}, u32[]{:S(2)}) %collective-permute-start.16) | collective-permute-done | bytes 262176 | tf_op jit(solution)/shard_map/ppermute | solution.py:28
  115.4 7.7 %collective-permute-done.18 = f32[32,32,128]{2,0,1:T(8,128)S(1)} collective-permute-done((f32[32,32,128]{2,0,1:T(8,128)S(1)}, f32[32,32,128]{2,0,1:T(8,128)S(1)}, u32[]{:S(2)}, u32[]{:S(2)}) %collective-permute-start.18) | collective-permute-done | bytes 524320 | tf_op jit(solution)/shard_map/ppermute | solution.py:258
  (98 shorter events, 29.0 us)
Async XLA Ops:
  1.4 9.6 %copy-start.7 = (f32[3,3,31]{2,1,0:T(4,128)S(1)}, f32[3,3,31]{2,1,0:T(4,128)}, u32[]{:S(2)}) copy-start(f32[3,3,31]{2,1,0:T(4,128)} %param.7) | copy-start | bytes 3352
  1.4 9.8 %copy-start.2 = (s32[3,4,4]{2,1,0:T(4,128)S(1)}, s32[3,4,4]{2,1,0:T(4,128)}, u32[]{:S(2)}) copy-start(s32[3,4,4]{2,1,0:T(4,128)} %lows.3) | copy-start | bytes 580
  1.4 9.9 %copy-start.1 = (s32[3,4,4]{2,1,0:T(4,128)S(1)}, s32[3,4,4]{2,1,0:T(4,128)}, u32[]{:S(2)}) copy-start(s32[3,4,4]{2,1,0:T(4,128)} %lengths.3) | copy-start | bytes 580
  1.4 7.1 %collective-permute-start = (bf16[32,16,128]{2,0,1:T(8,128)(2,1)S(1)}, bf16[32,16,128]{2,0,1:T(8,128)(2,1)S(1)}, u32[]{:S(2)}, u32[]{:S(2)}) collective-permute-start(bf16[32,16,128]{2,0,1:T(8,128)(2,1)S(1)} %get-tuple-element.55), channel_id=1, source_target_pairs={{1,2},{2,1},{5,6},{6,5},{9,10},{10,9},{13,14},{14,13},{17,18},{18,... | collective-permute-start | bytes 393224 | tf_op jit(solution)/shard_map/ppermute | solution.py:28
  3.8 5.0 %collective-permute-start.1 = (bf16[32,16,128]{2,0,1:T(8,128)(2,1)S(1)}, bf16[32,16,128]{2,0,1:T(8,128)(2,1)S(1)}, u32[]{:S(2)}, u32[]{:S(2)}) collective-permute-start(bf16[32,16,128]{2,0,1:T(8,128)(2,1)S(1)} %get-tuple-element.56), channel_id=1, source_target_pairs={{0,1},{1,0},{2,3},{3,2},{4,5},{5,4},{6,7},{7,6},{8,9},{9,8},{10,11... | collective-permute-start | bytes 393224 | tf_op jit(solution)/shard_map/ppermute | solution.py:27
  9.0 7.7 %collective-permute-start.2 = (bf16[16,64,128]{2,0,1:T(8,128)(2,1)S(1)}, bf16[16,64,128]{2,0,1:T(8,128)(2,1)S(1)}, u32[]{:S(2)}, u32[]{:S(2)}) collective-permute-start(bf16[16,64,128]{2,0,1:T(8,128)(2,1)S(1)} %get-tuple-element.47), channel_id=1, source_target_pairs={{4,8},{8,4},{5,9},{9,5},{6,10},{10,6},{7,11},{11,7},{20,24},{24,20... | collective-permute-start | bytes 786440 | tf_op jit(solution)/shard_map/ppermute | solution.py:28
  10.9 5.8 %collective-permute-start.3 = (bf16[16,64,128]{2,0,1:T(8,128)(2,1)S(1)}, bf16[16,64,128]{2,0,1:T(8,128)(2,1)S(1)}, u32[]{:S(2)}, u32[]{:S(2)}) collective-permute-start(bf16[16,64,128]{2,0,1:T(8,128)(2,1)S(1)} %get-tuple-element.48), channel_id=1, source_target_pairs={{0,4},{4,0},{8,12},{12,8},{1,5},{5,1},{9,13},{13,9},{2,6},{6,2},{1... | collective-permute-start | bytes 786440 | tf_op jit(solution)/shard_map/ppermute | solution.py:27
  11.4 3.6 %collective-permute-start.9 = (f32[375]{0:T(512)S(1)}, f32[375]{0:T(512)S(1)}, u32[]{:S(2)}, u32[]{:S(2)}) collective-permute-start(f32[375]{0:T(512)S(1)} %pad_maximum_fusion.2), channel_id=1, source_target_pairs={{0,16},{16,0},{1,17},{17,1},{2,18},{18,2},{3,19},{19,3},{4,20},{20... | collective-permute-start | bytes 4508 | tf_op jit(solution)/shard_map/ppermute | solution.py:205
  31.7 10.7 %collective-permute-start.4 = (f32[16,64,128]{2,0,1:T(8,128)}, f32[16,64,128]{2,0,1:T(8,128)S(1)}, u32[]{:S(2)}, u32[]{:S(2)}) collective-permute-start(f32[16,64,128]{2,0,1:T(8,128)} %get-tuple-element.27), channel_id=1, source_target_pairs={{4,8},{8,4},{5,9},{9,5},{6,10},{10,6},{7,11},{11,7},{20,24},{24,20... | collective-permute-start | bytes 1572872 | tf_op jit(solution)/shard_map/ppermute | solution.py:28
  33.8 8.6 %collective-permute-start.5 = (f32[16,64,128]{2,0,1:T(8,128)S(1)}, f32[16,64,128]{2,0,1:T(8,128)S(1)}, u32[]{:S(2)}, u32[]{:S(2)}) collective-permute-start(f32[16,64,128]{2,0,1:T(8,128)S(1)} %get-tuple-element.28), channel_id=1, source_target_pairs={{0,4},{4,0},{8,12},{12,8},{1,5},{5,1},{9,13},{13,9},{2,6},{6,2},{1... | collective-permute-start | bytes 1572872 | tf_op jit(solution)/shard_map/ppermute | solution.py:27
  34.0 8.5 %copy-start.4 = (f32[64,64,128]{2,0,1:T(8,128)S(1)}, f32[64,64,128]{2,0,1:T(8,128)}, u32[]{:S(2)}) copy-start(f32[64,64,128]{2,0,1:T(8,128)} %copy-done.3) | copy-start | bytes 6291460
  43.5 8.5 %collective-permute-start.6 = (f32[32,16,128]{2,0,1:T(8,128)}, f32[32,16,128]{2,0,1:T(8,128)S(1)}, u32[]{:S(2)}, u32[]{:S(2)}) collective-permute-start(f32[32,16,128]{2,0,1:T(8,128)} %get-tuple-element.33), channel_id=1, source_target_pairs={{1,2},{2,1},{5,6},{6,5},{9,10},{10,9},{13,14},{14,13},{17,18},{18,... | collective-permute-start | bytes 786440 | tf_op jit(solution)/shard_map/ppermute | solution.py:28
  47.2 6.8 %collective-permute-start.7 = (f32[32,16,128]{2,0,1:T(8,128)}, f32[32,16,128]{2,0,1:T(8,128)}, u32[]{:S(2)}, u32[]{:S(2)}) collective-permute-start(f32[32,16,128]{2,0,1:T(8,128)} %get-tuple-element.34), channel_id=1, source_target_pairs={{0,1},{1,0},{2,3},{3,2},{4,5},{5,4},{6,7},{7,6},{8,9},{9,8},{10,11... | collective-permute-start | bytes 786440 | tf_op jit(solution)/shard_map/ppermute | solution.py:27
  55.0 9.3 %copy-start.5 = (f32[32,32,128]{2,1,0:T(8,128)S(1)}, f32[32,32,128]{2,1,0:T(8,128)}, u32[]{:S(2)}) copy-start(f32[32,32,128]{2,1,0:T(8,128)} %param.5) | copy-start | bytes 1572868
  55.0 9.2 %collective-permute-start.8 = (f32[32,32,128]{2,0,1:T(8,128)S(1)}, f32[32,32,128]{2,0,1:T(8,128)S(1)}, u32[]{:S(2)}, u32[]{:S(2)}) collective-permute-start(f32[32,32,128]{2,0,1:T(8,128)S(1)} %fusion.45), channel_id=1, source_target_pairs={{0,16},{16,0},{1,17},{17,1},{2,18},{18,2},{3,19},{19,3},{4,20},{20... | collective-permute-start | bytes 1572872 | tf_op jit(solution)/shard_map/ppermute | solution.py:258
  65.0 6.9 %collective-permute-start.10 = (bf16[32,16,128]{2,0,1:T(8,128)(2,1)S(1)}, bf16[32,16,128]{2,0,1:T(8,128)(2,1)S(1)}, u32[]{:S(2)}, u32[]{:S(2)}) collective-permute-start(bf16[32,16,128]{2,0,1:T(8,128)(2,1)S(1)} %get-tuple-element.51), channel_id=1, source_target_pairs={{1,2},{2,1},{5,6},{6,5},{9,10},{10,9},{13,14},{14,13},{17,18},{18,... | collective-permute-start | bytes 393224 | tf_op jit(solution)/shard_map/ppermute | solution.py:28
  67.3 5.0 %collective-permute-start.11 = (bf16[32,16,128]{2,0,1:T(8,128)(2,1)S(1)}, bf16[32,16,128]{2,0,1:T(8,128)(2,1)S(1)}, u32[]{:S(2)}, u32[]{:S(2)}) collective-permute-start(bf16[32,16,128]{2,0,1:T(8,128)(2,1)S(1)} %get-tuple-element.52), channel_id=1, source_target_pairs={{0,1},{1,0},{2,3},{3,2},{4,5},{5,4},{6,7},{7,6},{8,9},{9,8},{10,11... | collective-permute-start | bytes 393224 | tf_op jit(solution)/shard_map/ppermute | solution.py:27
  72.5 7.7 %collective-permute-start.12 = (bf16[16,64,128]{2,0,1:T(8,128)(2,1)S(1)}, bf16[16,64,128]{2,0,1:T(8,128)(2,1)S(1)}, u32[]{:S(2)}, u32[]{:S(2)}) collective-permute-start(bf16[16,64,128]{2,0,1:T(8,128)(2,1)S(1)} %get-tuple-element.41), channel_id=1, source_target_pairs={{4,8},{8,4},{5,9},{9,5},{6,10},{10,6},{7,11},{11,7},{20,24},{24,20... | collective-permute-start | bytes 786440 | tf_op jit(solution)/shard_map/ppermute | solution.py:28
  74.7 5.5 %collective-permute-start.13 = (bf16[16,64,128]{2,0,1:T(8,128)(2,1)S(1)}, bf16[16,64,128]{2,0,1:T(8,128)(2,1)S(1)}, u32[]{:S(2)}, u32[]{:S(2)}) collective-permute-start(bf16[16,64,128]{2,0,1:T(8,128)(2,1)S(1)} %get-tuple-element.42), channel_id=1, source_target_pairs={{0,4},{4,0},{8,12},{12,8},{1,5},{5,1},{9,13},{13,9},{2,6},{6,2},{1... | collective-permute-start | bytes 786440 | tf_op jit(solution)/shard_map/ppermute | solution.py:27
  92.9 10.5 %collective-permute-start.14 = (f32[16,64,128]{2,0,1:T(8,128)S(1)}, f32[16,64,128]{2,0,1:T(8,128)S(1)}, u32[]{:S(2)}, u32[]{:S(2)}) collective-permute-start(f32[16,64,128]{2,0,1:T(8,128)S(1)} %get-tuple-element.25), channel_id=1, source_target_pairs={{4,8},{8,4},{5,9},{9,5},{6,10},{10,6},{7,11},{11,7},{20,24},{24,20... | collective-permute-start | bytes 1572872 | tf_op jit(solution)/shard_map/ppermute | solution.py:28
  94.8 8.6 %collective-permute-start.15 = (f32[16,64,128]{2,0,1:T(8,128)S(1)}, f32[16,64,128]{2,0,1:T(8,128)S(1)}, u32[]{:S(2)}, u32[]{:S(2)}) collective-permute-start(f32[16,64,128]{2,0,1:T(8,128)S(1)} %get-tuple-element.26), channel_id=1, source_target_pairs={{0,4},{4,0},{8,12},{12,8},{1,5},{5,1},{9,13},{13,9},{2,6},{6,2},{1... | collective-permute-start | bytes 1572872 | tf_op jit(solution)/shard_map/ppermute | solution.py:27
  103.7 8.3 %collective-permute-start.16 = (f32[32,16,128]{2,0,1:T(8,128)S(1)}, f32[32,16,128]{2,0,1:T(8,128)S(1)}, u32[]{:S(2)}, u32[]{:S(2)}) collective-permute-start(f32[32,16,128]{2,0,1:T(8,128)S(1)} %get-tuple-element.29), channel_id=1, source_target_pairs={{1,2},{2,1},{5,6},{6,5},{9,10},{10,9},{13,14},{14,13},{17,18},{18,... | collective-permute-start | bytes 786440 | tf_op jit(solution)/shard_map/ppermute | solution.py:28
  107.2 6.4 %collective-permute-start.17 = (f32[32,16,128]{2,0,1:T(8,128)S(1)}, f32[32,16,128]{2,0,1:T(8,128)S(1)}, u32[]{:S(2)}, u32[]{:S(2)}) collective-permute-start(f32[32,16,128]{2,0,1:T(8,128)S(1)} %get-tuple-element.30), channel_id=1, source_target_pairs={{0,1},{1,0},{2,3},{3,2},{4,5},{5,4},{6,7},{7,6},{8,9},{9,8},{10,11... | collective-permute-start | bytes 786440 | tf_op jit(solution)/shard_map/ppermute | solution.py:27
  113.8 9.2 %collective-permute-start.18 = (f32[32,32,128]{2,0,1:T(8,128)S(1)}, f32[32,32,128]{2,0,1:T(8,128)S(1)}, u32[]{:S(2)}, u32[]{:S(2)}) collective-permute-start(f32[32,32,128]{2,0,1:T(8,128)S(1)} %fusion.44), channel_id=1, source_target_pairs={{0,16},{16,0},{1,17},{17,1},{2,18},{18,2},{3,19},{19,3},{4,20},{20... | collective-permute-start | bytes 1572872 | tf_op jit(solution)/shard_map/ppermute | solution.py:258
  (3 other events, 8.4 us)

commit v5 on v3

--- a/solution.py
+++ b/solution.py
@@ -41,28 +41,22 @@
     return centre + lax.pad(below, zero, low) + lax.pad(above, zero, high)
 
 
-def pack_fixed(values, bound):
-    level = jnp.ceil(4.0 * jnp.log2(jnp.maximum(bound, 1e-30)) + 0.01)
+def pack_fixed(values):
+    top = jnp.max(jnp.abs(values), axis=1, keepdims=True)
+    level = jnp.ceil(4.0 * jnp.log2(jnp.maximum(top, 1e-30)) + 0.01)
     scale = 32700.0 * jnp.exp2(-0.25 * level)
     fixed = jnp.round(values * scale).astype(jnp.int16)
-    plane = jnp.broadcast_to(level.astype(jnp.int16), (1,) + values.shape[1:])
-    return jnp.concatenate([fixed, plane], axis=0)
+    return jnp.concatenate([fixed, level.astype(jnp.int16)], axis=1)
 
 
 def unpack_fixed(packed):
-    level = packed[-1, 0, 0].astype(jnp.float32)
-    step = jnp.exp2(0.25 * level) * (1.0 / 32700.0)
-    return packed[:-1].astype(jnp.float32) * step
+    step = jnp.exp2(0.25 * packed[:, -1:].astype(jnp.float32)) * (1.0 / 32700.0)
+    return packed[:, :-1].astype(jnp.float32) * step
 
 
-def bound_of(packed):
-    return jnp.exp2(0.25 * packed[-1, 0, 0].astype(jnp.float32))
-
-
-def swap_fixed(to_below, to_above, bound, axis):
-    below, above = swap_edges(pack_fixed(to_below, bound), pack_fixed(to_above, bound), axis)
-    limit = bound + bound_of(below) + bound_of(above)
-    return unpack_fixed(below), unpack_fixed(above), limit
+def swap_fixed(to_below, to_above, axis):
+    below, above = swap_edges(pack_fixed(to_below), pack_fixed(to_above), axis)
+    return unpack_fixed(below), unpack_fixed(above)
 
 
 def band(weights, rows, cols, shift):
@@ -151,11 +145,11 @@
         field = jnp.einsum("goz,gxyo->gxyz", table_z, ratio, precision=exact)
         field = jnp.einsum("goy,gxoz->gxyz", table_y, field, precision=exact)
         field = jnp.einsum("gox,goyz->xyz", table_x, field, precision=exact)
-        below, above, limit = swap_fixed(field[:halo], field[cells_x + halo :], jnp.max(field), "fx")
+        below, above = swap_fixed(field[:halo], field[cells_x + halo :], "fx")
         field = add_edges(field[halo : cells_x + halo], below, above, 0)
-        below, above, _ = swap_fixed(field[:, :halo], field[:, cells_y + halo :], limit, "fy")
+        below, above = swap_fixed(field[:, :halo], field[:, cells_y + halo :], "fy")
         field = add_edges(field[:, halo : cells_y + halo], below, above, 1)
-        moving = pack_fixed(field, jnp.max(field))
+        moving = pack_fixed(field)
         correction = unpack_fixed(moving)
         for _ in range(groups - 1):
             moving = lax.ppermute(moving, "view", swap)

time: 131 us -> 107 us (0.82)
  between operations: 11.8 us -> 0.82 us
  local copies, waits for them, and re-layouts: 9.41 us -> 3.71 us
  matrix products: 29.6 us -> 25.2 us
  other arithmetic: 8.88 us -> 6.88 us
  waiting for transfers between devices: 47.8 us -> 46.3 us
    slice x10 -> x0, local copies, waits for them, and re-layouts: 5.29 us -> none  [unpack_fixed(): level = packed[-1, 0, 0].astype(jnp.float32)]
    dot_general x4, matrix products: 3.7 us -> 2.06 us  [band(): jnp.einsum('oit,gt->goi', picks, weights, precision=lax.Precision.HIGHEST)]
    dot_general x2, matrix products: 7.27 us -> 5.65 us  [body(): field = jnp.einsum('gox,goyz->xyz', table_x, field, precision=exact)]
  transfers between devices with their start and end apart: 19 -> 19, of which waited for: 14 -> 14; matrix products, arithmetic and copies ran while one was open for 9% -> 8% of each run, Pallas kernels for 0% -> 0%
where the time goes in v5:
time: 107 us; the launch traced here: 106 us
  waiting for transfers between devices  46.3 us (43%)
  matrix products  25.2 us (24%)
  starting transfers between devices  23 us (21%)
  other arithmetic  6.88 us (6%)
  local copies, waits for them, and re-layouts  3.71 us (3%)
    ppermute x8, waiting for transfers between devices, swap_edges(): second = lax.ppermute(jnp.where(even, to_below, to_above), axis, pairs(1))  33.3 us
    ppermute x8, starting transfers between devices, swap_edges(): second = lax.ppermute(jnp.where(even, to_below, to_above), axis, pairs(1))  19.8 us
    ppermute x2, waiting for transfers between devices, body(): moving = lax.ppermute(moving, 'view', swap)  8.62 us
    dot_general x2, matrix products, body(): field = jnp.einsum('gox,goyz->xyz', table_x, field, precision=exact)  5.65 us
    dot_general x2, matrix products, body(): field = jnp.einsum('goy,gxyz->gxoz', table_y, field, precision=exact)  5.48 us
    ppermute x8, waiting for transfers between devices, swap_edges(): first = lax.ppermute(jnp.where(even, to_above, to_below), axis, pairs(0))  4.36 us
    dot_general x2, matrix products, body(): field = jnp.einsum('goy,gxoz->gxyz', table_y, field, precision=exact)  2.87 us
    dot_general x1, matrix products, weight_of(): jnp.einsum('xym,mz->xyz', plane, sums_z.reshape(-1, depth), precision=lax...  2.77 us
  transfers between devices with their start and end apart: 19, of which 14 were waited for; matrix products, arithmetic and copies ran while one was open for 8% of the time, Pallas kernels for 0%

profile of v5, /device:TPU:20, one launch (start us, length us, event | category | flops | bytes accessed | tf_op | source)
XLA Modules:
  0.0 105.9 jit_solution(3393877624673133806)
XLA Ops:
  1.4 2.4 %collective-permute-start = (bf16[32,16,128]{2,0,1:T(8,128)(2,1)S(1)}, bf16[32,16,128]{2,0,1:T(8,128)(2,1)S(1)}, u32[]{:S(2)}, u32[]{:S(2)}) collective-permute-start(bf16[32,16,128]{2,0,1:T(8,128)(2,1)S(1)} %get-tuple-element.57), channel_id=1, source_target_pairs={{1,2},{2,1},{5,6},{6,5},{9,10},{10,9},{13,14},{14,13},{17,18},{18,... | collective-permute-start | bytes 393224 | tf_op jit(solution)/shard_map/ppermute | solution.py:20
  11.1 2.1 %collective-permute-start.2 = (bf16[16,64,128]{2,0,1:T(8,128)(2,1)S(1)}, bf16[16,64,128]{2,0,1:T(8,128)(2,1)S(1)}, u32[]{:S(2)}, u32[]{:S(2)}) collective-permute-start(bf16[16,64,128]{2,0,1:T(8,128)(2,1)S(1)} %get-tuple-element.41), channel_id=1, source_target_pairs={{4,8},{8,4},{5,9},{9,5},{6,10},{10,6},{7,11},{11,7},{20,24},{24,20... | collective-permute-start | bytes 786440 | tf_op jit(solution)/shard_map/ppermute | solution.py:20
  13.4 5.4 %collective-permute-done.2 = bf16[16,64,128]{2,0,1:T(8,128)(2,1)S(1)} collective-permute-done((bf16[16,64,128]{2,0,1:T(8,128)(2,1)S(1)}, bf16[16,64,128]{2,0,1:T(8,128)(2,1)S(1)}, u32[]{:S(2)}, u32[]{:S(2)}) %collective-permute-start.2) | collective-permute-done | bytes 262176 | tf_op jit(solution)/shard_map/ppermute | solution.py:20
  19.8 2.7 %fusion.6 = f32[3,32,128,32]{2,3,1,0:T(8,128)S(1)} fusion(f32[3,32,64,128]{3,1,2,0:T(8,128)S(1)} %fusion.31, f32[3,32,64,1]{2,0,1,3:T(4,128)S(1)} %convolution_bitcast_fusion.2), kind=kOutput, calls=%fused_computation.6 | convolution fusion | flops 150994944 | bytes 4743168 | tf_op jit(solution)/shard_map/goy,gxyz->gxoz/dot_general | solution.py:142
  26.0 2.8 %fusion.12 = f32[64,64,128]{2,0,1:T(8,128)S(1)} fusion(f32[3,32,64,128]{3,2,1,0:T(8,128)S(1)} %convolution_bitcast_fusion.1, f32[3,32,64]{2,0,1:T(4,128)S(1)} %fusion.51), kind=kOutput, calls=%fused_computation.17 | convolution fusion | flops 301989888 | bytes 5267456 | tf_op jit(solution)/shard_map/gox,goyz->xyz/dot_general | solution.py:147
  29.3 1.9 %collective-permute-start.4 = (s16[16,65,128]{2,0,1:T(8,128)(2,1)S(1)}, s16[16,65,128]{2,0,1:T(8,128)(2,1)S(1)}, u32[]{:S(2)}, u32[]{:S(2)}) collective-permute-start(s16[16,65,128]{2,0,1:T(8,128)(2,1)S(1)} %get-tuple-element.33), channel_id=1, source_target_pairs={{4,8},{8,4},{5,9},{9,5},{6,10},{10,6},{7,11},{11,7},{20,24},{24,20... | collective-permute-start | bytes 798728 | tf_op jit(solution)/shard_map/ppermute | solution.py:20
  31.9 5.1 %collective-permute-done.4 = s16[16,65,128]{2,0,1:T(8,128)(2,1)S(1)} collective-permute-done((s16[16,65,128]{2,0,1:T(8,128)(2,1)S(1)}, s16[16,65,128]{2,0,1:T(8,128)(2,1)S(1)}, u32[]{:S(2)}, u32[]{:S(2)}) %collective-permute-start.4) | collective-permute-done | bytes 266272 | tf_op jit(solution)/shard_map/ppermute | solution.py:20
  37.8 3.7 %collective-permute-start.6 = (s16[32,17,128]{2,0,1:T(8,128)(2,1)S(1)}, s16[32,17,128]{2,0,1:T(8,128)(2,1)S(1)}, u32[]{:S(2)}, u32[]{:S(2)}) collective-permute-start(s16[32,17,128]{2,0,1:T(8,128)(2,1)S(1)} %get-tuple-element.49), channel_id=1, source_target_pairs={{1,2},{2,1},{5,6},{6,5},{9,10},{10,9},{13,14},{14,13},{17,18},{18,... | collective-permute-start | bytes 417800 | tf_op jit(solution)/shard_map/ppermute | solution.py:20
  42.6 2.1 %collective-permute-done.6 = s16[32,17,128]{2,0,1:T(8,128)(2,1)S(1)} collective-permute-done((s16[32,17,128]{2,0,1:T(8,128)(2,1)S(1)}, s16[32,17,128]{2,0,1:T(8,128)(2,1)S(1)}, u32[]{:S(2)}, u32[]{:S(2)}) %collective-permute-start.6) | collective-permute-done | bytes 139296 | tf_op jit(solution)/shard_map/ppermute | solution.py:20
  44.7 1.9 %collective-permute-done.7 = s16[32,17,128]{2,0,1:T(8,128)(2,1)S(1)} collective-permute-done((s16[32,17,128]{2,0,1:T(8,128)(2,1)S(1)}, s16[32,17,128]{2,0,1:T(8,128)(2,1)S(1)}, u32[]{:S(2)}, u32[]{:S(2)}) %collective-permute-start.7) | collective-permute-done | bytes 139296 | tf_op jit(solution)/shard_map/ppermute | solution.py:19
  48.2 2.8 %fusion.25 = f32[32,32,128]{2,1,0:T(8,128)S(1)} fusion(f32[32,6,4]{0,1,2:T(8,128)S(1)} %convolution_bitcast_fusion.4, f32[32,6,4]{1,0,2:T(8,128)S(1)} %copy.52, f32[6,4,4,128,1]{3,2,1,0,4:T(4,128)S(1)} %convolution_bitcast_fusion.3), kind=kOutput, calls=%fused_computation.26 | convolution fusion | flops 151093248 | bytes 579584 | tf_op jit(solution)/shard_map/xym,mz->xyz/dot_general | solution.py:96
  50.9 2.7 %collective-permute-done.8 = s16[32,33,128]{2,0,1:T(8,128)(2,1)S(1)} collective-permute-done((s16[32,33,128]{2,0,1:T(8,128)(2,1)S(1)}, s16[32,33,128]{2,0,1:T(8,128)(2,1)S(1)}, u32[]{:S(2)}, u32[]{:S(2)}) %collective-permute-start.8) | collective-permute-done | bytes 270368 | tf_op jit(solution)/shard_map/ppermute | solution.py:155
  54.4 2.4 %collective-permute-start.10 = (bf16[32,16,128]{2,0,1:T(8,128)(2,1)S(1)}, bf16[32,16,128]{2,0,1:T(8,128)(2,1)S(1)}, u32[]{:S(2)}, u32[]{:S(2)}) collective-permute-start(bf16[32,16,128]{2,0,1:T(8,128)(2,1)S(1)} %get-tuple-element.53), channel_id=1, source_target_pairs={{1,2},{2,1},{5,6},{6,5},{9,10},{10,9},{13,14},{14,13},{17,18},{18,... | collective-permute-start | bytes 393224 | tf_op jit(solution)/shard_map/ppermute | solution.py:20
  56.8 4.4 %collective-permute-done.10 = bf16[32,16,128]{2,0,1:T(8,128)(2,1)S(1)} collective-permute-done((bf16[32,16,128]{2,0,1:T(8,128)(2,1)S(1)}, bf16[32,16,128]{2,0,1:T(8,128)(2,1)S(1)}, u32[]{:S(2)}, u32[]{:S(2)}) %collective-permute-start.10) | collective-permute-done | bytes 131104 | tf_op jit(solution)/shard_map/ppermute | solution.py:20
  61.9 1.9 %collective-permute-start.12 = (bf16[16,64,128]{2,0,1:T(8,128)(2,1)S(1)}, bf16[16,64,128]{2,0,1:T(8,128)(2,1)S(1)}, u32[]{:S(2)}, u32[]{:S(2)}) collective-permute-start(bf16[16,64,128]{2,0,1:T(8,128)(2,1)S(1)} %get-tuple-element.37), channel_id=1, source_target_pairs={{4,8},{8,4},{5,9},{9,5},{6,10},{10,6},{7,11},{11,7},{20,24},{24,20... | collective-permute-start | bytes 786440 | tf_op jit(solution)/shard_map/ppermute | solution.py:20
  63.9 5.7 %collective-permute-done.12 = bf16[16,64,128]{2,0,1:T(8,128)(2,1)S(1)} collective-permute-done((bf16[16,64,128]{2,0,1:T(8,128)(2,1)S(1)}, bf16[16,64,128]{2,0,1:T(8,128)(2,1)S(1)}, u32[]{:S(2)}, u32[]{:S(2)}) %collective-permute-start.12) | collective-permute-done | bytes 262176 | tf_op jit(solution)/shard_map/ppermute | solution.py:20
  70.7 2.7 %fusion.2 = f32[3,32,128,32]{2,3,1,0:T(8,128)S(1)} fusion(f32[3,32,64,128]{3,1,2,0:T(8,128)S(1)} %fusion.36, f32[3,32,64,1]{2,0,1,3:T(4,128)S(1)} %convolution_bitcast_fusion.2), kind=kOutput, calls=%fused_computation.2 | convolution fusion | flops 150994944 | bytes 4743168 | tf_op jit(solution)/shard_map/goy,gxyz->gxoz/dot_general | solution.py:142
  76.6 2.8 %fusion.15 = f32[64,64,128]{2,0,1:T(8,128)S(1)} fusion(f32[3,32,64,128]{3,2,1,0:T(8,128)S(1)} %convolution_bitcast_fusion, f32[3,32,64]{2,0,1:T(4,128)S(1)} %fusion.51), kind=kOutput, calls=%fused_computation.18 | convolution fusion | flops 301989888 | bytes 5267456 | tf_op jit(solution)/shard_map/gox,goyz->xyz/dot_general | solution.py:147
  79.8 1.9 %collective-permute-start.14 = (s16[16,65,128]{2,0,1:T(8,128)(2,1)S(1)}, s16[16,65,128]{2,0,1:T(8,128)(2,1)S(1)}, u32[]{:S(2)}, u32[]{:S(2)}) collective-permute-start(s16[16,65,128]{2,0,1:T(8,128)(2,1)S(1)} %get-tuple-element.29), channel_id=1, source_target_pairs={{4,8},{8,4},{5,9},{9,5},{6,10},{10,6},{7,11},{11,7},{20,24},{24,20... | collective-permute-start | bytes 798728 | tf_op jit(solution)/shard_map/ppermute | solution.py:20
  81.8 5.7 %collective-permute-done.14 = s16[16,65,128]{2,0,1:T(8,128)(2,1)S(1)} collective-permute-done((s16[16,65,128]{2,0,1:T(8,128)(2,1)S(1)}, s16[16,65,128]{2,0,1:T(8,128)(2,1)S(1)}, u32[]{:S(2)}, u32[]{:S(2)}) %collective-permute-start.14) | collective-permute-done | bytes 266272 | tf_op jit(solution)/shard_map/ppermute | solution.py:20
  88.4 3.5 %collective-permute-start.16 = (s16[32,17,128]{2,0,1:T(8,128)(2,1)S(1)}, s16[32,17,128]{2,0,1:T(8,128)(2,1)S(1)}, u32[]{:S(2)}, u32[]{:S(2)}) collective-permute-start(s16[32,17,128]{2,0,1:T(8,128)(2,1)S(1)} %get-tuple-element.45), channel_id=1, source_target_pairs={{1,2},{2,1},{5,6},{6,5},{9,10},{10,9},{13,14},{14,13},{17,18},{18,... | collective-permute-start | bytes 417800 | tf_op jit(solution)/shard_map/ppermute | solution.py:20
  91.9 3.4 %collective-permute-done.16 = s16[32,17,128]{2,0,1:T(8,128)(2,1)S(1)} collective-permute-done((s16[32,17,128]{2,0,1:T(8,128)(2,1)S(1)}, s16[32,17,128]{2,0,1:T(8,128)(2,1)S(1)}, u32[]{:S(2)}, u32[]{:S(2)}) %collective-permute-start.16) | collective-permute-done | bytes 139296 | tf_op jit(solution)/shard_map/ppermute | solution.py:20
  95.3 1.7 %collective-permute-done.17 = s16[32,17,128]{2,0,1:T(8,128)(2,1)S(1)} collective-permute-done((s16[32,17,128]{2,0,1:T(8,128)(2,1)S(1)}, s16[32,17,128]{2,0,1:T(8,128)(2,1)S(1)}, u32[]{:S(2)}, u32[]{:S(2)}) %collective-permute-start.17) | collective-permute-done | bytes 139296 | tf_op jit(solution)/shard_map/ppermute | solution.py:19
  98.0 5.9 %collective-permute-done.18 = s16[32,33,128]{2,0,1:T(8,128)(2,1)S(1)} collective-permute-done((s16[32,33,128]{2,0,1:T(8,128)(2,1)S(1)}, s16[32,33,128]{2,0,1:T(8,128)(2,1)S(1)}, u32[]{:S(2)}, u32[]{:S(2)}) %collective-permute-start.18) | collective-permute-done | bytes 270368 | tf_op jit(solution)/shard_map/ppermute | solution.py:155
  (137 shorter events, 27.4 us)
Async XLA Ops:
  0.0 9.0 %copy-start.1 = (s32[3,4,4]{2,1,0:T(4,128)S(1)}, s32[3,4,4]{2,1,0:T(4,128)}, u32[]{:S(2)}) copy-start(s32[3,4,4]{2,1,0:T(4,128)} %param.9) | copy-start | bytes 580
  0.0 8.9 %copy-start.2 = (s32[3,4,4]{2,1,0:T(4,128)S(1)}, s32[3,4,4]{2,1,0:T(4,128)}, u32[]{:S(2)}) copy-start(s32[3,4,4]{2,1,0:T(4,128)} %param.8) | copy-start | bytes 580
  1.4 7.1 %collective-permute-start = (bf16[32,16,128]{2,0,1:T(8,128)(2,1)S(1)}, bf16[32,16,128]{2,0,1:T(8,128)(2,1)S(1)}, u32[]{:S(2)}, u32[]{:S(2)}) collective-permute-start(bf16[32,16,128]{2,0,1:T(8,128)(2,1)S(1)} %get-tuple-element.57), channel_id=1, source_target_pairs={{1,2},{2,1},{5,6},{6,5},{9,10},{10,9},{13,14},{14,13},{17,18},{18,... | collective-permute-start | bytes 393224 | tf_op jit(solution)/shard_map/ppermute | solution.py:20
  3.8 5.0 %collective-permute-start.1 = (bf16[32,16,128]{2,0,1:T(8,128)(2,1)S(1)}, bf16[32,16,128]{2,0,1:T(8,128)(2,1)S(1)}, u32[]{:S(2)}, u32[]{:S(2)}) collective-permute-start(bf16[32,16,128]{2,0,1:T(8,128)(2,1)S(1)} %get-tuple-element.58), channel_id=1, source_target_pairs={{0,1},{1,0},{2,3},{3,2},{4,5},{5,4},{6,7},{7,6},{8,9},{9,8},{10,11... | collective-permute-start | bytes 393224 | tf_op jit(solution)/shard_map/ppermute | solution.py:19
  9.2 4.1 %collective-permute-start.9 = (f32[375]{0:T(512)S(1)}, f32[375]{0:T(512)S(1)}, u32[]{:S(2)}, u32[]{:S(2)}) collective-permute-start(f32[375]{0:T(512)S(1)} %pad_maximum_fusion.2), channel_id=1, source_target_pairs={{0,16},{16,0},{1,17},{17,1},{2,18},{18,2},{3,19},{19,3},{4,20},{20... | collective-permute-start | bytes 4508 | tf_op jit(solution)/shard_map/ppermute | solution.py:118
  11.1 7.7 %collective-permute-start.2 = (bf16[16,64,128]{2,0,1:T(8,128)(2,1)S(1)}, bf16[16,64,128]{2,0,1:T(8,128)(2,1)S(1)}, u32[]{:S(2)}, u32[]{:S(2)}) collective-permute-start(bf16[16,64,128]{2,0,1:T(8,128)(2,1)S(1)} %get-tuple-element.41), channel_id=1, source_target_pairs={{4,8},{8,4},{5,9},{9,5},{6,10},{10,6},{7,11},{11,7},{20,24},{24,20... | collective-permute-start | bytes 786440 | tf_op jit(solution)/shard_map/ppermute | solution.py:20
  13.2 5.6 %collective-permute-start.3 = (bf16[16,64,128]{2,0,1:T(8,128)(2,1)S(1)}, bf16[16,64,128]{2,0,1:T(8,128)(2,1)S(1)}, u32[]{:S(2)}, u32[]{:S(2)}) collective-permute-start(bf16[16,64,128]{2,0,1:T(8,128)(2,1)S(1)} %get-tuple-element.42), channel_id=1, source_target_pairs={{0,4},{4,0},{8,12},{12,8},{1,5},{5,1},{9,13},{13,9},{2,6},{6,2},{1... | collective-permute-start | bytes 786440 | tf_op jit(solution)/shard_map/ppermute | solution.py:19
  22.6 1.1 %copy-start.3 = (bf16[3,32,32,128]{3,2,1,0:T(8,128)(2,1)S(1)}, bf16[3,32,32,128]{3,2,1,0:T(8,128)(2,1)}, u32[]{:S(2)}) copy-start(bf16[3,32,32,128]{3,2,1,0:T(8,128)(2,1)} %param.6) | copy-start | bytes 2359300
  29.3 7.7 %collective-permute-start.4 = (s16[16,65,128]{2,0,1:T(8,128)(2,1)S(1)}, s16[16,65,128]{2,0,1:T(8,128)(2,1)S(1)}, u32[]{:S(2)}, u32[]{:S(2)}) collective-permute-start(s16[16,65,128]{2,0,1:T(8,128)(2,1)S(1)} %get-tuple-element.33), channel_id=1, source_target_pairs={{4,8},{8,4},{5,9},{9,5},{6,10},{10,6},{7,11},{11,7},{20,24},{24,20... | collective-permute-start | bytes 798728 | tf_op jit(solution)/shard_map/ppermute | solution.py:20
  31.2 5.8 %collective-permute-start.5 = (s16[16,65,128]{2,0,1:T(8,128)(2,1)S(1)}, s16[16,65,128]{2,0,1:T(8,128)(2,1)S(1)}, u32[]{:S(2)}, u32[]{:S(2)}) collective-permute-start(s16[16,65,128]{2,0,1:T(8,128)(2,1)S(1)} %get-tuple-element.34), channel_id=1, source_target_pairs={{0,4},{4,0},{8,12},{12,8},{1,5},{5,1},{9,13},{13,9},{2,6},{6,2},{1... | collective-permute-start | bytes 798728 | tf_op jit(solution)/shard_map/ppermute | solution.py:19
  37.8 6.9 %collective-permute-start.6 = (s16[32,17,128]{2,0,1:T(8,128)(2,1)S(1)}, s16[32,17,128]{2,0,1:T(8,128)(2,1)S(1)}, u32[]{:S(2)}, u32[]{:S(2)}) collective-permute-start(s16[32,17,128]{2,0,1:T(8,128)(2,1)S(1)} %get-tuple-element.49), channel_id=1, source_target_pairs={{1,2},{2,1},{5,6},{6,5},{9,10},{10,9},{13,14},{14,13},{17,18},{18,... | collective-permute-start | bytes 417800 | tf_op jit(solution)/shard_map/ppermute | solution.py:20
  41.5 5.1 %collective-permute-start.7 = (s16[32,17,128]{2,0,1:T(8,128)(2,1)S(1)}, s16[32,17,128]{2,0,1:T(8,128)(2,1)S(1)}, u32[]{:S(2)}, u32[]{:S(2)}) collective-permute-start(s16[32,17,128]{2,0,1:T(8,128)(2,1)S(1)} %get-tuple-element.50), channel_id=1, source_target_pairs={{0,1},{1,0},{2,3},{3,2},{4,5},{5,4},{6,7},{7,6},{8,9},{9,8},{10,11... | collective-permute-start | bytes 417800 | tf_op jit(solution)/shard_map/ppermute | solution.py:19
  47.1 6.5 %collective-permute-start.8 = (s16[32,33,128]{2,0,1:T(8,128)(2,1)S(1)}, s16[32,33,128]{2,0,1:T(8,128)(2,1)S(1)}, u32[]{:S(2)}, u32[]{:S(2)}) collective-permute-start(s16[32,33,128]{2,0,1:T(8,128)(2,1)S(1)} %pad_add_fusion), channel_id=1, source_target_pairs={{0,16},{16,0},{1,17},{17,1},{2,18},{18,2},{3,19},{19,3},{4,20},{20... | collective-permute-start | bytes 811016 | tf_op jit(solution)/shard_map/ppermute | solution.py:155
  48.1 5.6 %copy-start = (f32[32,32,128]{2,1,0:T(8,128)S(1)}, f32[32,32,128]{2,1,0:T(8,128)}, u32[]{:S(2)}) copy-start(f32[32,32,128]{2,1,0:T(8,128)} %param.5) | copy-start | bytes 1572868
  54.4 6.9 %collective-permute-start.10 = (bf16[32,16,128]{2,0,1:T(8,128)(2,1)S(1)}, bf16[32,16,128]{2,0,1:T(8,128)(2,1)S(1)}, u32[]{:S(2)}, u32[]{:S(2)}) collective-permute-start(bf16[32,16,128]{2,0,1:T(8,128)(2,1)S(1)} %get-tuple-element.53), channel_id=1, source_target_pairs={{1,2},{2,1},{5,6},{6,5},{9,10},{10,9},{13,14},{14,13},{17,18},{18,... | collective-permute-start | bytes 393224 | tf_op jit(solution)/shard_map/ppermute | solution.py:20
  56.8 5.0 %collective-permute-start.11 = (bf16[32,16,128]{2,0,1:T(8,128)(2,1)S(1)}, bf16[32,16,128]{2,0,1:T(8,128)(2,1)S(1)}, u32[]{:S(2)}, u32[]{:S(2)}) collective-permute-start(bf16[32,16,128]{2,0,1:T(8,128)(2,1)S(1)} %get-tuple-element.54), channel_id=1, source_target_pairs={{0,1},{1,0},{2,3},{3,2},{4,5},{5,4},{6,7},{7,6},{8,9},{9,8},{10,11... | collective-permute-start | bytes 393224 | tf_op jit(solution)/shard_map/ppermute | solution.py:19
  61.9 7.7 %collective-permute-start.12 = (bf16[16,64,128]{2,0,1:T(8,128)(2,1)S(1)}, bf16[16,64,128]{2,0,1:T(8,128)(2,1)S(1)}, u32[]{:S(2)}, u32[]{:S(2)}) collective-permute-start(bf16[16,64,128]{2,0,1:T(8,128)(2,1)S(1)} %get-tuple-element.37), channel_id=1, source_target_pairs={{4,8},{8,4},{5,9},{9,5},{6,10},{10,6},{7,11},{11,7},{20,24},{24,20... | collective-permute-start | bytes 786440 | tf_op jit(solution)/shard_map/ppermute | solution.py:20
  63.9 5.8 %collective-permute-start.13 = (bf16[16,64,128]{2,0,1:T(8,128)(2,1)S(1)}, bf16[16,64,128]{2,0,1:T(8,128)(2,1)S(1)}, u32[]{:S(2)}, u32[]{:S(2)}) collective-permute-start(bf16[16,64,128]{2,0,1:T(8,128)(2,1)S(1)} %get-tuple-element.38), channel_id=1, source_target_pairs={{0,4},{4,0},{8,12},{12,8},{1,5},{5,1},{9,13},{13,9},{2,6},{6,2},{1... | collective-permute-start | bytes 786440 | tf_op jit(solution)/shard_map/ppermute | solution.py:19
  79.8 7.7 %collective-permute-start.14 = (s16[16,65,128]{2,0,1:T(8,128)(2,1)S(1)}, s16[16,65,128]{2,0,1:T(8,128)(2,1)S(1)}, u32[]{:S(2)}, u32[]{:S(2)}) collective-permute-start(s16[16,65,128]{2,0,1:T(8,128)(2,1)S(1)} %get-tuple-element.29), channel_id=1, source_target_pairs={{4,8},{8,4},{5,9},{9,5},{6,10},{10,6},{7,11},{11,7},{20,24},{24,20... | collective-permute-start | bytes 798728 | tf_op jit(solution)/shard_map/ppermute | solution.py:20
  81.8 5.8 %collective-permute-start.15 = (s16[16,65,128]{2,0,1:T(8,128)(2,1)S(1)}, s16[16,65,128]{2,0,1:T(8,128)(2,1)S(1)}, u32[]{:S(2)}, u32[]{:S(2)}) collective-permute-start(s16[16,65,128]{2,0,1:T(8,128)(2,1)S(1)} %get-tuple-element.30), channel_id=1, source_target_pairs={{0,4},{4,0},{8,12},{12,8},{1,5},{5,1},{9,13},{13,9},{2,6},{6,2},{1... | collective-permute-start | bytes 798728 | tf_op jit(solution)/shard_map/ppermute | solution.py:19
  88.4 6.9 %collective-permute-start.16 = (s16[32,17,128]{2,0,1:T(8,128)(2,1)S(1)}, s16[32,17,128]{2,0,1:T(8,128)(2,1)S(1)}, u32[]{:S(2)}, u32[]{:S(2)}) collective-permute-start(s16[32,17,128]{2,0,1:T(8,128)(2,1)S(1)} %get-tuple-element.45), channel_id=1, source_target_pairs={{1,2},{2,1},{5,6},{6,5},{9,10},{10,9},{13,14},{14,13},{17,18},{18,... | collective-permute-start | bytes 417800 | tf_op jit(solution)/shard_map/ppermute | solution.py:20
  91.9 5.1 %collective-permute-start.17 = (s16[32,17,128]{2,0,1:T(8,128)(2,1)S(1)}, s16[32,17,128]{2,0,1:T(8,128)(2,1)S(1)}, u32[]{:S(2)}, u32[]{:S(2)}) collective-permute-start(s16[32,17,128]{2,0,1:T(8,128)(2,1)S(1)} %get-tuple-element.46), channel_id=1, source_target_pairs={{0,1},{1,0},{2,3},{3,2},{4,5},{5,4},{6,7},{7,6},{8,9},{9,8},{10,11... | collective-permute-start | bytes 417800 | tf_op jit(solution)/shard_map/ppermute | solution.py:19
  97.4 6.5 %collective-permute-start.18 = (s16[32,33,128]{2,0,1:T(8,128)(2,1)S(1)}, s16[32,33,128]{2,0,1:T(8,128)(2,1)S(1)}, u32[]{:S(2)}, u32[]{:S(2)}) collective-permute-start(s16[32,33,128]{2,0,1:T(8,128)(2,1)S(1)} %pad_add_fusion.1), channel_id=1, source_target_pairs={{0,16},{16,0},{1,17},{17,1},{2,18},{18,2},{3,19},{19,3},{4,20},{20... | collective-permute-start | bytes 811016 | tf_op jit(solution)/shard_map/ppermute | solution.py:155

commit v6 on v5

--- a/solution.py
+++ b/solution.py
@@ -1,12 +1,19 @@
+import functools
+
 import jax
 import jax.numpy as jnp
 from jax import lax
+from jax.experimental import pallas as pl
+from jax.experimental.pallas import tpu as pltpu
 from jax.sharding import PartitionSpec as P
 
 ITERS = 2
-
-
-def swap_edges(to_below, to_above, axis):
+LANES = 128
+OUTER_FIRST, OUTER_LAST = (1, 0), (0, 1)
+VMEM = pl.BlockSpec(memory_space=pltpu.VMEM)
+
+
+def swap_edges(to_below, to_above, axis, order):
     peers = lax.axis_size(axis)
     even = lax.axis_index(axis) % 2 == 0
 
@@ -16,17 +23,23 @@
             out += [(i, i + 1), (i + 1, i)]
         return out
 
-    first = lax.ppermute(jnp.where(even, to_above, to_below), axis, pairs(0))
-    second = lax.ppermute(jnp.where(even, to_below, to_above), axis, pairs(1))
+    parts = [jnp.where(even, to_above, to_below), jnp.where(even, to_below, to_above)]
+    for turn in order:
+        parts[turn] = lax.ppermute(parts[turn], axis, pairs(turn))
+    first, second = parts
+    if order == OUTER_FIRST:
+        odd = jnp.logical_not(even)
+        return jnp.where(odd, first, second), jnp.where(odd, second, first)
     return jnp.where(even, second, first), jnp.where(even, first, second)
 
 
-def gather_halo(array, axis, dim, width):
+def gather_halo(array, axis, dim, width, order):
     length = array.shape[dim]
     before, after = swap_edges(
         lax.slice_in_dim(array, 0, width, axis=dim),
         lax.slice_in_dim(array, length - width, length, axis=dim),
         axis,
+        order,
     )
     return jnp.concatenate([before, array, after], axis=dim)
 
@@ -54,9 +67,27 @@
     return packed[:, :-1].astype(jnp.float32) * step
 
 
-def swap_fixed(to_below, to_above, axis):
-    below, above = swap_edges(pack_fixed(to_below), pack_fixed(to_above), axis)
+def swap_fixed(to_below, to_above, axis, order):
+    below, above = swap_edges(pack_fixed(to_below), pack_fixed(to_above), axis, order)
     return unpack_fixed(below), unpack_fixed(above)
+
+
+def table_kernel(taps, halo, psf, table_x, table_y, table_z):
+    radius = (taps - 1) // 2
+    depth = table_z.shape[1]
+    for k in range(psf.shape[0]):
+        rows = psf[k]
+        rows = rows / jnp.sum(rows, axis=1, keepdims=True)
+        for axis, table in ((0, table_x), (1, table_y)):
+            _, cells, wide = table.shape
+            base = jnp.broadcast_to(pltpu.roll(rows[axis : axis + 1], halo - radius, 1), (cells, LANES))
+            table[k] = pltpu.roll(base, 0, 1, stride=1, stride_axis=0)[:, :wide]
+        base = jnp.broadcast_to(pltpu.roll(rows[2:3], depth - radius, 1), (depth, depth))
+        turned = pltpu.roll(base, 0, 1, stride=1, stride_axis=0)
+        gap = lax.broadcasted_iota(jnp.int32, (depth, depth), 1) - lax.broadcasted_iota(
+            jnp.int32, (depth, depth), 0
+        )
+        table_z[k] = jnp.where((gap >= -radius) & (gap <= radius), turned, 0.0)
 
 
 def band(weights, rows, cols, shift):
@@ -107,11 +138,12 @@
     groups = lax.axis_size("view")
     swap = [(i, (i + 1) % groups) for i in range(groups)]
 
-    kern = psf / jnp.sum(psf, axis=-1, keepdims=True)
-    start = gather_halo(estimate.astype(jnp.bfloat16), "fy", 1, halo)
-    start, psf, cover_lo, cover_len = lax.optimization_barrier((start, psf, cover_lo, cover_len))
+    start = gather_halo(estimate.astype(jnp.bfloat16), "fy", 1, halo, OUTER_FIRST)
+    start = gather_halo(start, "fx", 0, halo, OUTER_LAST)
+    start, psf_late, lo_late, len_late = lax.optimization_barrier((start, psf, cover_lo, cover_len))
+    kern = psf_late / jnp.sum(psf_late, axis=-1, keepdims=True)
     pack = jnp.concatenate(
-        [kern.reshape(-1), cover_lo.reshape(-1).astype(jnp.float32), cover_len.reshape(-1).astype(jnp.float32)]
+        [kern.reshape(-1), lo_late.reshape(-1).astype(jnp.float32), len_late.reshape(-1).astype(jnp.float32)]
     )
     packs = [pack]
     for _ in range(groups - 1):
@@ -130,14 +162,26 @@
     own = (levels >= low) & (levels < low + span)
     masked = jnp.where(own, images, jnp.zeros_like(images)).astype(jnp.float32)
 
-    table_x = band(kern[:, 0], cells_x, cells_x + 2 * halo, radius - halo)
-    table_y = band(kern[:, 1], cells_y, cells_y + 2 * halo, radius - halo)
-    table_z = band(kern[:, 2], depth, depth, radius)
+    padded = jnp.pad(psf, ((0, 0), (0, 0), (0, LANES - taps)))
+    shape = functools.partial(jax.ShapeDtypeStruct, dtype=jnp.float32)
+    table_x, table_y, table_z = pl.pallas_call(
+        functools.partial(table_kernel, taps, halo),
+        out_shape=[
+            shape((group, cells_x, cells_x + 2 * halo)),
+            shape((group, cells_y, cells_y + 2 * halo)),
+            shape((group, depth, depth)),
+        ],
+        in_specs=[VMEM],
+        out_specs=[VMEM] * 3,
+    )(padded)
 
     joined = estimate
     for step in range(ITERS):
-        wide = start if step == 0 else gather_halo(joined.astype(jnp.bfloat16), "fy", 1, halo)
-        wide = gather_halo(wide, "fx", 0, halo).astype(jnp.float32)
+        wide = start
+        if step > 0:
+            wide = gather_halo(joined.astype(jnp.bfloat16), "fy", 1, halo, OUTER_FIRST)
+            wide = gather_halo(wide, "fx", 0, halo, OUTER_LAST)
+        wide = wide.astype(jnp.float32)
         field = jnp.einsum("gox,xyz->goyz", table_x, wide, precision=exact)
         field = jnp.einsum("goy,gxyz->gxoz", table_y, field, precision=exact)
         blurred = jnp.einsum("goz,gxyz->gxyo", table_z, field, precision=exact)
@@ -145,9 +189,9 @@
         field = jnp.einsum("goz,gxyo->gxyz", table_z, ratio, precision=exact)
         field = jnp.einsum("goy,gxoz->gxyz", table_y, field, precision=exact)
         field = jnp.einsum("gox,goyz->xyz", table_x, field, precision=exact)
-        below, above = swap_fixed(field[:halo], field[cells_x + halo :], "fx")
+        below, above = swap_fixed(field[:halo], field[cells_x + halo :], "fx", OUTER_LAST)
         field = add_edges(field[halo : cells_x + halo], below, above, 0)
-        below, above = swap_fixed(field[:, :halo], field[:, cells_y + halo :], "fy")
+        below, above = swap_fixed(field[:, :halo], field[:, cells_y + halo :], "fy", OUTER_FIRST)
         field = add_edges(field[:, halo : cells_y + halo], below, above, 1)
         moving = pack_fixed(field)
         correction = unpack_fixed(moving)

time: 107 us -> 106 us (level)
  waiting for transfers between devices: 46.3 us -> 44.3 us
  Pallas kernels: 0 us -> 1.66 us
  local copies, waits for them, and re-layouts: 3.71 us -> 5.32 us
  starting transfers between devices: 23 us -> 21.5 us
  matrix products: 25.2 us -> 24 us
    ppermute x16, waiting for transfers between devices: 37.7 us -> 35.7 us  [swap_edges(): parts[turn] = lax.ppermute(parts[turn], axis, pairs(turn))]
    pallas_call x0 -> x1, Pallas kernels: none -> 1.66 us  [body(): pl.pallas_call(functools.partial(table_kernel, taps, halo), out_shape=[sh...]
    ppermute x16, starting transfers between devices: 20.3 us -> 18.8 us  [swap_edges(): parts[turn] = lax.ppermute(parts[turn], axis, pairs(turn))]
  transfers between devices with their start and end apart: 19 -> 19, of which waited for: 14 -> 14; matrix products, arithmetic and copies ran while one was open for 8% -> 17% of each run, Pallas kernels for 0% -> 2%
where the time goes in v6:
time: 106 us; the launch traced here: 105 us
  waiting for transfers between devices  44.3 us (42%)
  matrix products  24 us (23%)
  starting transfers between devices  21.5 us (20%)
  other arithmetic  7.51 us (7%)
  local copies, waits for them, and re-layouts  5.32 us (5%)
  Pallas kernels  1.66 us (2%)
    ppermute x16, waiting for transfers between devices, swap_edges(): parts[turn] = lax.ppermute(parts[turn], axis, pairs(turn))  35.7 us
    ppermute x16, starting transfers between devices, swap_edges(): parts[turn] = lax.ppermute(parts[turn], axis, pairs(turn))  18.8 us
    ppermute x2, waiting for transfers between devices, body(): moving = lax.ppermute(moving, 'view', swap)  8.58 us
    dot_general x2, matrix products, body(): field = jnp.einsum('gox,goyz->xyz', table_x, field, precision=exact)  5.56 us
    dot_general x2, matrix products, body(): field = jnp.einsum('goy,gxyz->gxoz', table_y, field, precision=exact)  5.48 us
    dot_general x2, matrix products, body(): field = jnp.einsum('goy,gxoz->gxyz', table_y, field, precision=exact)  2.88 us
    dot_general x1, matrix products, weight_of(): jnp.einsum('xym,mz->xyz', plane, sums_z.reshape(-1, depth), precision=lax...  2.77 us
  transfers between devices with their start and end apart: 19, of which 14 were waited for; matrix products, arithmetic and copies ran while one was open for 17% of the time, Pallas kernels for 2%

profile of v6, /device:TPU:20, one launch (start us, length us, event | category | flops | bytes accessed | tf_op | source)
XLA Modules:
  0.0 105.2 jit_solution(1228460084209345446)
XLA Ops:
  3.0 1.9 %collective-permute-start.1 = (bf16[32,16,128]{2,0,1:T(8,128)(2,1)S(1)}, bf16[32,16,128]{2,0,1:T(8,128)(2,1)S(1)}, u32[]{:S(2)}, u32[]{:S(2)}) collective-permute-start(bf16[32,16,128]{2,0,1:T(8,128)(2,1)S(1)} %get-tuple-element.66), channel_id=1, source_target_pairs={{1,2},{2,1},{5,6},{6,5},{9,10},{10,9},{13,14},{14,13},{17,18},{18,... | collective-permute-start | bytes 393224 | tf_op jit(solution)/shard_map/ppermute | solution.py:28
  6.7 3.2 %collective-permute-done.1 = bf16[32,16,128]{2,0,1:T(8,128)(2,1)S(1)} collective-permute-done((bf16[32,16,128]{2,0,1:T(8,128)(2,1)S(1)}, bf16[32,16,128]{2,0,1:T(8,128)(2,1)S(1)}, u32[]{:S(2)}, u32[]{:S(2)}) %collective-permute-start.1) | collective-permute-done | bytes 131104 | tf_op jit(solution)/shard_map/ppermute | solution.py:28
  10.1 1.9 %collective-permute-start.2 = (bf16[16,64,128]{2,0,1:T(8,128)(2,1)S(1)}, bf16[16,64,128]{2,0,1:T(8,128)(2,1)S(1)}, u32[]{:S(2)}, u32[]{:S(2)}) collective-permute-start(bf16[16,64,128]{2,0,1:T(8,128)(2,1)S(1)} %get-tuple-element.49), channel_id=1, source_target_pairs={{4,8},{8,4},{5,9},{9,5},{6,10},{10,6},{7,11},{11,7},{20,24},{24,20... | collective-permute-start | bytes 786440 | tf_op jit(solution)/shard_map/ppermute | solution.py:28
  14.7 3.1 %collective-permute-done.2 = bf16[16,64,128]{2,0,1:T(8,128)(2,1)S(1)} collective-permute-done((bf16[16,64,128]{2,0,1:T(8,128)(2,1)S(1)}, bf16[16,64,128]{2,0,1:T(8,128)(2,1)S(1)}, u32[]{:S(2)}, u32[]{:S(2)}) %collective-permute-start.2) | collective-permute-done | bytes 262176 | tf_op jit(solution)/shard_map/ppermute | solution.py:28
  20.9 2.7 %fusion.7 = f32[3,32,128,32]{2,3,1,0:T(8,128)S(1)} fusion(f32[3,32,64,128]{3,1,2,0:T(8,128)S(1)} %fusion.43, f32[3,32,64]{2,1,0:T(8,128)S(1)} %copy-done.1), kind=kOutput, calls=%fused_computation.7 | convolution fusion | flops 150994944 | bytes 4743168 | tf_op jit(solution)/shard_map/goy,gxyz->gxoz/dot_general | solution.py:186
  27.1 2.8 %fusion.13 = f32[64,64,128]{2,0,1:T(8,128)S(1)} fusion(f32[3,32,64,128]{3,2,1,0:T(8,128)S(1)} %convolution_bitcast_fusion.1, f32[3,32,64]{2,1,0:T(8,128)S(1)} %copy-done.3), kind=kOutput, calls=%fused_computation.18 | convolution fusion | flops 301989888 | bytes 5267456 | tf_op jit(solution)/shard_map/gox,goyz->xyz/dot_general | solution.py:191
  31.0 2.1 %collective-permute-start.4 = (s16[16,65,128]{2,0,1:T(8,128)(2,1)}, s16[16,65,128]{2,0,1:T(8,128)(2,1)S(1)}, u32[]{:S(2)}, u32[]{:S(2)}) collective-permute-start(s16[16,65,128]{2,0,1:T(8,128)(2,1)} %get-tuple-element.41), channel_id=1, source_target_pairs={{4,8},{8,4},{5,9},{9,5},{6,10},{10,6},{7,11},{11,7},{20,24},{24,20... | collective-permute-start | bytes 798728 | tf_op jit(solution)/shard_map/ppermute | solution.py:28
  34.2 4.7 %collective-permute-done.4 = s16[16,65,128]{2,0,1:T(8,128)(2,1)S(1)} collective-permute-done((s16[16,65,128]{2,0,1:T(8,128)(2,1)}, s16[16,65,128]{2,0,1:T(8,128)(2,1)S(1)}, u32[]{:S(2)}, u32[]{:S(2)}) %collective-permute-start.4) | collective-permute-done | bytes 266272 | tf_op jit(solution)/shard_map/ppermute | solution.py:28
  40.8 2.2 %collective-permute-start.7 = (s16[32,17,128]{2,0,1:T(8,128)(2,1)S(1)}, s16[32,17,128]{2,0,1:T(8,128)(2,1)S(1)}, u32[]{:S(2)}, u32[]{:S(2)}) collective-permute-start(s16[32,17,128]{2,0,1:T(8,128)(2,1)S(1)} %get-tuple-element.58), channel_id=1, source_target_pairs={{1,2},{2,1},{5,6},{6,5},{9,10},{10,9},{13,14},{14,13},{17,18},{18,... | collective-permute-start | bytes 417800 | tf_op jit(solution)/shard_map/ppermute | solution.py:28
  45.8 1.9 %collective-permute-done.7 = s16[32,17,128]{2,0,1:T(8,128)(2,1)S(1)} collective-permute-done((s16[32,17,128]{2,0,1:T(8,128)(2,1)S(1)}, s16[32,17,128]{2,0,1:T(8,128)(2,1)S(1)}, u32[]{:S(2)}, u32[]{:S(2)}) %collective-permute-start.7) | collective-permute-done | bytes 139296 | tf_op jit(solution)/shard_map/ppermute | solution.py:28
  49.3 2.8 %fusion.25 = f32[32,32,128]{2,1,0:T(8,128)S(1)} fusion(f32[32,6,4]{0,1,2:T(8,128)S(1)} %convolution_bitcast_fusion.3, f32[32,6,4]{1,0,2:T(8,128)S(1)} %copy.31, f32[6,4,4,128,1]{3,2,1,0,4:T(4,128)S(1)} %convolution_bitcast_fusion.2), kind=kOutput, calls=%fused_computation.26 | convolution fusion | flops 151093248 | bytes 579584 | tf_op jit(solution)/shard_map/xym,mz->xyz/dot_general | solution.py:127
  52.0 2.7 %collective-permute-done.8 = s16[32,33,128]{2,0,1:T(8,128)(2,1)S(1)} collective-permute-done((s16[32,33,128]{2,0,1:T(8,128)(2,1)S(1)}, s16[32,33,128]{2,0,1:T(8,128)(2,1)S(1)}, u32[]{:S(2)}, u32[]{:S(2)}) %collective-permute-start.8) | collective-permute-done | bytes 270368 | tf_op jit(solution)/shard_map/ppermute | solution.py:199
  55.6 2.2 %collective-permute-start.11 = (bf16[32,16,128]{2,0,1:T(8,128)(2,1)S(1)}, bf16[32,16,128]{2,0,1:T(8,128)(2,1)S(1)}, u32[]{:S(2)}, u32[]{:S(2)}) collective-permute-start(bf16[32,16,128]{2,0,1:T(8,128)(2,1)S(1)} %get-tuple-element.62), channel_id=1, source_target_pairs={{1,2},{2,1},{5,6},{6,5},{9,10},{10,9},{13,14},{14,13},{17,18},{18,... | collective-permute-start | bytes 393224 | tf_op jit(solution)/shard_map/ppermute | solution.py:28
  57.7 2.8 %collective-permute-done.10 = bf16[32,16,128]{2,0,1:T(8,128)(2,1)S(1)} collective-permute-done((bf16[32,16,128]{2,0,1:T(8,128)(2,1)S(1)}, bf16[32,16,128]{2,0,1:T(8,128)(2,1)S(1)}, u32[]{:S(2)}, u32[]{:S(2)}) %collective-permute-start.10) | collective-permute-done | bytes 131104 | tf_op jit(solution)/shard_map/ppermute | solution.py:28
  60.5 1.9 %collective-permute-done.11 = bf16[32,16,128]{2,0,1:T(8,128)(2,1)S(1)} collective-permute-done((bf16[32,16,128]{2,0,1:T(8,128)(2,1)S(1)}, bf16[32,16,128]{2,0,1:T(8,128)(2,1)S(1)}, u32[]{:S(2)}, u32[]{:S(2)}) %collective-permute-start.11) | collective-permute-done | bytes 131104 | tf_op jit(solution)/shard_map/ppermute | solution.py:28
  62.6 2.2 %collective-permute-start.12 = (bf16[16,64,128]{2,0,1:T(8,128)(2,1)S(1)}, bf16[16,64,128]{2,0,1:T(8,128)(2,1)S(1)}, u32[]{:S(2)}, u32[]{:S(2)}) collective-permute-start(bf16[16,64,128]{2,0,1:T(8,128)(2,1)S(1)} %get-tuple-element.45), channel_id=1, source_target_pairs={{4,8},{8,4},{5,9},{9,5},{6,10},{10,6},{7,11},{11,7},{20,24},{24,20... | collective-permute-start | bytes 786440 | tf_op jit(solution)/shard_map/ppermute | solution.py:28
  64.8 5.4 %collective-permute-done.12 = bf16[16,64,128]{2,0,1:T(8,128)(2,1)S(1)} collective-permute-done((bf16[16,64,128]{2,0,1:T(8,128)(2,1)S(1)}, bf16[16,64,128]{2,0,1:T(8,128)(2,1)S(1)}, u32[]{:S(2)}, u32[]{:S(2)}) %collective-permute-start.12) | collective-permute-done | bytes 262176 | tf_op jit(solution)/shard_map/ppermute | solution.py:28
  71.3 2.7 %fusion.3 = f32[3,32,128,32]{2,3,1,0:T(8,128)S(1)} fusion(f32[3,32,64,128]{3,1,2,0:T(8,128)S(1)} %fusion.34, f32[3,32,64]{2,1,0:T(8,128)S(1)} %copy-done.1), kind=kOutput, calls=%fused_computation.3 | convolution fusion | flops 150994944 | bytes 4743168 | tf_op jit(solution)/shard_map/goy,gxyz->gxoz/dot_general | solution.py:186
  77.5 2.8 %fusion.16 = f32[64,64,128]{2,0,1:T(8,128)S(1)} fusion(f32[3,32,64,128]{3,2,1,0:T(8,128)S(1)} %convolution_bitcast_fusion, f32[3,32,64]{2,1,0:T(8,128)S(1)} %copy-done.3), kind=kOutput, calls=%fused_computation.19 | convolution fusion | flops 301989888 | bytes 5267456 | tf_op jit(solution)/shard_map/gox,goyz->xyz/dot_general | solution.py:191
  80.7 2.0 %collective-permute-start.14 = (s16[16,65,128]{2,0,1:T(8,128)(2,1)S(1)}, s16[16,65,128]{2,0,1:T(8,128)(2,1)S(1)}, u32[]{:S(2)}, u32[]{:S(2)}) collective-permute-start(s16[16,65,128]{2,0,1:T(8,128)(2,1)S(1)} %get-tuple-element.37), channel_id=1, source_target_pairs={{4,8},{8,4},{5,9},{9,5},{6,10},{10,6},{7,11},{11,7},{20,24},{24,20... | collective-permute-start | bytes 798728 | tf_op jit(solution)/shard_map/ppermute | solution.py:28
  82.8 5.7 %collective-permute-done.14 = s16[16,65,128]{2,0,1:T(8,128)(2,1)S(1)} collective-permute-done((s16[16,65,128]{2,0,1:T(8,128)(2,1)S(1)}, s16[16,65,128]{2,0,1:T(8,128)(2,1)S(1)}, u32[]{:S(2)}, u32[]{:S(2)}) %collective-permute-start.14) | collective-permute-done | bytes 266272 | tf_op jit(solution)/shard_map/ppermute | solution.py:28
  89.3 2.2 %collective-permute-start.17 = (s16[32,17,128]{2,0,1:T(8,128)(2,1)S(1)}, s16[32,17,128]{2,0,1:T(8,128)(2,1)S(1)}, u32[]{:S(2)}, u32[]{:S(2)}) collective-permute-start(s16[32,17,128]{2,0,1:T(8,128)(2,1)S(1)} %get-tuple-element.54), channel_id=1, source_target_pairs={{1,2},{2,1},{5,6},{6,5},{9,10},{10,9},{13,14},{14,13},{17,18},{18,... | collective-permute-start | bytes 417800 | tf_op jit(solution)/shard_map/ppermute | solution.py:28
  91.5 2.8 %collective-permute-done.16 = s16[32,17,128]{2,0,1:T(8,128)(2,1)S(1)} collective-permute-done((s16[32,17,128]{2,0,1:T(8,128)(2,1)S(1)}, s16[32,17,128]{2,0,1:T(8,128)(2,1)S(1)}, u32[]{:S(2)}, u32[]{:S(2)}) %collective-permute-start.16) | collective-permute-done | bytes 139296 | tf_op jit(solution)/shard_map/ppermute | solution.py:28
  97.3 5.9 %collective-permute-done.18 = s16[32,33,128]{2,0,1:T(8,128)(2,1)S(1)} collective-permute-done((s16[32,33,128]{2,0,1:T(8,128)(2,1)S(1)}, s16[32,33,128]{2,0,1:T(8,128)(2,1)S(1)}, u32[]{:S(2)}, u32[]{:S(2)}) %collective-permute-start.18) | collective-permute-done | bytes 270368 | tf_op jit(solution)/shard_map/ppermute | solution.py:199
  (145 shorter events, 33.8 us)
Async XLA Ops:
  0.0 12.1 %copy-start.6 = (f32[3,3,31]{2,1,0:T(4,128)S(1)}, f32[3,3,31]{2,1,0:T(4,128)}, u32[]{:S(2)}) copy-start(f32[3,3,31]{2,1,0:T(4,128)} %param.7) | copy-start | bytes 3352
  1.4 5.3 %collective-permute-start = (bf16[32,16,128]{2,0,1:T(8,128)(2,1)S(1)}, bf16[32,16,128]{2,0,1:T(8,128)(2,1)S(1)}, u32[]{:S(2)}, u32[]{:S(2)}) collective-permute-start(bf16[32,16,128]{2,0,1:T(8,128)(2,1)S(1)} %get-tuple-element.65), channel_id=1, source_target_pairs={{0,1},{1,0},{2,3},{3,2},{4,5},{5,4},{6,7},{7,6},{8,9},{9,8},{10,11... | collective-permute-start | bytes 393224 | tf_op jit(solution)/shard_map/ppermute | solution.py:28
  3.0 6.8 %collective-permute-start.1 = (bf16[32,16,128]{2,0,1:T(8,128)(2,1)S(1)}, bf16[32,16,128]{2,0,1:T(8,128)(2,1)S(1)}, u32[]{:S(2)}, u32[]{:S(2)}) collective-permute-start(bf16[32,16,128]{2,0,1:T(8,128)(2,1)S(1)} %get-tuple-element.66), channel_id=1, source_target_pairs={{1,2},{2,1},{5,6},{6,5},{9,10},{10,9},{13,14},{14,13},{17,18},{18,... | collective-permute-start | bytes 393224 | tf_op jit(solution)/shard_map/ppermute | solution.py:28
  10.0 8.1 %copy-start.4 = (s32[3,4,4]{2,1,0:T(4,128)S(1)}, s32[3,4,4]{2,1,0:T(4,128)}, u32[]{:S(2)}) copy-start(s32[3,4,4]{2,1,0:T(4,128)} %param.8) | copy-start | bytes 580
  10.0 8.2 %copy-start.5 = (s32[3,4,4]{2,1,0:T(4,128)S(1)}, s32[3,4,4]{2,1,0:T(4,128)}, u32[]{:S(2)}) copy-start(s32[3,4,4]{2,1,0:T(4,128)} %param.9) | copy-start | bytes 580
  10.1 7.7 %collective-permute-start.2 = (bf16[16,64,128]{2,0,1:T(8,128)(2,1)S(1)}, bf16[16,64,128]{2,0,1:T(8,128)(2,1)S(1)}, u32[]{:S(2)}, u32[]{:S(2)}) collective-permute-start(bf16[16,64,128]{2,0,1:T(8,128)(2,1)S(1)} %get-tuple-element.49), channel_id=1, source_target_pairs={{4,8},{8,4},{5,9},{9,5},{6,10},{10,6},{7,11},{11,7},{20,24},{24,20... | collective-permute-start | bytes 786440 | tf_op jit(solution)/shard_map/ppermute | solution.py:28
  12.0 5.8 %collective-permute-start.3 = (bf16[16,64,128]{2,0,1:T(8,128)(2,1)S(1)}, bf16[16,64,128]{2,0,1:T(8,128)(2,1)S(1)}, u32[]{:S(2)}, u32[]{:S(2)}) collective-permute-start(bf16[16,64,128]{2,0,1:T(8,128)(2,1)S(1)} %get-tuple-element.50), channel_id=1, source_target_pairs={{0,4},{4,0},{8,12},{12,8},{1,5},{5,1},{9,13},{13,9},{2,6},{6,2},{1... | collective-permute-start | bytes 786440 | tf_op jit(solution)/shard_map/ppermute | solution.py:28
  14.4 5.6 %copy-start.3 = (f32[3,32,64]{2,1,0:T(8,128)S(1)}, f32[3,32,64]{2,1,0:T(8,128)}, u32[]{:S(2)}) copy-start(f32[3,32,64]{2,1,0:T(8,128)} %get-tuple-element.12) | copy-start | bytes 73732
  18.4 14.8 %collective-permute-start.9 = (f32[375]{0:T(512)S(1)}, f32[375]{0:T(512)S(1)}, u32[]{:S(2)}, u32[]{:S(2)}) collective-permute-start(f32[375]{0:T(512)S(1)} %pad_maximum_fusion.3), channel_id=1, source_target_pairs={{0,16},{16,0},{1,17},{17,1},{2,18},{18,2},{3,19},{19,3},{4,20},{20... | collective-permute-start | bytes 4508 | tf_op jit(solution)/shard_map/ppermute | solution.py:150
  31.0 7.9 %collective-permute-start.4 = (s16[16,65,128]{2,0,1:T(8,128)(2,1)}, s16[16,65,128]{2,0,1:T(8,128)(2,1)S(1)}, u32[]{:S(2)}, u32[]{:S(2)}) collective-permute-start(s16[16,65,128]{2,0,1:T(8,128)(2,1)} %get-tuple-element.41), channel_id=1, source_target_pairs={{4,8},{8,4},{5,9},{9,5},{6,10},{10,6},{7,11},{11,7},{20,24},{24,20... | collective-permute-start | bytes 798728 | tf_op jit(solution)/shard_map/ppermute | solution.py:28
  33.1 5.8 %collective-permute-start.5 = (s16[16,65,128]{2,0,1:T(8,128)(2,1)S(1)}, s16[16,65,128]{2,0,1:T(8,128)(2,1)}, u32[]{:S(2)}, u32[]{:S(2)}) collective-permute-start(s16[16,65,128]{2,0,1:T(8,128)(2,1)S(1)} %get-tuple-element.42), channel_id=1, source_target_pairs={{0,4},{4,0},{8,12},{12,8},{1,5},{5,1},{9,13},{13,9},{2,6},{6,2},{1... | collective-permute-start | bytes 798728 | tf_op jit(solution)/shard_map/ppermute | solution.py:28
  40.7 5.1 %collective-permute-start.6 = (s16[32,17,128]{2,0,1:T(8,128)(2,1)S(1)}, s16[32,17,128]{2,0,1:T(8,128)(2,1)S(1)}, u32[]{:S(2)}, u32[]{:S(2)}) collective-permute-start(s16[32,17,128]{2,0,1:T(8,128)(2,1)S(1)} %get-tuple-element.57), channel_id=1, source_target_pairs={{0,1},{1,0},{2,3},{3,2},{4,5},{5,4},{6,7},{7,6},{8,9},{9,8},{10,11... | collective-permute-start | bytes 417800 | tf_op jit(solution)/shard_map/ppermute | solution.py:28
  40.8 6.9 %collective-permute-start.7 = (s16[32,17,128]{2,0,1:T(8,128)(2,1)S(1)}, s16[32,17,128]{2,0,1:T(8,128)(2,1)S(1)}, u32[]{:S(2)}, u32[]{:S(2)}) collective-permute-start(s16[32,17,128]{2,0,1:T(8,128)(2,1)S(1)} %get-tuple-element.58), channel_id=1, source_target_pairs={{1,2},{2,1},{5,6},{6,5},{9,10},{10,9},{13,14},{14,13},{17,18},{18,... | collective-permute-start | bytes 417800 | tf_op jit(solution)/shard_map/ppermute | solution.py:28
  48.2 6.5 %collective-permute-start.8 = (s16[32,33,128]{2,0,1:T(8,128)(2,1)S(1)}, s16[32,33,128]{2,0,1:T(8,128)(2,1)S(1)}, u32[]{:S(2)}, u32[]{:S(2)}) collective-permute-start(s16[32,33,128]{2,0,1:T(8,128)(2,1)S(1)} %pad_add_fusion), channel_id=1, source_target_pairs={{0,16},{16,0},{1,17},{17,1},{2,18},{18,2},{3,19},{19,3},{4,20},{20... | collective-permute-start | bytes 811016 | tf_op jit(solution)/shard_map/ppermute | solution.py:199
  49.2 5.6 %copy-start = (f32[32,32,128]{2,1,0:T(8,128)S(1)}, f32[32,32,128]{2,1,0:T(8,128)}, u32[]{:S(2)}) copy-start(f32[32,32,128]{2,1,0:T(8,128)} %param.5) | copy-start | bytes 1572868
  55.5 5.0 %collective-permute-start.10 = (bf16[32,16,128]{2,0,1:T(8,128)(2,1)S(1)}, bf16[32,16,128]{2,0,1:T(8,128)(2,1)S(1)}, u32[]{:S(2)}, u32[]{:S(2)}) collective-permute-start(bf16[32,16,128]{2,0,1:T(8,128)(2,1)S(1)} %get-tuple-element.61), channel_id=1, source_target_pairs={{0,1},{1,0},{2,3},{3,2},{4,5},{5,4},{6,7},{7,6},{8,9},{9,8},{10,11... | collective-permute-start | bytes 393224 | tf_op jit(solution)/shard_map/ppermute | solution.py:28
  55.6 6.9 %collective-permute-start.11 = (bf16[32,16,128]{2,0,1:T(8,128)(2,1)S(1)}, bf16[32,16,128]{2,0,1:T(8,128)(2,1)S(1)}, u32[]{:S(2)}, u32[]{:S(2)}) collective-permute-start(bf16[32,16,128]{2,0,1:T(8,128)(2,1)S(1)} %get-tuple-element.62), channel_id=1, source_target_pairs={{1,2},{2,1},{5,6},{6,5},{9,10},{10,9},{13,14},{14,13},{17,18},{18,... | collective-permute-start | bytes 393224 | tf_op jit(solution)/shard_map/ppermute | solution.py:28
  62.6 7.7 %collective-permute-start.12 = (bf16[16,64,128]{2,0,1:T(8,128)(2,1)S(1)}, bf16[16,64,128]{2,0,1:T(8,128)(2,1)S(1)}, u32[]{:S(2)}, u32[]{:S(2)}) collective-permute-start(bf16[16,64,128]{2,0,1:T(8,128)(2,1)S(1)} %get-tuple-element.45), channel_id=1, source_target_pairs={{4,8},{8,4},{5,9},{9,5},{6,10},{10,6},{7,11},{11,7},{20,24},{24,20... | collective-permute-start | bytes 786440 | tf_op jit(solution)/shard_map/ppermute | solution.py:28
  64.8 5.5 %collective-permute-start.13 = (bf16[16,64,128]{2,0,1:T(8,128)(2,1)S(1)}, bf16[16,64,128]{2,0,1:T(8,128)(2,1)S(1)}, u32[]{:S(2)}, u32[]{:S(2)}) collective-permute-start(bf16[16,64,128]{2,0,1:T(8,128)(2,1)S(1)} %get-tuple-element.46), channel_id=1, source_target_pairs={{0,4},{4,0},{8,12},{12,8},{1,5},{5,1},{9,13},{13,9},{2,6},{6,2},{1... | collective-permute-start | bytes 786440 | tf_op jit(solution)/shard_map/ppermute | solution.py:28
  80.7 7.7 %collective-permute-start.14 = (s16[16,65,128]{2,0,1:T(8,128)(2,1)S(1)}, s16[16,65,128]{2,0,1:T(8,128)(2,1)S(1)}, u32[]{:S(2)}, u32[]{:S(2)}) collective-permute-start(s16[16,65,128]{2,0,1:T(8,128)(2,1)S(1)} %get-tuple-element.37), channel_id=1, source_target_pairs={{4,8},{8,4},{5,9},{9,5},{6,10},{10,6},{7,11},{11,7},{20,24},{24,20... | collective-permute-start | bytes 798728 | tf_op jit(solution)/shard_map/ppermute | solution.py:28
  82.7 5.7 %collective-permute-start.15 = (s16[16,65,128]{2,0,1:T(8,128)(2,1)S(1)}, s16[16,65,128]{2,0,1:T(8,128)(2,1)S(1)}, u32[]{:S(2)}, u32[]{:S(2)}) collective-permute-start(s16[16,65,128]{2,0,1:T(8,128)(2,1)S(1)} %get-tuple-element.38), channel_id=1, source_target_pairs={{0,4},{4,0},{8,12},{12,8},{1,5},{5,1},{9,13},{13,9},{2,6},{6,2},{1... | collective-permute-start | bytes 798728 | tf_op jit(solution)/shard_map/ppermute | solution.py:28
  89.2 5.1 %collective-permute-start.16 = (s16[32,17,128]{2,0,1:T(8,128)(2,1)S(1)}, s16[32,17,128]{2,0,1:T(8,128)(2,1)S(1)}, u32[]{:S(2)}, u32[]{:S(2)}) collective-permute-start(s16[32,17,128]{2,0,1:T(8,128)(2,1)S(1)} %get-tuple-element.53), channel_id=1, source_target_pairs={{0,1},{1,0},{2,3},{3,2},{4,5},{5,4},{6,7},{7,6},{8,9},{9,8},{10,11... | collective-permute-start | bytes 417800 | tf_op jit(solution)/shard_map/ppermute | solution.py:28
  89.3 6.9 %collective-permute-start.17 = (s16[32,17,128]{2,0,1:T(8,128)(2,1)S(1)}, s16[32,17,128]{2,0,1:T(8,128)(2,1)S(1)}, u32[]{:S(2)}, u32[]{:S(2)}) collective-permute-start(s16[32,17,128]{2,0,1:T(8,128)(2,1)S(1)} %get-tuple-element.54), channel_id=1, source_target_pairs={{1,2},{2,1},{5,6},{6,5},{9,10},{10,9},{13,14},{14,13},{17,18},{18,... | collective-permute-start | bytes 417800 | tf_op jit(solution)/shard_map/ppermute | solution.py:28
  96.7 6.5 %collective-permute-start.18 = (s16[32,33,128]{2,0,1:T(8,128)(2,1)S(1)}, s16[32,33,128]{2,0,1:T(8,128)(2,1)S(1)}, u32[]{:S(2)}, u32[]{:S(2)}) collective-permute-start(s16[32,33,128]{2,0,1:T(8,128)(2,1)S(1)} %pad_add_fusion.1), channel_id=1, source_target_pairs={{0,16},{16,0},{1,17},{17,1},{2,18},{18,2},{3,19},{19,3},{4,20},{20... | collective-permute-start | bytes 811016 | tf_op jit(solution)/shard_map/ppermute | solution.py:199
  (4 other events, 6.0 us)

commit v7 on v6

--- a/solution.py
+++ b/solution.py
@@ -9,11 +9,10 @@
 
 ITERS = 2
 LANES = 128
-OUTER_FIRST, OUTER_LAST = (1, 0), (0, 1)
 VMEM = pl.BlockSpec(memory_space=pltpu.VMEM)
 
 
-def swap_edges(to_below, to_above, axis, order):
+def swap_edges(to_below, to_above, axis, late=()):
     peers = lax.axis_size(axis)
     even = lax.axis_index(axis) % 2 == 0
 
@@ -23,23 +22,20 @@
             out += [(i, i + 1), (i + 1, i)]
         return out
 
-    parts = [jnp.where(even, to_above, to_below), jnp.where(even, to_below, to_above)]
-    for turn in order:
-        parts[turn] = lax.ppermute(parts[turn], axis, pairs(turn))
-    first, second = parts
-    if order == OUTER_FIRST:
-        odd = jnp.logical_not(even)
-        return jnp.where(odd, first, second), jnp.where(odd, second, first)
-    return jnp.where(even, second, first), jnp.where(even, first, second)
-
-
-def gather_halo(array, axis, dim, width, order):
+    first = lax.ppermute(jnp.where(even, to_above, to_below), axis, pairs(0))
+    second = lax.ppermute(jnp.where(even, to_below, to_above), axis, pairs(1))
+    if late:
+        first, *late = lax.optimization_barrier((first, *late))
+    odd = jnp.logical_not(even)
+    return jnp.where(odd, first, second), jnp.where(odd, second, first), late
+
+
+def gather_halo(array, axis, dim, width):
     length = array.shape[dim]
-    before, after = swap_edges(
+    before, after, _ = swap_edges(
         lax.slice_in_dim(array, 0, width, axis=dim),
         lax.slice_in_dim(array, length - width, length, axis=dim),
         axis,
-        order,
     )
     return jnp.concatenate([before, array, after], axis=dim)
 
@@ -67,9 +63,9 @@
     return packed[:, :-1].astype(jnp.float32) * step
 
 
-def swap_fixed(to_below, to_above, axis, order):
-    below, above = swap_edges(pack_fixed(to_below), pack_fixed(to_above), axis, order)
-    return unpack_fixed(below), unpack_fixed(above)
+def swap_fixed(to_below, to_above, axis, late=()):
+    below, above, late = swap_edges(pack_fixed(to_below), pack_fixed(to_above), axis, late)
+    return unpack_fixed(below), unpack_fixed(above), late
 
 
 def table_kernel(taps, halo, psf, table_x, table_y, table_z):
@@ -129,6 +125,22 @@
     )
 
 
+def view_tables(psf, cover_lo, cover_len, swap):
+    kern = psf / jnp.sum(psf, axis=-1, keepdims=True)
+    pack = jnp.concatenate(
+        [kern.reshape(-1), cover_lo.reshape(-1).astype(jnp.float32), cover_len.reshape(-1).astype(jnp.float32)]
+    )
+    packs = [pack]
+    for _ in range(len(swap) - 1):
+        packs.append(lax.ppermute(packs[-1], "view", swap))
+    packs = jnp.stack(packs)
+    all_kern = packs[:, : kern.size].reshape((-1,) + kern.shape[1:])
+    cells = cover_lo.size
+    all_low = packs[:, kern.size : kern.size + cells].astype(jnp.int32).reshape((-1,) + cover_lo.shape[1:])
+    all_span = packs[:, kern.size + cells :].astype(jnp.int32).reshape((-1,) + cover_len.shape[1:])
+    return all_kern, all_low, all_span
+
+
 def body(estimate, images, psf, cover_lo, cover_len):
     group, cells_x, cells_y, depth = images.shape
     taps = psf.shape[-1]
@@ -138,23 +150,8 @@
     groups = lax.axis_size("view")
     swap = [(i, (i + 1) % groups) for i in range(groups)]
 
-    start = gather_halo(estimate.astype(jnp.bfloat16), "fy", 1, halo, OUTER_FIRST)
-    start = gather_halo(start, "fx", 0, halo, OUTER_LAST)
-    start, psf_late, lo_late, len_late = lax.optimization_barrier((start, psf, cover_lo, cover_len))
-    kern = psf_late / jnp.sum(psf_late, axis=-1, keepdims=True)
-    pack = jnp.concatenate(
-        [kern.reshape(-1), lo_late.reshape(-1).astype(jnp.float32), len_late.reshape(-1).astype(jnp.float32)]
-    )
-    packs = [pack]
-    for _ in range(groups - 1):
-        packs.append(lax.ppermute(packs[-1], "view", swap))
-    packs = jnp.stack(packs)
-    all_kern = packs[:, : kern.size].reshape((-1,) + kern.shape[1:])
-    cells = cover_lo.size
-    all_low = packs[:, kern.size : kern.size + cells].astype(jnp.int32).reshape((-1,) + cover_lo.shape[1:])
-    all_span = packs[:, kern.size + cells :].astype(jnp.int32).reshape((-1,) + cover_len.shape[1:])
-    lower_part = weight_of(all_kern, all_low, all_span, cells_x, cells_y, depth) + 0.5
-
+    start = gather_halo(estimate.astype(jnp.bfloat16), "fy", 1, halo)
+    start = gather_halo(start, "fx", 0, halo)
     block_x, block_y = lax.axis_index("fx"), lax.axis_index("fy")
     low = lax.dynamic_slice(cover_lo, (0, block_x, block_y), (group, 1, 1))[..., None]
     span = lax.dynamic_slice(cover_len, (0, block_x, block_y), (group, 1, 1))[..., None]
@@ -179,8 +176,8 @@
     for step in range(ITERS):
         wide = start
         if step > 0:
-            wide = gather_halo(joined.astype(jnp.bfloat16), "fy", 1, halo, OUTER_FIRST)
-            wide = gather_halo(wide, "fx", 0, halo, OUTER_LAST)
+            wide = gather_halo(joined.astype(jnp.bfloat16), "fy", 1, halo)
+            wide = gather_halo(wide, "fx", 0, halo)
         wide = wide.astype(jnp.float32)
         field = jnp.einsum("gox,xyz->goyz", table_x, wide, precision=exact)
         field = jnp.einsum("goy,gxyz->gxoz", table_y, field, precision=exact)
@@ -189,9 +186,12 @@
         field = jnp.einsum("goz,gxyo->gxyz", table_z, ratio, precision=exact)
         field = jnp.einsum("goy,gxoz->gxyz", table_y, field, precision=exact)
         field = jnp.einsum("gox,goyz->xyz", table_x, field, precision=exact)
-        below, above = swap_fixed(field[:halo], field[cells_x + halo :], "fx", OUTER_LAST)
+        late = (psf, cover_lo, cover_len) if step == 0 else ()
+        below, above, late = swap_fixed(field[:halo], field[cells_x + halo :], "fx", late)
+        if step == 0:
+            lower_part = weight_of(*view_tables(*late, swap), cells_x, cells_y, depth) + 0.5
         field = add_edges(field[halo : cells_x + halo], below, above, 0)
-        below, above = swap_fixed(field[:, :halo], field[:, cells_y + halo :], "fy", OUTER_FIRST)
+        below, above, _ = swap_fixed(field[:, :halo], field[:, cells_y + halo :], "fy")
         field = add_edges(field[:, halo : cells_y + halo], below, above, 1)
         moving = pack_fixed(field)
         correction = unpack_fixed(moving)

time: 106 us -> 105 us (level)
  waiting for transfers between devices: 44.3 us -> 42.2 us
  starting transfers between devices: 21.5 us -> 22.6 us
    ppermute x17, waiting for transfers between devices: 35.7 us -> 33.6 us  [the longest x8 26.6 us: swap_edges(): second = lax.ppermute(jnp.where(even, to_below, to_above), axis, pairs(1))]
    select_n x16, other arithmetic: 2.58 us -> 0.92 us  [the longest x8 0.45 us: swap_edges(): return (jnp.where(odd, first, second), jnp.where(odd, second, first), late)]
  transfers between devices with their start and end apart: 19 -> 19, of which waited for: 14 -> 14; matrix products, arithmetic and copies ran while one was open for 17% -> 9% of each run, Pallas kernels for 2% -> 2%
where the time goes in v7:
time: 105 us; the launch traced here: 104 us
  waiting for transfers between devices  42.2 us (40%)
  matrix products  24.9 us (24%)
  starting transfers between devices  22.6 us (22%)
  other arithmetic  6.47 us (6%)
  local copies, waits for them, and re-layouts  5.34 us (5%)
  Pallas kernels  1.67 us (2%)
    ppermute x8, waiting for transfers between devices, swap_edges(): second = lax.ppermute(jnp.where(even, to_below, to_above), axis, pairs(1))  26.6 us
    ppermute x8, starting transfers between devices, swap_edges(): second = lax.ppermute(jnp.where(even, to_below, to_above), axis, pairs(1))  17.7 us
    ppermute x2, waiting for transfers between devices, body(): moving = lax.ppermute(moving, 'view', swap)  8.61 us
    ppermute x8, waiting for transfers between devices, swap_edges(): first = lax.ppermute(jnp.where(even, to_above, to_below), axis, pairs(0))  6.92 us
    dot_general x2, matrix products, body(): field = jnp.einsum('gox,goyz->xyz', table_x, field, precision=exact)  5.57 us
    dot_general x2, matrix products, body(): field = jnp.einsum('goy,gxyz->gxoz', table_y, field, precision=exact)  5.48 us
    dot_general x2, matrix products, body(): field = jnp.einsum('goy,gxoz->gxyz', table_y, field, precision=exact)  2.88 us
    dot_general x1, matrix products, weight_of(): jnp.einsum('xym,mz->xyz', plane, sums_z.reshape(-1, depth), precision=lax...  2.77 us
  transfers between devices with their start and end apart: 19, of which 14 were waited for; matrix products, arithmetic and copies ran while one was open for 9% of the time, Pallas kernels for 2%

profile of v7, /device:TPU:20, one launch (start us, length us, event | category | flops | bytes accessed | tf_op | source)
XLA Modules:
  0.0 104.0 jit_solution(13145552583825601284)
XLA Ops:
  3.0 1.9 %collective-permute-start.1 = (bf16[32,16,128]{2,0,1:T(8,128)(2,1)S(1)}, bf16[32,16,128]{2,0,1:T(8,128)(2,1)S(1)}, u32[]{:S(2)}, u32[]{:S(2)}) collective-permute-start(bf16[32,16,128]{2,0,1:T(8,128)(2,1)S(1)} %get-tuple-element.66), channel_id=1, source_target_pairs={{1,2},{2,1},{5,6},{6,5},{9,10},{10,9},{13,14},{14,13},{17,18},{18,... | collective-permute-start | bytes 393224 | tf_op jit(solution)/shard_map/ppermute | solution.py:26
  6.7 3.2 %collective-permute-done.1 = bf16[32,16,128]{2,0,1:T(8,128)(2,1)S(1)} collective-permute-done((bf16[32,16,128]{2,0,1:T(8,128)(2,1)S(1)}, bf16[32,16,128]{2,0,1:T(8,128)(2,1)S(1)}, u32[]{:S(2)}, u32[]{:S(2)}) %collective-permute-start.1) | collective-permute-done | bytes 131104 | tf_op jit(solution)/shard_map/ppermute | solution.py:26
  10.1 2.5 %collective-permute-start.3 = (bf16[16,64,128]{2,0,1:T(8,128)(2,1)S(1)}, bf16[16,64,128]{2,0,1:T(8,128)(2,1)S(1)}, u32[]{:S(2)}, u32[]{:S(2)}) collective-permute-start(bf16[16,64,128]{2,0,1:T(8,128)(2,1)S(1)} %get-tuple-element.50), channel_id=1, source_target_pairs={{4,8},{8,4},{5,9},{9,5},{6,10},{10,6},{7,11},{11,7},{20,24},{24,20... | collective-permute-start | bytes 786440 | tf_op jit(solution)/shard_map/ppermute | solution.py:26
  19.7 2.7 %fusion.7 = f32[3,32,128,32]{2,3,1,0:T(8,128)S(1)} fusion(f32[3,32,64,128]{3,1,2,0:T(8,128)S(1)} %fusion.34, f32[3,32,64]{2,1,0:T(8,128)S(1)} %copy-done.1), kind=kOutput, calls=%fused_computation.7 | convolution fusion | flops 150994944 | bytes 4743168 | tf_op jit(solution)/shard_map/goy,gxyz->gxoz/dot_general | solution.py:183
  25.9 2.8 %fusion.13 = f32[64,64,128]{2,0,1:T(8,128)S(1)} fusion(f32[3,32,64,128]{3,2,1,0:T(8,128)S(1)} %convolution_bitcast_fusion.1, f32[3,32,64]{2,1,0:T(8,128)S(1)} %copy-done.4), kind=kOutput, calls=%fused_computation.18 | convolution fusion | flops 301989888 | bytes 5267456 | tf_op jit(solution)/shard_map/gox,goyz->xyz/dot_general | solution.py:188
  29.3 2.7 %collective-permute-start.5 = (s16[16,65,128]{2,0,1:T(8,128)(2,1)S(1)}, s16[16,65,128]{2,0,1:T(8,128)(2,1)S(1)}, u32[]{:S(2)}, u32[]{:S(2)}) collective-permute-start(s16[16,65,128]{2,0,1:T(8,128)(2,1)S(1)} %get-tuple-element.41), channel_id=1, source_target_pairs={{4,8},{8,4},{5,9},{9,5},{6,10},{10,6},{7,11},{11,7},{20,24},{24,20... | collective-permute-start | bytes 798728 | tf_op jit(solution)/shard_map/ppermute | solution.py:26
  32.4 4.6 %collective-permute-done.5 = s16[16,65,128]{2,0,1:T(8,128)(2,1)S(1)} collective-permute-done((s16[16,65,128]{2,0,1:T(8,128)(2,1)S(1)}, s16[16,65,128]{2,0,1:T(8,128)(2,1)S(1)}, u32[]{:S(2)}, u32[]{:S(2)}) %collective-permute-start.5) | collective-permute-done | bytes 266272 | tf_op jit(solution)/shard_map/ppermute | solution.py:26
  39.5 2.2 %collective-permute-start.7 = (s16[32,17,128]{2,0,1:T(8,128)(2,1)S(1)}, s16[32,17,128]{2,0,1:T(8,128)(2,1)S(1)}, u32[]{:S(2)}, u32[]{:S(2)}) collective-permute-start(s16[32,17,128]{2,0,1:T(8,128)(2,1)S(1)} %get-tuple-element.58), channel_id=1, source_target_pairs={{1,2},{2,1},{5,6},{6,5},{9,10},{10,9},{13,14},{14,13},{17,18},{18,... | collective-permute-start | bytes 417800 | tf_op jit(solution)/shard_map/ppermute | solution.py:26
  44.5 1.9 %collective-permute-done.7 = s16[32,17,128]{2,0,1:T(8,128)(2,1)S(1)} collective-permute-done((s16[32,17,128]{2,0,1:T(8,128)(2,1)S(1)}, s16[32,17,128]{2,0,1:T(8,128)(2,1)S(1)}, u32[]{:S(2)}, u32[]{:S(2)}) %collective-permute-start.7) | collective-permute-done | bytes 139296 | tf_op jit(solution)/shard_map/ppermute | solution.py:26
  47.9 2.8 %fusion.25 = f32[32,32,128]{2,1,0:T(8,128)S(1)} fusion(f32[32,6,4]{0,1,2:T(8,128)S(1)} %convolution_bitcast_fusion.3, f32[32,6,4]{1,0,2:T(8,128)S(1)} %copy.31, f32[6,4,4,128,1]{3,2,1,0,4:T(4,128)S(1)} %convolution_bitcast_fusion.2), kind=kOutput, calls=%fused_computation.26 | convolution fusion | flops 151093248 | bytes 579584 | tf_op jit(solution)/shard_map/xym,mz->xyz/dot_general | solution.py:123
  50.7 2.7 %collective-permute-done.8 = s16[32,33,128]{2,0,1:T(8,128)(2,1)S(1)} collective-permute-done((s16[32,33,128]{2,0,1:T(8,128)(2,1)S(1)}, s16[32,33,128]{2,0,1:T(8,128)(2,1)S(1)}, u32[]{:S(2)}, u32[]{:S(2)}) %collective-permute-start.8) | collective-permute-done | bytes 270368 | tf_op jit(solution)/shard_map/ppermute | solution.py:199
  54.2 2.2 %collective-permute-start.11 = (bf16[32,16,128]{2,0,1:T(8,128)(2,1)S(1)}, bf16[32,16,128]{2,0,1:T(8,128)(2,1)S(1)}, u32[]{:S(2)}, u32[]{:S(2)}) collective-permute-start(bf16[32,16,128]{2,0,1:T(8,128)(2,1)S(1)} %get-tuple-element.62), channel_id=1, source_target_pairs={{1,2},{2,1},{5,6},{6,5},{9,10},{10,9},{13,14},{14,13},{17,18},{18,... | collective-permute-start | bytes 393224 | tf_op jit(solution)/shard_map/ppermute | solution.py:26
  56.4 2.8 %collective-permute-done.10 = bf16[32,16,128]{2,0,1:T(8,128)(2,1)S(1)} collective-permute-done((bf16[32,16,128]{2,0,1:T(8,128)(2,1)S(1)}, bf16[32,16,128]{2,0,1:T(8,128)(2,1)S(1)}, u32[]{:S(2)}, u32[]{:S(2)}) %collective-permute-start.10) | collective-permute-done | bytes 131104 | tf_op jit(solution)/shard_map/ppermute | solution.py:25
  59.2 1.9 %collective-permute-done.11 = bf16[32,16,128]{2,0,1:T(8,128)(2,1)S(1)} collective-permute-done((bf16[32,16,128]{2,0,1:T(8,128)(2,1)S(1)}, bf16[32,16,128]{2,0,1:T(8,128)(2,1)S(1)}, u32[]{:S(2)}, u32[]{:S(2)}) %collective-permute-start.11) | collective-permute-done | bytes 131104 | tf_op jit(solution)/shard_map/ppermute | solution.py:26
  61.3 2.1 %collective-permute-start.13 = (bf16[16,64,128]{2,0,1:T(8,128)(2,1)S(1)}, bf16[16,64,128]{2,0,1:T(8,128)(2,1)S(1)}, u32[]{:S(2)}, u32[]{:S(2)}) collective-permute-start(bf16[16,64,128]{2,0,1:T(8,128)(2,1)S(1)} %get-tuple-element.46), channel_id=1, source_target_pairs={{4,8},{8,4},{5,9},{9,5},{6,10},{10,6},{7,11},{11,7},{20,24},{24,20... | collective-permute-start | bytes 786440 | tf_op jit(solution)/shard_map/ppermute | solution.py:26
  63.5 5.5 %collective-permute-done.13 = bf16[16,64,128]{2,0,1:T(8,128)(2,1)S(1)} collective-permute-done((bf16[16,64,128]{2,0,1:T(8,128)(2,1)S(1)}, bf16[16,64,128]{2,0,1:T(8,128)(2,1)S(1)}, u32[]{:S(2)}, u32[]{:S(2)}) %collective-permute-start.13) | collective-permute-done | bytes 262176 | tf_op jit(solution)/shard_map/ppermute | solution.py:26
  70.0 2.7 %fusion.3 = f32[3,32,128,32]{2,3,1,0:T(8,128)S(1)} fusion(f32[3,32,64,128]{3,1,2,0:T(8,128)S(1)} %fusion.43, f32[3,32,64]{2,1,0:T(8,128)S(1)} %copy-done.1), kind=kOutput, calls=%fused_computation.3 | convolution fusion | flops 150994944 | bytes 4743168 | tf_op jit(solution)/shard_map/goy,gxyz->gxoz/dot_general | solution.py:183
  76.3 2.8 %fusion.16 = f32[64,64,128]{2,0,1:T(8,128)S(1)} fusion(f32[3,32,64,128]{3,2,1,0:T(8,128)S(1)} %convolution_bitcast_fusion, f32[3,32,64]{2,1,0:T(8,128)S(1)} %copy-done.4), kind=kOutput, calls=%fused_computation.19 | convolution fusion | flops 301989888 | bytes 5267456 | tf_op jit(solution)/shard_map/gox,goyz->xyz/dot_general | solution.py:188
  79.6 1.9 %collective-permute-start.15 = (s16[16,65,128]{2,0,1:T(8,128)(2,1)S(1)}, s16[16,65,128]{2,0,1:T(8,128)(2,1)S(1)}, u32[]{:S(2)}, u32[]{:S(2)}) collective-permute-start(s16[16,65,128]{2,0,1:T(8,128)(2,1)S(1)} %get-tuple-element.38), channel_id=1, source_target_pairs={{4,8},{8,4},{5,9},{9,5},{6,10},{10,6},{7,11},{11,7},{20,24},{24,20... | collective-permute-start | bytes 798728 | tf_op jit(solution)/shard_map/ppermute | solution.py:26
  81.5 5.8 %collective-permute-done.15 = s16[16,65,128]{2,0,1:T(8,128)(2,1)S(1)} collective-permute-done((s16[16,65,128]{2,0,1:T(8,128)(2,1)S(1)}, s16[16,65,128]{2,0,1:T(8,128)(2,1)S(1)}, u32[]{:S(2)}, u32[]{:S(2)}) %collective-permute-start.15) | collective-permute-done | bytes 266272 | tf_op jit(solution)/shard_map/ppermute | solution.py:26
  88.2 2.2 %collective-permute-start.17 = (s16[32,17,128]{2,0,1:T(8,128)(2,1)S(1)}, s16[32,17,128]{2,0,1:T(8,128)(2,1)S(1)}, u32[]{:S(2)}, u32[]{:S(2)}) collective-permute-start(s16[32,17,128]{2,0,1:T(8,128)(2,1)S(1)} %get-tuple-element.54), channel_id=1, source_target_pairs={{1,2},{2,1},{5,6},{6,5},{9,10},{10,9},{13,14},{14,13},{17,18},{18,... | collective-permute-start | bytes 417800 | tf_op jit(solution)/shard_map/ppermute | solution.py:26
  90.3 2.8 %collective-permute-done.16 = s16[32,17,128]{2,0,1:T(8,128)(2,1)S(1)} collective-permute-done((s16[32,17,128]{2,0,1:T(8,128)(2,1)S(1)}, s16[32,17,128]{2,0,1:T(8,128)(2,1)S(1)}, u32[]{:S(2)}, u32[]{:S(2)}) %collective-permute-start.16) | collective-permute-done | bytes 139296 | tf_op jit(solution)/shard_map/ppermute | solution.py:25
  93.2 1.9 %collective-permute-done.17 = s16[32,17,128]{2,0,1:T(8,128)(2,1)S(1)} collective-permute-done((s16[32,17,128]{2,0,1:T(8,128)(2,1)S(1)}, s16[32,17,128]{2,0,1:T(8,128)(2,1)S(1)}, u32[]{:S(2)}, u32[]{:S(2)}) %collective-permute-start.17) | collective-permute-done | bytes 139296 | tf_op jit(solution)/shard_map/ppermute | solution.py:26
  96.2 5.9 %collective-permute-done.18 = s16[32,33,128]{2,0,1:T(8,128)(2,1)S(1)} collective-permute-done((s16[32,33,128]{2,0,1:T(8,128)(2,1)S(1)}, s16[32,33,128]{2,0,1:T(8,128)(2,1)S(1)}, u32[]{:S(2)}, u32[]{:S(2)}) %collective-permute-start.18) | collective-permute-done | bytes 270368 | tf_op jit(solution)/shard_map/ppermute | solution.py:199
  (146 shorter events, 32.5 us)
Async XLA Ops:
  0.0 12.6 %copy-start.7 = (f32[3,3,31]{2,1,0:T(4,128)S(1)}, f32[3,3,31]{2,1,0:T(4,128)}, u32[]{:S(2)}) copy-start(f32[3,3,31]{2,1,0:T(4,128)} %param.7) | copy-start | bytes 3352
  1.4 5.3 %collective-permute-start = (bf16[32,16,128]{2,0,1:T(8,128)(2,1)S(1)}, bf16[32,16,128]{2,0,1:T(8,128)(2,1)S(1)}, u32[]{:S(2)}, u32[]{:S(2)}) collective-permute-start(bf16[32,16,128]{2,0,1:T(8,128)(2,1)S(1)} %get-tuple-element.65), channel_id=1, source_target_pairs={{0,1},{1,0},{2,3},{3,2},{4,5},{5,4},{6,7},{7,6},{8,9},{9,8},{10,11... | collective-permute-start | bytes 393224 | tf_op jit(solution)/shard_map/ppermute | solution.py:25
  3.0 6.8 %collective-permute-start.1 = (bf16[32,16,128]{2,0,1:T(8,128)(2,1)S(1)}, bf16[32,16,128]{2,0,1:T(8,128)(2,1)S(1)}, u32[]{:S(2)}, u32[]{:S(2)}) collective-permute-start(bf16[32,16,128]{2,0,1:T(8,128)(2,1)S(1)} %get-tuple-element.66), channel_id=1, source_target_pairs={{1,2},{2,1},{5,6},{6,5},{9,10},{10,9},{13,14},{14,13},{17,18},{18,... | collective-permute-start | bytes 393224 | tf_op jit(solution)/shard_map/ppermute | solution.py:26
  10.0 6.0 %collective-permute-start.2 = (bf16[16,64,128]{2,0,1:T(8,128)(2,1)S(1)}, bf16[16,64,128]{2,0,1:T(8,128)(2,1)S(1)}, u32[]{:S(2)}, u32[]{:S(2)}) collective-permute-start(bf16[16,64,128]{2,0,1:T(8,128)(2,1)S(1)} %get-tuple-element.49), channel_id=1, source_target_pairs={{0,4},{4,0},{8,12},{12,8},{1,5},{5,1},{9,13},{13,9},{2,6},{6,2},{1... | collective-permute-start | bytes 786440 | tf_op jit(solution)/shard_map/ppermute | solution.py:25
  10.1 7.7 %collective-permute-start.3 = (bf16[16,64,128]{2,0,1:T(8,128)(2,1)S(1)}, bf16[16,64,128]{2,0,1:T(8,128)(2,1)S(1)}, u32[]{:S(2)}, u32[]{:S(2)}) collective-permute-start(bf16[16,64,128]{2,0,1:T(8,128)(2,1)S(1)} %get-tuple-element.50), channel_id=1, source_target_pairs={{4,8},{8,4},{5,9},{9,5},{6,10},{10,6},{7,11},{11,7},{20,24},{24,20... | collective-permute-start | bytes 786440 | tf_op jit(solution)/shard_map/ppermute | solution.py:26
  28.7 3.5 %copy-start.5 = (s32[3,4,4]{2,1,0:T(4,128)S(1)}, s32[3,4,4]{2,1,0:T(4,128)}, u32[]{:S(2)}) copy-start(s32[3,4,4]{2,1,0:T(4,128)} %param.8) | copy-start | bytes 580
  28.7 3.6 %copy-start.6 = (s32[3,4,4]{2,1,0:T(4,128)S(1)}, s32[3,4,4]{2,1,0:T(4,128)}, u32[]{:S(2)}) copy-start(s32[3,4,4]{2,1,0:T(4,128)} %param.9) | copy-start | bytes 580
  29.1 2.9 %collective-permute-start.4 = (s16[16,65,128]{2,0,1:T(8,128)(2,1)S(1)}, s16[16,65,128]{2,0,1:T(8,128)(2,1)S(1)}, u32[]{:S(2)}, u32[]{:S(2)}) collective-permute-start(s16[16,65,128]{2,0,1:T(8,128)(2,1)S(1)} %get-tuple-element.42), channel_id=1, source_target_pairs={{0,4},{4,0},{8,12},{12,8},{1,5},{5,1},{9,13},{13,9},{2,6},{6,2},{1... | collective-permute-start | bytes 798728 | tf_op jit(solution)/shard_map/ppermute | solution.py:25
  29.3 7.7 %collective-permute-start.5 = (s16[16,65,128]{2,0,1:T(8,128)(2,1)S(1)}, s16[16,65,128]{2,0,1:T(8,128)(2,1)S(1)}, u32[]{:S(2)}, u32[]{:S(2)}) collective-permute-start(s16[16,65,128]{2,0,1:T(8,128)(2,1)S(1)} %get-tuple-element.41), channel_id=1, source_target_pairs={{4,8},{8,4},{5,9},{9,5},{6,10},{10,6},{7,11},{11,7},{20,24},{24,20... | collective-permute-start | bytes 798728 | tf_op jit(solution)/shard_map/ppermute | solution.py:26
  37.2 4.4 %collective-permute-start.9 = (f32[375]{0:T(512)S(1)}, f32[375]{0:T(512)S(1)}, u32[]{:S(2)}, u32[]{:S(2)}) collective-permute-start(f32[375]{0:T(512)S(1)} %pad_maximum_fusion.2), channel_id=1, source_target_pairs={{0,16},{16,0},{1,17},{17,1},{2,18},{18,2},{3,19},{19,3},{4,20},{20... | collective-permute-start | bytes 4508 | tf_op jit(solution)/shard_map/ppermute | solution.py:135
  39.1 3.6 %copy-start.3 = (pred[128,128,31]{1,0,2:T(32,128)(4,1)S(1)}, pred[128,128,31]{1,0,2:T(32,128)(4,1)}, u32[]{:S(2)}) copy-start(pred[128,128,31]{1,0,2:T(32,128)(4,1)} %iota_compare_fusion) | copy-start | bytes 1523716
  39.4 5.1 %collective-permute-start.6 = (s16[32,17,128]{2,0,1:T(8,128)(2,1)S(1)}, s16[32,17,128]{2,0,1:T(8,128)(2,1)S(1)}, u32[]{:S(2)}, u32[]{:S(2)}) collective-permute-start(s16[32,17,128]{2,0,1:T(8,128)(2,1)S(1)} %get-tuple-element.57), channel_id=1, source_target_pairs={{0,1},{1,0},{2,3},{3,2},{4,5},{5,4},{6,7},{7,6},{8,9},{9,8},{10,11... | collective-permute-start | bytes 417800 | tf_op jit(solution)/shard_map/ppermute | solution.py:25
  39.5 6.9 %collective-permute-start.7 = (s16[32,17,128]{2,0,1:T(8,128)(2,1)S(1)}, s16[32,17,128]{2,0,1:T(8,128)(2,1)S(1)}, u32[]{:S(2)}, u32[]{:S(2)}) collective-permute-start(s16[32,17,128]{2,0,1:T(8,128)(2,1)S(1)} %get-tuple-element.58), channel_id=1, source_target_pairs={{1,2},{2,1},{5,6},{6,5},{9,10},{10,9},{13,14},{14,13},{17,18},{18,... | collective-permute-start | bytes 417800 | tf_op jit(solution)/shard_map/ppermute | solution.py:26
  46.9 6.5 %collective-permute-start.8 = (s16[32,33,128]{2,0,1:T(8,128)(2,1)S(1)}, s16[32,33,128]{2,0,1:T(8,128)(2,1)S(1)}, u32[]{:S(2)}, u32[]{:S(2)}) collective-permute-start(s16[32,33,128]{2,0,1:T(8,128)(2,1)S(1)} %pad_add_fusion), channel_id=1, source_target_pairs={{0,16},{16,0},{1,17},{17,1},{2,18},{18,2},{3,19},{19,3},{4,20},{20... | collective-permute-start | bytes 811016 | tf_op jit(solution)/shard_map/ppermute | solution.py:199
  47.8 5.6 %copy-start = (f32[32,32,128]{2,1,0:T(8,128)S(1)}, f32[32,32,128]{2,1,0:T(8,128)}, u32[]{:S(2)}) copy-start(f32[32,32,128]{2,1,0:T(8,128)} %param.5) | copy-start | bytes 1572868
  54.2 5.0 %collective-permute-start.10 = (bf16[32,16,128]{2,0,1:T(8,128)(2,1)S(1)}, bf16[32,16,128]{2,0,1:T(8,128)(2,1)S(1)}, u32[]{:S(2)}, u32[]{:S(2)}) collective-permute-start(bf16[32,16,128]{2,0,1:T(8,128)(2,1)S(1)} %get-tuple-element.61), channel_id=1, source_target_pairs={{0,1},{1,0},{2,3},{3,2},{4,5},{5,4},{6,7},{7,6},{8,9},{9,8},{10,11... | collective-permute-start | bytes 393224 | tf_op jit(solution)/shard_map/ppermute | solution.py:25
  54.2 6.9 %collective-permute-start.11 = (bf16[32,16,128]{2,0,1:T(8,128)(2,1)S(1)}, bf16[32,16,128]{2,0,1:T(8,128)(2,1)S(1)}, u32[]{:S(2)}, u32[]{:S(2)}) collective-permute-start(bf16[32,16,128]{2,0,1:T(8,128)(2,1)S(1)} %get-tuple-element.62), channel_id=1, source_target_pairs={{1,2},{2,1},{5,6},{6,5},{9,10},{10,9},{13,14},{14,13},{17,18},{18,... | collective-permute-start | bytes 393224 | tf_op jit(solution)/shard_map/ppermute | solution.py:26
  61.3 2.2 %collective-permute-start.12 = (bf16[16,64,128]{2,0,1:T(8,128)(2,1)S(1)}, bf16[16,64,128]{2,0,1:T(8,128)(2,1)S(1)}, u32[]{:S(2)}, u32[]{:S(2)}) collective-permute-start(bf16[16,64,128]{2,0,1:T(8,128)(2,1)S(1)} %get-tuple-element.45), channel_id=1, source_target_pairs={{0,4},{4,0},{8,12},{12,8},{1,5},{5,1},{9,13},{13,9},{2,6},{6,2},{1... | collective-permute-start | bytes 786440 | tf_op jit(solution)/shard_map/ppermute | solution.py:25
  61.3 7.7 %collective-permute-start.13 = (bf16[16,64,128]{2,0,1:T(8,128)(2,1)S(1)}, bf16[16,64,128]{2,0,1:T(8,128)(2,1)S(1)}, u32[]{:S(2)}, u32[]{:S(2)}) collective-permute-start(bf16[16,64,128]{2,0,1:T(8,128)(2,1)S(1)} %get-tuple-element.46), channel_id=1, source_target_pairs={{4,8},{8,4},{5,9},{9,5},{6,10},{10,6},{7,11},{11,7},{20,24},{24,20... | collective-permute-start | bytes 786440 | tf_op jit(solution)/shard_map/ppermute | solution.py:26
  79.5 2.0 %collective-permute-start.14 = (s16[16,65,128]{2,0,1:T(8,128)(2,1)S(1)}, s16[16,65,128]{2,0,1:T(8,128)(2,1)S(1)}, u32[]{:S(2)}, u32[]{:S(2)}) collective-permute-start(s16[16,65,128]{2,0,1:T(8,128)(2,1)S(1)} %get-tuple-element.37), channel_id=1, source_target_pairs={{0,4},{4,0},{8,12},{12,8},{1,5},{5,1},{9,13},{13,9},{2,6},{6,2},{1... | collective-permute-start | bytes 798728 | tf_op jit(solution)/shard_map/ppermute | solution.py:25
  79.6 7.7 %collective-permute-start.15 = (s16[16,65,128]{2,0,1:T(8,128)(2,1)S(1)}, s16[16,65,128]{2,0,1:T(8,128)(2,1)S(1)}, u32[]{:S(2)}, u32[]{:S(2)}) collective-permute-start(s16[16,65,128]{2,0,1:T(8,128)(2,1)S(1)} %get-tuple-element.38), channel_id=1, source_target_pairs={{4,8},{8,4},{5,9},{9,5},{6,10},{10,6},{7,11},{11,7},{20,24},{24,20... | collective-permute-start | bytes 798728 | tf_op jit(solution)/shard_map/ppermute | solution.py:26
  88.1 5.1 %collective-permute-start.16 = (s16[32,17,128]{2,0,1:T(8,128)(2,1)S(1)}, s16[32,17,128]{2,0,1:T(8,128)(2,1)S(1)}, u32[]{:S(2)}, u32[]{:S(2)}) collective-permute-start(s16[32,17,128]{2,0,1:T(8,128)(2,1)S(1)} %get-tuple-element.53), channel_id=1, source_target_pairs={{0,1},{1,0},{2,3},{3,2},{4,5},{5,4},{6,7},{7,6},{8,9},{9,8},{10,11... | collective-permute-start | bytes 417800 | tf_op jit(solution)/shard_map/ppermute | solution.py:25
  88.2 6.9 %collective-permute-start.17 = (s16[32,17,128]{2,0,1:T(8,128)(2,1)S(1)}, s16[32,17,128]{2,0,1:T(8,128)(2,1)S(1)}, u32[]{:S(2)}, u32[]{:S(2)}) collective-permute-start(s16[32,17,128]{2,0,1:T(8,128)(2,1)S(1)} %get-tuple-element.54), channel_id=1, source_target_pairs={{1,2},{2,1},{5,6},{6,5},{9,10},{10,9},{13,14},{14,13},{17,18},{18,... | collective-permute-start | bytes 417800 | tf_op jit(solution)/shard_map/ppermute | solution.py:26
  95.6 6.5 %collective-permute-start.18 = (s16[32,33,128]{2,0,1:T(8,128)(2,1)S(1)}, s16[32,33,128]{2,0,1:T(8,128)(2,1)S(1)}, u32[]{:S(2)}, u32[]{:S(2)}) collective-permute-start(s16[32,33,128]{2,0,1:T(8,128)(2,1)S(1)} %pad_add_fusion.1), channel_id=1, source_target_pairs={{0,16},{16,0},{1,17},{17,1},{2,18},{18,2},{3,19},{19,3},{4,20},{20... | collective-permute-start | bytes 811016 | tf_op jit(solution)/shard_map/ppermute | solution.py:199
  (5 other events, 8.3 us)

commit v8 on v7

--- a/solution.py
+++ b/solution.py
@@ -26,6 +26,8 @@
     second = lax.ppermute(jnp.where(even, to_below, to_above), axis, pairs(1))
     if late:
         first, *late = lax.optimization_barrier((first, *late))
+    if axis == "fx":
+        return jnp.where(even, second, first), jnp.where(even, first, second), late
     odd = jnp.logical_not(even)
     return jnp.where(odd, first, second), jnp.where(odd, second, first), late
 
@@ -86,17 +88,6 @@
         table_z[k] = jnp.where((gap >= -radius) & (gap <= radius), turned, 0.0)
 
 
-def band(weights, rows, cols, shift):
-    taps = weights.shape[-1]
-    gap = (
-        jnp.arange(cols, dtype=jnp.int32)[None, :]
-        - jnp.arange(rows, dtype=jnp.int32)[:, None]
-        + shift
-    )
-    picks = (gap[:, :, None] == jnp.arange(taps, dtype=jnp.int32)).astype(jnp.float32)
-    return jnp.einsum("oit,gt->goi", picks, weights, precision=lax.Precision.HIGHEST)
-
-
 def block_sums(weights, axis, cells):
     blocks = lax.axis_size(axis)
     taps = weights.shape[-1]
@@ -112,12 +103,10 @@
     taps = kern.shape[-1]
     sums_x = block_sums(kern[:, 0], "fx", cells_x)
     sums_y = block_sums(kern[:, 1], "fy", cells_y)
-    levels = jnp.arange(depth, dtype=jnp.int32)
-    inside = (levels >= low[..., None]) & (levels < (low + span)[..., None])
-    table_z = band(kern[:, 2], depth, depth, (taps - 1) // 2)
-    sums_z = jnp.einsum(
-        "gxyi,gio->gxyo", inside.astype(jnp.float32), table_z, precision=lax.Precision.HIGHEST
-    )
+    shift = jnp.arange(depth, dtype=jnp.int32)[None, :] - jnp.arange(taps, dtype=jnp.int32)[:, None]
+    source = (shift + (taps - 1) // 2)[:, None, None, None, :]
+    inside = (source >= low[None, ..., None]) & (source < (low + span)[None, ..., None])
+    sums_z = jnp.sum(jnp.where(inside, kern[:, 2].T[:, :, None, None, None], 0.0), axis=0)
     plane = sums_x[:, None, :, :, None] * sums_y[None, :, :, None, :]
     plane = plane.reshape(cells_x, cells_y, -1)
     return jnp.einsum(

time: 105 us -> 104 us (level)
  waiting for transfers between devices: 42.2 us -> 44.3 us
  matrix products: 24.9 us -> 23.5 us
  starting transfers between devices: 22.6 us -> 21.4 us
    ppermute x8, waiting for transfers between devices: 26.6 us -> 28.6 us  [swap_edges(): second = lax.ppermute(jnp.where(even, to_below, to_above), axis, pairs(1))]
    dot_general x2 -> x0, matrix products: 1.4 us -> none  [the longest x1 1.04 us: band(): jnp.einsum('oit,gt->goi', picks, weights, precision=lax.Precision.HIGHEST)]
    reduce_sum x0 -> x1, other arithmetic: none -> 1.31 us  [weight_of(): jnp.sum(jnp.where(inside, kern[:, 2].T[:, :, None, None, None], 0.0), axi...]
    ppermute x8, starting transfers between devices: 17.7 us -> 16.6 us  [swap_edges(): second = lax.ppermute(jnp.where(even, to_below, to_above), axis, pairs(1))]
    eq x1 -> x0, other arithmetic: 1.08 us -> none  [band(): gap[:, :, None] == jnp.arange(taps, dtype=jnp.int32)]
  transfers between devices with their start and end apart: 19 -> 19, of which waited for: 14 -> 14; matrix products, arithmetic and copies ran while one was open for 9% -> 8% of each run, Pallas kernels for 2% -> 2%
where the time goes in v8:
time: 104 us
  waiting for transfers between devices  44.3 us (43%)
  matrix products  23.5 us (23%)
  starting transfers between devices  21.4 us (21%)
  other arithmetic  6.7 us (6%)
  local copies, waits for them, and re-layouts  5.44 us (5%)
  Pallas kernels  1.66 us (2%)
    ppermute x8, waiting for transfers between devices, swap_edges(): second = lax.ppermute(jnp.where(even, to_below, to_above), axis, pairs(1))  28.6 us
    ppermute x8, starting transfers between devices, swap_edges(): second = lax.ppermute(jnp.where(even, to_below, to_above), axis, pairs(1))  16.6 us
    ppermute x2, waiting for transfers between devices, body(): moving = lax.ppermute(moving, 'view', swap)  8.67 us
    ppermute x8, waiting for transfers between devices, swap_edges(): first = lax.ppermute(jnp.where(even, to_above, to_below), axis, pairs(0))  7.02 us
    dot_general x2, matrix products, body(): field = jnp.einsum('gox,goyz->xyz', table_x, field, precision=exact)  5.57 us
    dot_general x2, matrix products, body(): field = jnp.einsum('goy,gxyz->gxoz', table_y, field, precision=exact)  5.48 us
    dot_general x2, matrix products, body(): field = jnp.einsum('goy,gxoz->gxyz', table_y, field, precision=exact)  2.88 us
    dot_general x1, matrix products, weight_of(): jnp.einsum('xym,mz->xyz', plane, sums_z.reshape(-1, depth), precision=lax...  2.78 us
  transfers between devices with their start and end apart: 19, of which 14 were waited for; matrix products, arithmetic and copies ran while one was open for 8% of the time, Pallas kernels for 2%

profile of v8, /device:TPU:20, one launch (start us, length us, event | category | flops | bytes accessed | tf_op | source)
XLA Modules:
  0.0 103.8 jit_solution(16203881636575110554)
XLA Ops:
  3.0 1.9 %collective-permute-start.1 = (bf16[32,16,128]{2,0,1:T(8,128)(2,1)S(1)}, bf16[32,16,128]{2,0,1:T(8,128)(2,1)S(1)}, u32[]{:S(2)}, u32[]{:S(2)}) collective-permute-start(bf16[32,16,128]{2,0,1:T(8,128)(2,1)S(1)} %get-tuple-element.66), channel_id=1, source_target_pairs={{1,2},{2,1},{5,6},{6,5},{9,10},{10,9},{13,14},{14,13},{17,18},{18,... | collective-permute-start | bytes 393224 | tf_op jit(solution)/shard_map/ppermute | solution.py:26
  6.7 3.2 %collective-permute-done.1 = bf16[32,16,128]{2,0,1:T(8,128)(2,1)S(1)} collective-permute-done((bf16[32,16,128]{2,0,1:T(8,128)(2,1)S(1)}, bf16[32,16,128]{2,0,1:T(8,128)(2,1)S(1)}, u32[]{:S(2)}, u32[]{:S(2)}) %collective-permute-start.1) | collective-permute-done | bytes 131104 | tf_op jit(solution)/shard_map/ppermute | solution.py:26
  10.0 1.9 %collective-permute-start.2 = (bf16[16,64,128]{2,0,1:T(8,128)(2,1)S(1)}, bf16[16,64,128]{2,0,1:T(8,128)(2,1)S(1)}, u32[]{:S(2)}, u32[]{:S(2)}) collective-permute-start(bf16[16,64,128]{2,0,1:T(8,128)(2,1)S(1)} %get-tuple-element.49), channel_id=1, source_target_pairs={{4,8},{8,4},{5,9},{9,5},{6,10},{10,6},{7,11},{11,7},{20,24},{24,20... | collective-permute-start | bytes 786440 | tf_op jit(solution)/shard_map/ppermute | solution.py:26
  14.4 3.3 %collective-permute-done.2 = bf16[16,64,128]{2,0,1:T(8,128)(2,1)S(1)} collective-permute-done((bf16[16,64,128]{2,0,1:T(8,128)(2,1)S(1)}, bf16[16,64,128]{2,0,1:T(8,128)(2,1)S(1)}, u32[]{:S(2)}, u32[]{:S(2)}) %collective-permute-start.2) | collective-permute-done | bytes 262176 | tf_op jit(solution)/shard_map/ppermute | solution.py:26
  19.6 2.7 %fusion.7 = f32[3,32,128,32]{2,3,1,0:T(8,128)S(1)} fusion(f32[3,32,64,128]{3,1,2,0:T(8,128)S(1)} %fusion.29, f32[3,32,64]{2,1,0:T(8,128)S(1)} %copy-done.1), kind=kOutput, calls=%fused_computation.7 | convolution fusion | flops 150994944 | bytes 4743168 | tf_op jit(solution)/shard_map/goy,gxyz->gxoz/dot_general | solution.py:172
  25.9 2.8 %fusion.11 = f32[64,64,128]{2,0,1:T(8,128)S(1)} fusion(f32[3,32,64,128]{3,2,1,0:T(8,128)S(1)} %convolution_bitcast_fusion.1, f32[3,32,64]{2,1,0:T(8,128)S(1)} %copy-done.3), kind=kOutput, calls=%fused_computation.15 | convolution fusion | flops 301989888 | bytes 5267456 | tf_op jit(solution)/shard_map/gox,goyz->xyz/dot_general | solution.py:177
  29.2 2.1 %collective-permute-start.4 = (s16[16,65,128]{2,0,1:T(8,128)(2,1)S(1)}, s16[16,65,128]{2,0,1:T(8,128)(2,1)S(1)}, u32[]{:S(2)}, u32[]{:S(2)}) collective-permute-start(s16[16,65,128]{2,0,1:T(8,128)(2,1)S(1)} %get-tuple-element.41), channel_id=1, source_target_pairs={{4,8},{8,4},{5,9},{9,5},{6,10},{10,6},{7,11},{11,7},{20,24},{24,20... | collective-permute-start | bytes 798728 | tf_op jit(solution)/shard_map/ppermute | solution.py:26
  31.7 5.2 %collective-permute-done.4 = s16[16,65,128]{2,0,1:T(8,128)(2,1)S(1)} collective-permute-done((s16[16,65,128]{2,0,1:T(8,128)(2,1)S(1)}, s16[16,65,128]{2,0,1:T(8,128)(2,1)S(1)}, u32[]{:S(2)}, u32[]{:S(2)}) %collective-permute-start.4) | collective-permute-done | bytes 266272 | tf_op jit(solution)/shard_map/ppermute | solution.py:26
  39.4 2.2 %collective-permute-start.7 = (s16[32,17,128]{2,0,1:T(8,128)(2,1)S(1)}, s16[32,17,128]{2,0,1:T(8,128)(2,1)S(1)}, u32[]{:S(2)}, u32[]{:S(2)}) collective-permute-start(s16[32,17,128]{2,0,1:T(8,128)(2,1)S(1)} %get-tuple-element.58), channel_id=1, source_target_pairs={{1,2},{2,1},{5,6},{6,5},{9,10},{10,9},{13,14},{14,13},{17,18},{18,... | collective-permute-start | bytes 417800 | tf_op jit(solution)/shard_map/ppermute | solution.py:26
  44.4 1.9 %collective-permute-done.7 = s16[32,17,128]{2,0,1:T(8,128)(2,1)S(1)} collective-permute-done((s16[32,17,128]{2,0,1:T(8,128)(2,1)S(1)}, s16[32,17,128]{2,0,1:T(8,128)(2,1)S(1)}, u32[]{:S(2)}, u32[]{:S(2)}) %collective-permute-start.7) | collective-permute-done | bytes 139296 | tf_op jit(solution)/shard_map/ppermute | solution.py:26
  47.8 2.8 %fusion.23 = f32[32,32,128]{2,1,0:T(8,128)S(1)} fusion(f32[32,6,4]{0,1,2:T(8,128)S(1)} %convolution_bitcast_fusion.2, f32[32,6,4]{1,0,2:T(8,128)S(1)} %copy.32, f32[6,4,4,128,1]{3,2,1,0,4:T(4,128)S(1)} %bitcast.120), kind=kOutput, calls=%fused_computation.24 | convolution fusion | flops 151093248 | bytes 579584 | tf_op jit(solution)/shard_map/xym,mz->xyz/dot_general | solution.py:112
  50.6 2.7 %collective-permute-done.8 = s16[32,33,128]{2,0,1:T(8,128)(2,1)S(1)} collective-permute-done((s16[32,33,128]{2,0,1:T(8,128)(2,1)S(1)}, s16[32,33,128]{2,0,1:T(8,128)(2,1)S(1)}, u32[]{:S(2)}, u32[]{:S(2)}) %collective-permute-start.8) | collective-permute-done | bytes 270368 | tf_op jit(solution)/shard_map/ppermute | solution.py:188
  54.2 2.2 %collective-permute-start.11 = (bf16[32,16,128]{2,0,1:T(8,128)(2,1)S(1)}, bf16[32,16,128]{2,0,1:T(8,128)(2,1)S(1)}, u32[]{:S(2)}, u32[]{:S(2)}) collective-permute-start(bf16[32,16,128]{2,0,1:T(8,128)(2,1)S(1)} %get-tuple-element.62), channel_id=1, source_target_pairs={{1,2},{2,1},{5,6},{6,5},{9,10},{10,9},{13,14},{14,13},{17,18},{18,... | collective-permute-start | bytes 393224 | tf_op jit(solution)/shard_map/ppermute | solution.py:26
  56.4 2.8 %collective-permute-done.10 = bf16[32,16,128]{2,0,1:T(8,128)(2,1)S(1)} collective-permute-done((bf16[32,16,128]{2,0,1:T(8,128)(2,1)S(1)}, bf16[32,16,128]{2,0,1:T(8,128)(2,1)S(1)}, u32[]{:S(2)}, u32[]{:S(2)}) %collective-permute-start.10) | collective-permute-done | bytes 131104 | tf_op jit(solution)/shard_map/ppermute | solution.py:25
  59.1 1.9 %collective-permute-done.11 = bf16[32,16,128]{2,0,1:T(8,128)(2,1)S(1)} collective-permute-done((bf16[32,16,128]{2,0,1:T(8,128)(2,1)S(1)}, bf16[32,16,128]{2,0,1:T(8,128)(2,1)S(1)}, u32[]{:S(2)}, u32[]{:S(2)}) %collective-permute-start.11) | collective-permute-done | bytes 131104 | tf_op jit(solution)/shard_map/ppermute | solution.py:26
  61.2 2.1 %collective-permute-start.12 = (bf16[16,64,128]{2,0,1:T(8,128)(2,1)S(1)}, bf16[16,64,128]{2,0,1:T(8,128)(2,1)S(1)}, u32[]{:S(2)}, u32[]{:S(2)}) collective-permute-start(bf16[16,64,128]{2,0,1:T(8,128)(2,1)S(1)} %get-tuple-element.45), channel_id=1, source_target_pairs={{4,8},{8,4},{5,9},{9,5},{6,10},{10,6},{7,11},{11,7},{20,24},{24,20... | collective-permute-start | bytes 786440 | tf_op jit(solution)/shard_map/ppermute | solution.py:26
  63.4 5.5 %collective-permute-done.12 = bf16[16,64,128]{2,0,1:T(8,128)(2,1)S(1)} collective-permute-done((bf16[16,64,128]{2,0,1:T(8,128)(2,1)S(1)}, bf16[16,64,128]{2,0,1:T(8,128)(2,1)S(1)}, u32[]{:S(2)}, u32[]{:S(2)}) %collective-permute-start.12) | collective-permute-done | bytes 262176 | tf_op jit(solution)/shard_map/ppermute | solution.py:26
  69.9 2.7 %fusion.3 = f32[3,32,128,32]{2,3,1,0:T(8,128)S(1)} fusion(f32[3,32,64,128]{3,1,2,0:T(8,128)S(1)} %fusion.38, f32[3,32,64]{2,1,0:T(8,128)S(1)} %copy-done.1), kind=kOutput, calls=%fused_computation.3 | convolution fusion | flops 150994944 | bytes 4743168 | tf_op jit(solution)/shard_map/goy,gxyz->gxoz/dot_general | solution.py:172
  76.1 2.8 %fusion.14 = f32[64,64,128]{2,0,1:T(8,128)S(1)} fusion(f32[3,32,64,128]{3,2,1,0:T(8,128)S(1)} %convolution_bitcast_fusion, f32[3,32,64]{2,1,0:T(8,128)S(1)} %copy-done.3), kind=kOutput, calls=%fused_computation.16 | convolution fusion | flops 301989888 | bytes 5267456 | tf_op jit(solution)/shard_map/gox,goyz->xyz/dot_general | solution.py:177
  79.4 1.9 %collective-permute-start.14 = (s16[16,65,128]{2,0,1:T(8,128)(2,1)S(1)}, s16[16,65,128]{2,0,1:T(8,128)(2,1)S(1)}, u32[]{:S(2)}, u32[]{:S(2)}) collective-permute-start(s16[16,65,128]{2,0,1:T(8,128)(2,1)S(1)} %get-tuple-element.37), channel_id=1, source_target_pairs={{4,8},{8,4},{5,9},{9,5},{6,10},{10,6},{7,11},{11,7},{20,24},{24,20... | collective-permute-start | bytes 798728 | tf_op jit(solution)/shard_map/ppermute | solution.py:26
  81.4 5.7 %collective-permute-done.14 = s16[16,65,128]{2,0,1:T(8,128)(2,1)S(1)} collective-permute-done((s16[16,65,128]{2,0,1:T(8,128)(2,1)S(1)}, s16[16,65,128]{2,0,1:T(8,128)(2,1)S(1)}, u32[]{:S(2)}, u32[]{:S(2)}) %collective-permute-start.14) | collective-permute-done | bytes 266272 | tf_op jit(solution)/shard_map/ppermute | solution.py:26
  87.9 2.2 %collective-permute-start.17 = (s16[32,17,128]{2,0,1:T(8,128)(2,1)S(1)}, s16[32,17,128]{2,0,1:T(8,128)(2,1)S(1)}, u32[]{:S(2)}, u32[]{:S(2)}) collective-permute-start(s16[32,17,128]{2,0,1:T(8,128)(2,1)S(1)} %get-tuple-element.54), channel_id=1, source_target_pairs={{1,2},{2,1},{5,6},{6,5},{9,10},{10,9},{13,14},{14,13},{17,18},{18,... | collective-permute-start | bytes 417800 | tf_op jit(solution)/shard_map/ppermute | solution.py:26
  90.1 2.8 %collective-permute-done.16 = s16[32,17,128]{2,0,1:T(8,128)(2,1)S(1)} collective-permute-done((s16[32,17,128]{2,0,1:T(8,128)(2,1)S(1)}, s16[32,17,128]{2,0,1:T(8,128)(2,1)S(1)}, u32[]{:S(2)}, u32[]{:S(2)}) %collective-permute-start.16) | collective-permute-done | bytes 139296 | tf_op jit(solution)/shard_map/ppermute | solution.py:25
  96.0 5.9 %collective-permute-done.18 = s16[32,33,128]{2,0,1:T(8,128)(2,1)S(1)} collective-permute-done((s16[32,33,128]{2,0,1:T(8,128)(2,1)S(1)}, s16[32,33,128]{2,0,1:T(8,128)(2,1)S(1)}, u32[]{:S(2)}, u32[]{:S(2)}) %collective-permute-start.18) | collective-permute-done | bytes 270368 | tf_op jit(solution)/shard_map/ppermute | solution.py:188
  (143 shorter events, 31.6 us)
Async XLA Ops:
  0.0 12.1 %copy-start.6 = (f32[3,3,31]{2,1,0:T(4,128)S(1)}, f32[3,3,31]{2,1,0:T(4,128)}, u32[]{:S(2)}) copy-start(f32[3,3,31]{2,1,0:T(4,128)} %param.7) | copy-start | bytes 3352
  1.4 5.3 %collective-permute-start = (bf16[32,16,128]{2,0,1:T(8,128)(2,1)S(1)}, bf16[32,16,128]{2,0,1:T(8,128)(2,1)S(1)}, u32[]{:S(2)}, u32[]{:S(2)}) collective-permute-start(bf16[32,16,128]{2,0,1:T(8,128)(2,1)S(1)} %get-tuple-element.65), channel_id=1, source_target_pairs={{0,1},{1,0},{2,3},{3,2},{4,5},{5,4},{6,7},{7,6},{8,9},{9,8},{10,11... | collective-permute-start | bytes 393224 | tf_op jit(solution)/shard_map/ppermute | solution.py:25
  3.0 6.8 %collective-permute-start.1 = (bf16[32,16,128]{2,0,1:T(8,128)(2,1)S(1)}, bf16[32,16,128]{2,0,1:T(8,128)(2,1)S(1)}, u32[]{:S(2)}, u32[]{:S(2)}) collective-permute-start(bf16[32,16,128]{2,0,1:T(8,128)(2,1)S(1)} %get-tuple-element.66), channel_id=1, source_target_pairs={{1,2},{2,1},{5,6},{6,5},{9,10},{10,9},{13,14},{14,13},{17,18},{18,... | collective-permute-start | bytes 393224 | tf_op jit(solution)/shard_map/ppermute | solution.py:26
  10.0 7.7 %collective-permute-start.2 = (bf16[16,64,128]{2,0,1:T(8,128)(2,1)S(1)}, bf16[16,64,128]{2,0,1:T(8,128)(2,1)S(1)}, u32[]{:S(2)}, u32[]{:S(2)}) collective-permute-start(bf16[16,64,128]{2,0,1:T(8,128)(2,1)S(1)} %get-tuple-element.49), channel_id=1, source_target_pairs={{4,8},{8,4},{5,9},{9,5},{6,10},{10,6},{7,11},{11,7},{20,24},{24,20... | collective-permute-start | bytes 786440 | tf_op jit(solution)/shard_map/ppermute | solution.py:26
  12.0 5.8 %collective-permute-start.3 = (bf16[16,64,128]{2,0,1:T(8,128)(2,1)S(1)}, bf16[16,64,128]{2,0,1:T(8,128)(2,1)S(1)}, u32[]{:S(2)}, u32[]{:S(2)}) collective-permute-start(bf16[16,64,128]{2,0,1:T(8,128)(2,1)S(1)} %get-tuple-element.50), channel_id=1, source_target_pairs={{0,4},{4,0},{8,12},{12,8},{1,5},{5,1},{9,13},{13,9},{2,6},{6,2},{1... | collective-permute-start | bytes 786440 | tf_op jit(solution)/shard_map/ppermute | solution.py:25
  19.6 2.8 %copy-start.2 = (f32[3,128,128]{2,1,0:T(8,128)S(1)}, f32[3,128,128]{2,1,0:T(8,128)}, u32[]{:S(2)}) copy-start(f32[3,128,128]{2,1,0:T(8,128)} %get-tuple-element.14) | copy-start | bytes 589828
  28.6 2.9 %copy-start.4 = (s32[3,4,4]{2,1,0:T(4,128)S(1)}, s32[3,4,4]{2,1,0:T(4,128)}, u32[]{:S(2)}) copy-start(s32[3,4,4]{2,1,0:T(4,128)} %param.8) | copy-start | bytes 580
  28.6 3.0 %copy-start.5 = (s32[3,4,4]{2,1,0:T(4,128)S(1)}, s32[3,4,4]{2,1,0:T(4,128)}, u32[]{:S(2)}) copy-start(s32[3,4,4]{2,1,0:T(4,128)} %param.9) | copy-start | bytes 580
  29.1 2.3 %collective-permute-start.5 = (s16[16,65,128]{2,0,1:T(8,128)(2,1)S(1)}, s16[16,65,128]{2,0,1:T(8,128)(2,1)S(1)}, u32[]{:S(2)}, u32[]{:S(2)}) collective-permute-start(s16[16,65,128]{2,0,1:T(8,128)(2,1)S(1)} %get-tuple-element.42), channel_id=1, source_target_pairs={{0,4},{4,0},{8,12},{12,8},{1,5},{5,1},{9,13},{13,9},{2,6},{6,2},{1... | collective-permute-start | bytes 798728 | tf_op jit(solution)/shard_map/ppermute | solution.py:25
  29.2 7.7 %collective-permute-start.4 = (s16[16,65,128]{2,0,1:T(8,128)(2,1)S(1)}, s16[16,65,128]{2,0,1:T(8,128)(2,1)S(1)}, u32[]{:S(2)}, u32[]{:S(2)}) collective-permute-start(s16[16,65,128]{2,0,1:T(8,128)(2,1)S(1)} %get-tuple-element.41), channel_id=1, source_target_pairs={{4,8},{8,4},{5,9},{9,5},{6,10},{10,6},{7,11},{11,7},{20,24},{24,20... | collective-permute-start | bytes 798728 | tf_op jit(solution)/shard_map/ppermute | solution.py:26
  37.2 4.4 %collective-permute-start.9 = (f32[375]{0:T(512)S(1)}, f32[375]{0:T(512)S(1)}, u32[]{:S(2)}, u32[]{:S(2)}) collective-permute-start(f32[375]{0:T(512)S(1)} %pad_maximum_fusion.2), channel_id=1, source_target_pairs={{0,16},{16,0},{1,17},{17,1},{2,18},{18,2},{3,19},{19,3},{4,20},{20... | collective-permute-start | bytes 4508 | tf_op jit(solution)/shard_map/ppermute | solution.py:124
  39.3 5.1 %collective-permute-start.6 = (s16[32,17,128]{2,0,1:T(8,128)(2,1)S(1)}, s16[32,17,128]{2,0,1:T(8,128)(2,1)S(1)}, u32[]{:S(2)}, u32[]{:S(2)}) collective-permute-start(s16[32,17,128]{2,0,1:T(8,128)(2,1)S(1)} %get-tuple-element.57), channel_id=1, source_target_pairs={{0,1},{1,0},{2,3},{3,2},{4,5},{5,4},{6,7},{7,6},{8,9},{9,8},{10,11... | collective-permute-start | bytes 417800 | tf_op jit(solution)/shard_map/ppermute | solution.py:25
  39.4 6.9 %collective-permute-start.7 = (s16[32,17,128]{2,0,1:T(8,128)(2,1)S(1)}, s16[32,17,128]{2,0,1:T(8,128)(2,1)S(1)}, u32[]{:S(2)}, u32[]{:S(2)}) collective-permute-start(s16[32,17,128]{2,0,1:T(8,128)(2,1)S(1)} %get-tuple-element.58), channel_id=1, source_target_pairs={{1,2},{2,1},{5,6},{6,5},{9,10},{10,9},{13,14},{14,13},{17,18},{18,... | collective-permute-start | bytes 417800 | tf_op jit(solution)/shard_map/ppermute | solution.py:26
  46.8 6.6 %copy-start = (f32[32,32,128]{2,1,0:T(8,128)S(1)}, f32[32,32,128]{2,1,0:T(8,128)}, u32[]{:S(2)}) copy-start(f32[32,32,128]{2,1,0:T(8,128)} %param.5) | copy-start | bytes 1572868
  46.8 6.5 %collective-permute-start.8 = (s16[32,33,128]{2,0,1:T(8,128)(2,1)S(1)}, s16[32,33,128]{2,0,1:T(8,128)(2,1)S(1)}, u32[]{:S(2)}, u32[]{:S(2)}) collective-permute-start(s16[32,33,128]{2,0,1:T(8,128)(2,1)S(1)} %pad_add_fusion), channel_id=1, source_target_pairs={{0,16},{16,0},{1,17},{17,1},{2,18},{18,2},{3,19},{19,3},{4,20},{20... | collective-permute-start | bytes 811016 | tf_op jit(solution)/shard_map/ppermute | solution.py:188
  54.1 5.0 %collective-permute-start.10 = (bf16[32,16,128]{2,0,1:T(8,128)(2,1)S(1)}, bf16[32,16,128]{2,0,1:T(8,128)(2,1)S(1)}, u32[]{:S(2)}, u32[]{:S(2)}) collective-permute-start(bf16[32,16,128]{2,0,1:T(8,128)(2,1)S(1)} %get-tuple-element.61), channel_id=1, source_target_pairs={{0,1},{1,0},{2,3},{3,2},{4,5},{5,4},{6,7},{7,6},{8,9},{9,8},{10,11... | collective-permute-start | bytes 393224 | tf_op jit(solution)/shard_map/ppermute | solution.py:25
  54.2 6.9 %collective-permute-start.11 = (bf16[32,16,128]{2,0,1:T(8,128)(2,1)S(1)}, bf16[32,16,128]{2,0,1:T(8,128)(2,1)S(1)}, u32[]{:S(2)}, u32[]{:S(2)}) collective-permute-start(bf16[32,16,128]{2,0,1:T(8,128)(2,1)S(1)} %get-tuple-element.62), channel_id=1, source_target_pairs={{1,2},{2,1},{5,6},{6,5},{9,10},{10,9},{13,14},{14,13},{17,18},{18,... | collective-permute-start | bytes 393224 | tf_op jit(solution)/shard_map/ppermute | solution.py:26
  61.2 7.7 %collective-permute-start.12 = (bf16[16,64,128]{2,0,1:T(8,128)(2,1)S(1)}, bf16[16,64,128]{2,0,1:T(8,128)(2,1)S(1)}, u32[]{:S(2)}, u32[]{:S(2)}) collective-permute-start(bf16[16,64,128]{2,0,1:T(8,128)(2,1)S(1)} %get-tuple-element.45), channel_id=1, source_target_pairs={{4,8},{8,4},{5,9},{9,5},{6,10},{10,6},{7,11},{11,7},{20,24},{24,20... | collective-permute-start | bytes 786440 | tf_op jit(solution)/shard_map/ppermute | solution.py:26
  63.3 5.5 %collective-permute-start.13 = (bf16[16,64,128]{2,0,1:T(8,128)(2,1)S(1)}, bf16[16,64,128]{2,0,1:T(8,128)(2,1)S(1)}, u32[]{:S(2)}, u32[]{:S(2)}) collective-permute-start(bf16[16,64,128]{2,0,1:T(8,128)(2,1)S(1)} %get-tuple-element.46), channel_id=1, source_target_pairs={{0,4},{4,0},{8,12},{12,8},{1,5},{5,1},{9,13},{13,9},{2,6},{6,2},{1... | collective-permute-start | bytes 786440 | tf_op jit(solution)/shard_map/ppermute | solution.py:25
  79.4 7.7 %collective-permute-start.14 = (s16[16,65,128]{2,0,1:T(8,128)(2,1)S(1)}, s16[16,65,128]{2,0,1:T(8,128)(2,1)S(1)}, u32[]{:S(2)}, u32[]{:S(2)}) collective-permute-start(s16[16,65,128]{2,0,1:T(8,128)(2,1)S(1)} %get-tuple-element.37), channel_id=1, source_target_pairs={{4,8},{8,4},{5,9},{9,5},{6,10},{10,6},{7,11},{11,7},{20,24},{24,20... | collective-permute-start | bytes 798728 | tf_op jit(solution)/shard_map/ppermute | solution.py:26
  81.3 5.8 %collective-permute-start.15 = (s16[16,65,128]{2,0,1:T(8,128)(2,1)S(1)}, s16[16,65,128]{2,0,1:T(8,128)(2,1)S(1)}, u32[]{:S(2)}, u32[]{:S(2)}) collective-permute-start(s16[16,65,128]{2,0,1:T(8,128)(2,1)S(1)} %get-tuple-element.38), channel_id=1, source_target_pairs={{0,4},{4,0},{8,12},{12,8},{1,5},{5,1},{9,13},{13,9},{2,6},{6,2},{1... | collective-permute-start | bytes 798728 | tf_op jit(solution)/shard_map/ppermute | solution.py:25
  87.9 5.1 %collective-permute-start.16 = (s16[32,17,128]{2,0,1:T(8,128)(2,1)S(1)}, s16[32,17,128]{2,0,1:T(8,128)(2,1)S(1)}, u32[]{:S(2)}, u32[]{:S(2)}) collective-permute-start(s16[32,17,128]{2,0,1:T(8,128)(2,1)S(1)} %get-tuple-element.53), channel_id=1, source_target_pairs={{0,1},{1,0},{2,3},{3,2},{4,5},{5,4},{6,7},{7,6},{8,9},{9,8},{10,11... | collective-permute-start | bytes 417800 | tf_op jit(solution)/shard_map/ppermute | solution.py:25
  87.9 6.9 %collective-permute-start.17 = (s16[32,17,128]{2,0,1:T(8,128)(2,1)S(1)}, s16[32,17,128]{2,0,1:T(8,128)(2,1)S(1)}, u32[]{:S(2)}, u32[]{:S(2)}) collective-permute-start(s16[32,17,128]{2,0,1:T(8,128)(2,1)S(1)} %get-tuple-element.54), channel_id=1, source_target_pairs={{1,2},{2,1},{5,6},{6,5},{9,10},{10,9},{13,14},{14,13},{17,18},{18,... | collective-permute-start | bytes 417800 | tf_op jit(solution)/shard_map/ppermute | solution.py:26
  95.4 6.5 %collective-permute-start.18 = (s16[32,33,128]{2,0,1:T(8,128)(2,1)S(1)}, s16[32,33,128]{2,0,1:T(8,128)(2,1)S(1)}, u32[]{:S(2)}, u32[]{:S(2)}) collective-permute-start(s16[32,33,128]{2,0,1:T(8,128)(2,1)S(1)} %pad_add_fusion.1), channel_id=1, source_target_pairs={{0,16},{16,0},{1,17},{17,1},{2,18},{18,2},{3,19},{19,3},{4,20},{20... | collective-permute-start | bytes 811016 | tf_op jit(solution)/shard_map/ppermute | solution.py:188
  (4 other events, 5.5 us)

commit v9 on v8

--- a/solution.py
+++ b/solution.py
@@ -161,12 +161,13 @@
         out_specs=[VMEM] * 3,
     )(padded)
 
-    joined = estimate
+    chunks = 2 if cells_x % 32 == 0 else 1
+    start = lax.optimization_barrier(start)
+    joined = jnp.split(estimate, chunks, axis=0)
     for step in range(ITERS):
         wide = start
         if step > 0:
-            wide = gather_halo(joined.astype(jnp.bfloat16), "fy", 1, halo)
-            wide = gather_halo(wide, "fx", 0, halo)
+            wide = gather_halo(jnp.concatenate(wides, axis=0), "fx", 0, halo)
         wide = wide.astype(jnp.float32)
         field = jnp.einsum("gox,xyz->goyz", table_x, wide, precision=exact)
         field = jnp.einsum("goy,gxyz->gxoz", table_y, field, precision=exact)
@@ -178,17 +179,32 @@
         late = (psf, cover_lo, cover_len) if step == 0 else ()
         below, above, late = swap_fixed(field[:halo], field[cells_x + halo :], "fx", late)
         if step == 0:
-            lower_part = weight_of(*view_tables(*late, swap), cells_x, cells_y, depth) + 0.5
+            weight = weight_of(*view_tables(*late, swap), cells_x, cells_y, depth)
+            lower_parts = jnp.split(weight + 0.5, chunks, axis=0)
         field = add_edges(field[halo : cells_x + halo], below, above, 0)
-        below, above, _ = swap_fixed(field[:, :halo], field[:, cells_y + halo :], "fy")
-        field = add_edges(field[:, halo : cells_y + halo], below, above, 1)
-        moving = pack_fixed(field)
-        correction = unpack_fixed(moving)
-        for _ in range(groups - 1):
-            moving = lax.ppermute(moving, "view", swap)
-            correction = correction + unpack_fixed(moving)
-        joined = joined * (correction + 0.5) / lower_part
-    return joined
+        own, moves = [], []
+        for chunk in jnp.split(field, chunks, axis=0):
+            low, high = pack_fixed(chunk[:, :halo]), pack_fixed(chunk[:, cells_y + halo :])
+            below, above, _ = swap_edges(low, high, "fy")
+            if own:
+                below, above, _ = lax.optimization_barrier((below, above, own[-1]))
+            chunk = chunk[:, halo : cells_y + halo]
+            own.append(pack_fixed(add_edges(chunk, unpack_fixed(below), unpack_fixed(above), 1)))
+            moves.append([])
+            moving = own[-1]
+            for _ in range(groups - 1):
+                moving = lax.ppermute(moving, "view", swap)
+                moves[-1].append(moving)
+        wides, ready = [], None
+        for at in range(chunks):
+            if ready is not None:
+                moves[at], _ = lax.optimization_barrier((moves[at], ready))
+            correction = sum(map(unpack_fixed, moves[at]), unpack_fixed(own[at]))
+            joined[at] = joined[at] * (correction + 0.5) / lower_parts[at]
+            ready = joined[at].astype(jnp.bfloat16)
+            if step < ITERS - 1:
+                wides.append(gather_halo(ready, "fy", 1, halo))
+    return jnp.concatenate(joined, axis=0)
 
 
 def solution(mesh):

time: 104 us -> 116 us (1.12)
  the two profiles are of different devices: /device:TPU:20 before, /device:TPU:0 now
where the time goes in v9:
time: 116 us
  starting transfers between devices  58.1 us (50%)
  matrix products  22.6 us (19%)
  waiting for transfers between devices  18.6 us (16%)
  local copies, waits for them, and re-layouts  7.08 us (6%)
  other arithmetic  6.54 us (6%)
  Pallas kernels  1.66 us (1%)
    ppermute x11, starting transfers between devices, swap_edges(): first = lax.ppermute(jnp.where(even, to_above, to_below), axis, pairs(0))  44.7 us
    ppermute x4, waiting for transfers between devices, body(): moving = lax.ppermute(moving, 'view', swap)  10.8 us
    ppermute x11, waiting for transfers between devices, swap_edges(): first = lax.ppermute(jnp.where(even, to_above, to_below), axis, pairs(0))  7.73 us
    ppermute x11, starting transfers between devices, swap_edges(): second = lax.ppermute(jnp.where(even, to_below, to_above), axis, pairs(1))  7.7 us
    dot_general x2, matrix products, body(): field = jnp.einsum('gox,goyz->xyz', table_x, field, precision=exact)  5.58 us
    dot_general x2, matrix products, body(): field = jnp.einsum('goy,gxyz->gxoz', table_y, field, precision=exact)  5.48 us
    ppermute x4, starting transfers between devices, body(): moving = lax.ppermute(moving, 'view', swap)  4.25 us
    unnamed x22, local copies, waits for them, and re-layouts  3.63 us
  transfers between devices with their start and end apart: 27, of which 9 were waited for; matrix products, arithmetic and copies ran while one was open for 9% of the time, Pallas kernels for 1%

profile of v9, /device:TPU:0, one launch (start us, length us, event | category | flops | bytes accessed | tf_op | source)
XLA Modules:
  0.0 115.6 jit_solution(17432234295360109641)
XLA Ops:
  1.4 3.1 %collective-permute-start = (bf16[32,16,128]{2,0,1:T(8,128)(2,1)S(1)}, bf16[32,16,128]{2,0,1:T(8,128)(2,1)S(1)}, u32[]{:S(2)}, u32[]{:S(2)}) collective-permute-start(bf16[32,16,128]{2,0,1:T(8,128)(2,1)S(1)} %get-tuple-element.77), channel_id=1, source_target_pairs={{0,1},{1,0},{2,3},{3,2},{4,5},{5,4},{6,7},{7,6},{8,9},{9,8},{10,11... | collective-permute-start | bytes 393224 | tf_op jit(solution)/shard_map/ppermute | solution.py:25
  6.2 1.7 %collective-permute-done = bf16[32,16,128]{2,0,1:T(8,128)(2,1)S(1)} collective-permute-done((bf16[32,16,128]{2,0,1:T(8,128)(2,1)S(1)}, bf16[32,16,128]{2,0,1:T(8,128)(2,1)S(1)}, u32[]{:S(2)}, u32[]{:S(2)}) %collective-permute-start) | collective-permute-done | bytes 131104 | tf_op jit(solution)/shard_map/ppermute | solution.py:25
  8.8 3.1 %collective-permute-start.3 = (bf16[16,64,128]{2,0,1:T(8,128)(2,1)S(1)}, bf16[16,64,128]{2,0,1:T(8,128)(2,1)S(1)}, u32[]{:S(2)}, u32[]{:S(2)}) collective-permute-start(bf16[16,64,128]{2,0,1:T(8,128)(2,1)S(1)} %get-tuple-element.74), channel_id=1, source_target_pairs={{0,4},{4,0},{8,12},{12,8},{1,5},{5,1},{9,13},{13,9},{2,6},{6,2},{1... | collective-permute-start | bytes 786440 | tf_op jit(solution)/shard_map/ppermute | solution.py:25
  12.5 1.7 %shard_map.55 = (f32[3,32,64]{2,1,0:T(8,128)}, f32[3,32,64]{2,1,0:T(8,128)}, f32[3,128,128]{2,1,0:T(8,128)}) custom-call(f32[3,3,128]{2,1,0:T(4,128)} %pad.40.psf), custom_call_target="tpu_custom_call" | custom-call | tf_op jit(solution)/shard_map/pallas_call | solution.py:153
  16.0 2.7 %fusion.7 = f32[3,32,128,32]{2,3,1,0:T(8,128)S(1)} fusion(f32[3,32,64,128]{3,1,2,0:T(8,128)S(1)} %fusion.44, f32[3,32,64]{2,1,0:T(8,128)S(1)} %copy-done.2), kind=kOutput, calls=%fused_computation.7 | convolution fusion | flops 150994944 | bytes 4743168 | tf_op jit(solution)/shard_map/goy,gxyz->gxoz/dot_general | solution.py:173
  20.7 1.4 %convolution_bitcast_fusion.1 = f32[3,32,64,128]{3,2,1,0:T(8,128)S(1)} fusion(f32[3,32,32,128]{3,2,1,0:T(8,128)S(1)} %fusion.17, f32[3,32,64]{2,1,0:T(8,128)S(1)} %copy-done.2), kind=kOutput, calls=%fused_computation.14 | convolution fusion | flops 150994944 | bytes 4743168 | tf_op jit(solution)/shard_map/goy,gxoz->gxyz/dot_general | solution.py:177
  22.2 2.8 %fusion.11 = f32[64,64,128]{2,0,1:T(8,128)S(1)} fusion(f32[3,32,64,128]{3,2,1,0:T(8,128)S(1)} %convolution_bitcast_fusion.1, f32[3,32,64]{2,1,0:T(8,128)S(1)} %copy-done.4), kind=kOutput, calls=%fused_computation.15 | convolution fusion | flops 301989888 | bytes 5267456 | tf_op jit(solution)/shard_map/gox,goyz->xyz/dot_general | solution.py:178
  29.1 1.5 %collective-permute-start.9 = (f32[375]{0:T(512)S(1)}, f32[375]{0:T(512)S(1)}, u32[]{:S(2)}, u32[]{:S(2)}) collective-permute-start(f32[375]{0:T(512)S(1)} %pad_maximum_fusion.5), channel_id=1, source_target_pairs={{0,16},{16,0},{1,17},{17,1},{2,18},{18,2},{3,19},{19,3},{4,20},{20... | collective-permute-start | bytes 4508 | tf_op jit(solution)/shard_map/ppermute | solution.py:124
  31.4 4.7 %collective-permute-start.6 = (s16[16,17,128]{2,0,1:T(8,128)(2,1)S(1)}, s16[16,17,128]{2,0,1:T(8,128)(2,1)S(1)}, u32[]{:S(2)}, u32[]{:S(2)}) collective-permute-start(s16[16,17,128]{2,0,1:T(8,128)(2,1)S(1)} %get-tuple-element.89), channel_id=1, source_target_pairs={{0,1},{1,0},{2,3},{3,2},{4,5},{5,4},{6,7},{7,6},{8,9},{9,8},{10,11... | collective-permute-start | bytes 208904 | tf_op jit(solution)/shard_map/ppermute | solution.py:25
  37.5 4.6 %collective-permute-start.12 = (s16[16,17,128]{2,0,1:T(8,128)(2,1)S(1)}, s16[16,17,128]{2,0,1:T(8,128)(2,1)S(1)}, u32[]{:S(2)}, u32[]{:S(2)}) collective-permute-start(s16[16,17,128]{2,0,1:T(8,128)(2,1)S(1)} %get-tuple-element.94), channel_id=1, source_target_pairs={{0,1},{1,0},{2,3},{3,2},{4,5},{5,4},{6,7},{7,6},{8,9},{9,8},{10,11... | collective-permute-start | bytes 208904 | tf_op jit(solution)/shard_map/ppermute | solution.py:25
  44.6 2.8 %fusion.23 = f32[32,32,128]{2,1,0:T(8,128)S(1)} fusion(f32[32,6,4]{0,1,2:T(8,128)S(1)} %convolution_bitcast_fusion.2, f32[32,6,4]{1,0,2:T(8,128)S(1)} %copy.35, f32[6,4,4,128,1]{3,2,1,0,4:T(4,128)S(1)} %bitcast.144), kind=kOutput, calls=%fused_computation.24 | convolution fusion | flops 151093248 | bytes 579584 | tf_op jit(solution)/shard_map/xym,mz->xyz/dot_general | solution.py:112
  48.9 1.6 %collective-permute-start.14 = (s16[16,33,128]{2,0,1:T(8,128)(2,1)S(1)}, s16[16,33,128]{2,0,1:T(8,128)(2,1)S(1)}, u32[]{:S(2)}, u32[]{:S(2)}) collective-permute-start(s16[16,33,128]{2,0,1:T(8,128)(2,1)S(1)} %pad_add_fusion.5), channel_id=1, source_target_pairs={{0,16},{16,0},{1,17},{17,1},{2,18},{18,2},{3,19},{19,3},{4,20},{20... | collective-permute-start | bytes 405512 | tf_op jit(solution)/shard_map/ppermute | solution.py:196
  50.5 2.6 %collective-permute-done.8 = s16[16,33,128]{2,0,1:T(8,128)(2,1)S(1)} collective-permute-done((s16[16,33,128]{2,0,1:T(8,128)(2,1)S(1)}, s16[16,33,128]{2,0,1:T(8,128)(2,1)S(1)}, u32[]{:S(2)}, u32[]{:S(2)}) %collective-permute-start.8) | collective-permute-done | bytes 135200 | tf_op jit(solution)/shard_map/ppermute | solution.py:196
  55.6 5.0 %collective-permute-start.10 = (bf16[16,16,128]{2,0,1:T(8,128)(2,1)S(1)}, bf16[16,16,128]{2,0,1:T(8,128)(2,1)S(1)}, u32[]{:S(2)}, u32[]{:S(2)}) collective-permute-start(bf16[16,16,128]{2,0,1:T(8,128)(2,1)S(1)} %get-tuple-element.97), channel_id=1, source_target_pairs={{0,1},{1,0},{2,3},{3,2},{4,5},{5,4},{6,7},{7,6},{8,9},{9,8},{10,11... | collective-permute-start | bytes 196616 | tf_op jit(solution)/shard_map/ppermute | solution.py:25
  61.3 1.7 %collective-permute-done.10 = bf16[16,16,128]{2,0,1:T(8,128)(2,1)S(1)} collective-permute-done((bf16[16,16,128]{2,0,1:T(8,128)(2,1)S(1)}, bf16[16,16,128]{2,0,1:T(8,128)(2,1)S(1)}, u32[]{:S(2)}, u32[]{:S(2)}) %collective-permute-start.10) | collective-permute-done | bytes 65568 | tf_op jit(solution)/shard_map/ppermute | solution.py:25
  64.0 8.7 %collective-permute-start.18 = (bf16[16,64,128]{2,0,1:T(8,128)(2,1)S(1)}, bf16[16,64,128]{2,0,1:T(8,128)(2,1)S(1)}, u32[]{:S(2)}, u32[]{:S(2)}) collective-permute-start(bf16[16,64,128]{2,0,1:T(8,128)(2,1)S(1)} %get-tuple-element.70), channel_id=1, source_target_pairs={{0,4},{4,0},{8,12},{12,8},{1,5},{5,1},{9,13},{13,9},{2,6},{6,2},{1... | collective-permute-start | bytes 786440 | tf_op jit(solution)/shard_map/ppermute | solution.py:25
  74.9 2.7 %fusion.3 = f32[3,32,128,32]{2,3,1,0:T(8,128)S(1)} fusion(f32[3,32,64,128]{3,1,2,0:T(8,128)S(1)} %fusion.29, f32[3,32,64]{2,1,0:T(8,128)S(1)} %copy-done.2), kind=kOutput, calls=%fused_computation.3 | convolution fusion | flops 150994944 | bytes 4743168 | tf_op jit(solution)/shard_map/goy,gxyz->gxoz/dot_general | solution.py:173
  81.1 2.8 %fusion.14 = f32[64,64,128]{2,0,1:T(8,128)S(1)} fusion(f32[3,32,64,128]{3,2,1,0:T(8,128)S(1)} %convolution_bitcast_fusion, f32[3,32,64]{2,1,0:T(8,128)S(1)} %copy-done.4), kind=kOutput, calls=%fused_computation.16 | convolution fusion | flops 301989888 | bytes 5267456 | tf_op jit(solution)/shard_map/gox,goyz->xyz/dot_general | solution.py:178
  85.0 5.6 %collective-permute-start.20 = (s16[16,65,128]{2,0,1:T(8,128)(2,1)S(1)}, s16[16,65,128]{2,0,1:T(8,128)(2,1)S(1)}, u32[]{:S(2)}, u32[]{:S(2)}) collective-permute-start(s16[16,65,128]{2,0,1:T(8,128)(2,1)S(1)} %get-tuple-element.60), channel_id=1, source_target_pairs={{0,4},{4,0},{8,12},{12,8},{1,5},{5,1},{9,13},{13,9},{2,6},{6,2},{1... | collective-permute-start | bytes 798728 | tf_op jit(solution)/shard_map/ppermute | solution.py:25
  92.6 4.0 %collective-permute-start.21 = (s16[16,17,128]{2,0,1:T(8,128)(2,1)S(1)}, s16[16,17,128]{2,0,1:T(8,128)(2,1)S(1)}, u32[]{:S(2)}, u32[]{:S(2)}) collective-permute-start(s16[16,17,128]{2,0,1:T(8,128)(2,1)S(1)} %get-tuple-element.81), channel_id=1, source_target_pairs={{0,1},{1,0},{2,3},{3,2},{4,5},{5,4},{6,7},{7,6},{8,9},{9,8},{10,11... | collective-permute-start | bytes 208904 | tf_op jit(solution)/shard_map/ppermute | solution.py:25
  97.9 4.6 %collective-permute-start.24 = (s16[16,17,128]{2,0,1:T(8,128)(2,1)S(1)}, s16[16,17,128]{2,0,1:T(8,128)(2,1)S(1)}, u32[]{:S(2)}, u32[]{:S(2)}) collective-permute-start(s16[16,17,128]{2,0,1:T(8,128)(2,1)S(1)} %get-tuple-element.86), channel_id=1, source_target_pairs={{0,1},{1,0},{2,3},{3,2},{4,5},{5,4},{6,7},{7,6},{8,9},{9,8},{10,11... | collective-permute-start | bytes 208904 | tf_op jit(solution)/shard_map/ppermute | solution.py:25
  102.9 2.0 %collective-permute-done.24 = s16[16,17,128]{2,0,1:T(8,128)(2,1)S(1)} collective-permute-done((s16[16,17,128]{2,0,1:T(8,128)(2,1)S(1)}, s16[16,17,128]{2,0,1:T(8,128)(2,1)S(1)}, u32[]{:S(2)}, u32[]{:S(2)}) %collective-permute-start.24) | collective-permute-done | bytes 69664 | tf_op jit(solution)/shard_map/ppermute | solution.py:25
  107.2 4.0 %collective-permute-done.26 = s16[16,33,128]{2,0,1:T(8,128)(2,1)S(1)} collective-permute-done((s16[16,33,128]{2,0,1:T(8,128)(2,1)S(1)}, s16[16,33,128]{2,0,1:T(8,128)(2,1)S(1)}, u32[]{:S(2)}, u32[]{:S(2)}) %collective-permute-start.26) | collective-permute-done | bytes 135200 | tf_op jit(solution)/shard_map/ppermute | solution.py:196
  111.3 2.9 %collective-permute-done.23 = s16[16,33,128]{2,0,1:T(8,128)(2,1)S(1)} collective-permute-done((s16[16,33,128]{2,0,1:T(8,128)(2,1)S(1)}, s16[16,33,128]{2,0,1:T(8,128)(2,1)S(1)}, u32[]{:S(2)}, u32[]{:S(2)}) %collective-permute-start.23) | collective-permute-done | bytes 135200 | tf_op jit(solution)/shard_map/ppermute | solution.py:196
  (193 shorter events, 36.3 us)
Async XLA Ops:
  1.4 6.6 %collective-permute-start = (bf16[32,16,128]{2,0,1:T(8,128)(2,1)S(1)}, bf16[32,16,128]{2,0,1:T(8,128)(2,1)S(1)}, u32[]{:S(2)}, u32[]{:S(2)}) collective-permute-start(bf16[32,16,128]{2,0,1:T(8,128)(2,1)S(1)} %get-tuple-element.77), channel_id=1, source_target_pairs={{0,1},{1,0},{2,3},{3,2},{4,5},{5,4},{6,7},{7,6},{8,9},{9,8},{10,11... | collective-permute-start | bytes 393224 | tf_op jit(solution)/shard_map/ppermute | solution.py:25
  4.5 3.5 %collective-permute-start.1 = (bf16[32,16,128]{2,0,1:T(8,128)(2,1)S(1)}, bf16[32,16,128]{2,0,1:T(8,128)(2,1)S(1)}, u32[]{:S(2)}, u32[]{:S(2)}) collective-permute-start(bf16[32,16,128]{2,0,1:T(8,128)(2,1)S(1)} %get-tuple-element.78), channel_id=1, source_target_pairs={{1,2},{2,1},{5,6},{6,5},{9,10},{10,9},{13,14},{14,13},{17,18},{18,... | collective-permute-start | bytes 393224 | tf_op jit(solution)/shard_map/ppermute | solution.py:26
  8.1 6.1 %collective-permute-start.2 = (bf16[16,64,128]{2,0,1:T(8,128)(2,1)S(1)}, bf16[16,64,128]{2,0,1:T(8,128)(2,1)S(1)}, u32[]{:S(2)}, u32[]{:S(2)}) collective-permute-start(bf16[16,64,128]{2,0,1:T(8,128)(2,1)S(1)} %get-tuple-element.73), channel_id=1, source_target_pairs={{4,8},{8,4},{5,9},{9,5},{6,10},{10,6},{7,11},{11,7},{20,24},{24,20... | collective-permute-start | bytes 786440 | tf_op jit(solution)/shard_map/ppermute | solution.py:26
  8.8 5.4 %collective-permute-start.3 = (bf16[16,64,128]{2,0,1:T(8,128)(2,1)S(1)}, bf16[16,64,128]{2,0,1:T(8,128)(2,1)S(1)}, u32[]{:S(2)}, u32[]{:S(2)}) collective-permute-start(bf16[16,64,128]{2,0,1:T(8,128)(2,1)S(1)} %get-tuple-element.74), channel_id=1, source_target_pairs={{0,4},{4,0},{8,12},{12,8},{1,5},{5,1},{9,13},{13,9},{2,6},{6,2},{1... | collective-permute-start | bytes 786440 | tf_op jit(solution)/shard_map/ppermute | solution.py:25
  29.1 12.9 %collective-permute-start.9 = (f32[375]{0:T(512)S(1)}, f32[375]{0:T(512)S(1)}, u32[]{:S(2)}, u32[]{:S(2)}) collective-permute-start(f32[375]{0:T(512)S(1)} %pad_maximum_fusion.5), channel_id=1, source_target_pairs={{0,16},{16,0},{1,17},{17,1},{2,18},{18,2},{3,19},{19,3},{4,20},{20... | collective-permute-start | bytes 4508 | tf_op jit(solution)/shard_map/ppermute | solution.py:124
  31.4 16.3 %collective-permute-start.6 = (s16[16,17,128]{2,0,1:T(8,128)(2,1)S(1)}, s16[16,17,128]{2,0,1:T(8,128)(2,1)S(1)}, u32[]{:S(2)}, u32[]{:S(2)}) collective-permute-start(s16[16,17,128]{2,0,1:T(8,128)(2,1)S(1)} %get-tuple-element.89), channel_id=1, source_target_pairs={{0,1},{1,0},{2,3},{3,2},{4,5},{5,4},{6,7},{7,6},{8,9},{9,8},{10,11... | collective-permute-start | bytes 208904 | tf_op jit(solution)/shard_map/ppermute | solution.py:25
  36.1 11.7 %collective-permute-start.7 = (s16[16,17,128]{2,0,1:T(8,128)(2,1)S(1)}, s16[16,17,128]{2,0,1:T(8,128)(2,1)S(1)}, u32[]{:S(2)}, u32[]{:S(2)}) collective-permute-start(s16[16,17,128]{2,0,1:T(8,128)(2,1)S(1)} %get-tuple-element.90), channel_id=1, source_target_pairs={{1,2},{2,1},{5,6},{6,5},{9,10},{10,9},{13,14},{14,13},{17,18},{18,... | collective-permute-start | bytes 208904 | tf_op jit(solution)/shard_map/ppermute | solution.py:26
  36.8 11.9 %collective-permute-start.13 = (s16[16,17,128]{2,0,1:T(8,128)(2,1)S(1)}, s16[16,17,128]{2,0,1:T(8,128)(2,1)S(1)}, u32[]{:S(2)}, u32[]{:S(2)}) collective-permute-start(s16[16,17,128]{2,0,1:T(8,128)(2,1)S(1)} %get-tuple-element.93), channel_id=1, source_target_pairs={{1,2},{2,1},{5,6},{6,5},{9,10},{10,9},{13,14},{14,13},{17,18},{18,... | collective-permute-start | bytes 208904 | tf_op jit(solution)/shard_map/ppermute | solution.py:26
  37.5 11.2 %collective-permute-start.12 = (s16[16,17,128]{2,0,1:T(8,128)(2,1)S(1)}, s16[16,17,128]{2,0,1:T(8,128)(2,1)S(1)}, u32[]{:S(2)}, u32[]{:S(2)}) collective-permute-start(s16[16,17,128]{2,0,1:T(8,128)(2,1)S(1)} %get-tuple-element.94), channel_id=1, source_target_pairs={{0,1},{1,0},{2,3},{3,2},{4,5},{5,4},{6,7},{7,6},{8,9},{9,8},{10,11... | collective-permute-start | bytes 208904 | tf_op jit(solution)/shard_map/ppermute | solution.py:25
  48.1 5.1 %collective-permute-start.8 = (s16[16,33,128]{2,0,1:T(8,128)(2,1)S(1)}, s16[16,33,128]{2,0,1:T(8,128)(2,1)S(1)}, u32[]{:S(2)}, u32[]{:S(2)}) collective-permute-start(s16[16,33,128]{2,0,1:T(8,128)(2,1)S(1)} %pad_add_fusion.4), channel_id=1, source_target_pairs={{0,16},{16,0},{1,17},{17,1},{2,18},{18,2},{3,19},{19,3},{4,20},{20... | collective-permute-start | bytes 405512 | tf_op jit(solution)/shard_map/ppermute | solution.py:196
  48.9 5.6 %collective-permute-start.14 = (s16[16,33,128]{2,0,1:T(8,128)(2,1)S(1)}, s16[16,33,128]{2,0,1:T(8,128)(2,1)S(1)}, u32[]{:S(2)}, u32[]{:S(2)}) collective-permute-start(s16[16,33,128]{2,0,1:T(8,128)(2,1)S(1)} %pad_add_fusion.5), channel_id=1, source_target_pairs={{0,16},{16,0},{1,17},{17,1},{2,18},{18,2},{3,19},{19,3},{4,20},{20... | collective-permute-start | bytes 405512 | tf_op jit(solution)/shard_map/ppermute | solution.py:196
  54.8 6.5 %collective-permute-start.15 = (bf16[16,16,128]{2,0,1:T(8,128)(2,1)S(1)}, bf16[16,16,128]{2,0,1:T(8,128)(2,1)S(1)}, u32[]{:S(2)}, u32[]{:S(2)}) collective-permute-start(bf16[16,16,128]{2,0,1:T(8,128)(2,1)S(1)} %get-tuple-element.101), channel_id=1, source_target_pairs={{0,1},{1,0},{2,3},{3,2},{4,5},{5,4},{6,7},{7,6},{8,9},{9,8},{10,11... | collective-permute-start | bytes 196616 | tf_op jit(solution)/shard_map/ppermute | solution.py:25
  54.9 6.4 %collective-permute-start.16 = (bf16[16,16,128]{2,0,1:T(8,128)(2,1)S(1)}, bf16[16,16,128]{2,0,1:T(8,128)(2,1)S(1)}, u32[]{:S(2)}, u32[]{:S(2)}) collective-permute-start(bf16[16,16,128]{2,0,1:T(8,128)(2,1)S(1)} %get-tuple-element.102), channel_id=1, source_target_pairs={{1,2},{2,1},{5,6},{6,5},{9,10},{10,9},{13,14},{14,13},{17,18},{18,... | collective-permute-start | bytes 196616 | tf_op jit(solution)/shard_map/ppermute | solution.py:26
  55.6 7.4 %collective-permute-start.10 = (bf16[16,16,128]{2,0,1:T(8,128)(2,1)S(1)}, bf16[16,16,128]{2,0,1:T(8,128)(2,1)S(1)}, u32[]{:S(2)}, u32[]{:S(2)}) collective-permute-start(bf16[16,16,128]{2,0,1:T(8,128)(2,1)S(1)} %get-tuple-element.97), channel_id=1, source_target_pairs={{0,1},{1,0},{2,3},{3,2},{4,5},{5,4},{6,7},{7,6},{8,9},{9,8},{10,11... | collective-permute-start | bytes 196616 | tf_op jit(solution)/shard_map/ppermute | solution.py:25
  63.1 9.6 %collective-permute-start.17 = (bf16[16,64,128]{2,0,1:T(8,128)(2,1)S(1)}, bf16[16,64,128]{2,0,1:T(8,128)(2,1)S(1)}, u32[]{:S(2)}, u32[]{:S(2)}) collective-permute-start(bf16[16,64,128]{2,0,1:T(8,128)(2,1)S(1)} %get-tuple-element.69), channel_id=1, source_target_pairs={{4,8},{8,4},{5,9},{9,5},{6,10},{10,6},{7,11},{11,7},{20,24},{24,20... | collective-permute-start | bytes 786440 | tf_op jit(solution)/shard_map/ppermute | solution.py:26
  64.0 9.9 %collective-permute-start.18 = (bf16[16,64,128]{2,0,1:T(8,128)(2,1)S(1)}, bf16[16,64,128]{2,0,1:T(8,128)(2,1)S(1)}, u32[]{:S(2)}, u32[]{:S(2)}) collective-permute-start(bf16[16,64,128]{2,0,1:T(8,128)(2,1)S(1)} %get-tuple-element.70), channel_id=1, source_target_pairs={{0,4},{4,0},{8,12},{12,8},{1,5},{5,1},{9,13},{13,9},{2,6},{6,2},{1... | collective-permute-start | bytes 786440 | tf_op jit(solution)/shard_map/ppermute | solution.py:25
  84.3 6.3 %collective-permute-start.19 = (s16[16,65,128]{2,0,1:T(8,128)(2,1)S(1)}, s16[16,65,128]{2,0,1:T(8,128)(2,1)S(1)}, u32[]{:S(2)}, u32[]{:S(2)}) collective-permute-start(s16[16,65,128]{2,0,1:T(8,128)(2,1)S(1)} %get-tuple-element.59), channel_id=1, source_target_pairs={{4,8},{8,4},{5,9},{9,5},{6,10},{10,6},{7,11},{11,7},{20,24},{24,20... | collective-permute-start | bytes 798728 | tf_op jit(solution)/shard_map/ppermute | solution.py:26
  85.0 6.8 %collective-permute-start.20 = (s16[16,65,128]{2,0,1:T(8,128)(2,1)S(1)}, s16[16,65,128]{2,0,1:T(8,128)(2,1)S(1)}, u32[]{:S(2)}, u32[]{:S(2)}) collective-permute-start(s16[16,65,128]{2,0,1:T(8,128)(2,1)S(1)} %get-tuple-element.60), channel_id=1, source_target_pairs={{0,4},{4,0},{8,12},{12,8},{1,5},{5,1},{9,13},{13,9},{2,6},{6,2},{1... | collective-permute-start | bytes 798728 | tf_op jit(solution)/shard_map/ppermute | solution.py:25
  92.6 10.0 %collective-permute-start.21 = (s16[16,17,128]{2,0,1:T(8,128)(2,1)S(1)}, s16[16,17,128]{2,0,1:T(8,128)(2,1)S(1)}, u32[]{:S(2)}, u32[]{:S(2)}) collective-permute-start(s16[16,17,128]{2,0,1:T(8,128)(2,1)S(1)} %get-tuple-element.81), channel_id=1, source_target_pairs={{0,1},{1,0},{2,3},{3,2},{4,5},{5,4},{6,7},{7,6},{8,9},{9,8},{10,11... | collective-permute-start | bytes 208904 | tf_op jit(solution)/shard_map/ppermute | solution.py:25
  96.6 6.0 %collective-permute-start.22 = (s16[16,17,128]{2,0,1:T(8,128)(2,1)S(1)}, s16[16,17,128]{2,0,1:T(8,128)(2,1)S(1)}, u32[]{:S(2)}, u32[]{:S(2)}) collective-permute-start(s16[16,17,128]{2,0,1:T(8,128)(2,1)S(1)} %get-tuple-element.82), channel_id=1, source_target_pairs={{1,2},{2,1},{5,6},{6,5},{9,10},{10,9},{13,14},{14,13},{17,18},{18,... | collective-permute-start | bytes 208904 | tf_op jit(solution)/shard_map/ppermute | solution.py:26
  97.3 5.6 %collective-permute-start.25 = (s16[16,17,128]{2,0,1:T(8,128)(2,1)S(1)}, s16[16,17,128]{2,0,1:T(8,128)(2,1)S(1)}, u32[]{:S(2)}, u32[]{:S(2)}) collective-permute-start(s16[16,17,128]{2,0,1:T(8,128)(2,1)S(1)} %get-tuple-element.85), channel_id=1, source_target_pairs={{1,2},{2,1},{5,6},{6,5},{9,10},{10,9},{13,14},{14,13},{17,18},{18,... | collective-permute-start | bytes 208904 | tf_op jit(solution)/shard_map/ppermute | solution.py:26
  97.9 6.9 %collective-permute-start.24 = (s16[16,17,128]{2,0,1:T(8,128)(2,1)S(1)}, s16[16,17,128]{2,0,1:T(8,128)(2,1)S(1)}, u32[]{:S(2)}, u32[]{:S(2)}) collective-permute-start(s16[16,17,128]{2,0,1:T(8,128)(2,1)S(1)} %get-tuple-element.86), channel_id=1, source_target_pairs={{0,1},{1,0},{2,3},{3,2},{4,5},{5,4},{6,7},{7,6},{8,9},{9,8},{10,11... | collective-permute-start | bytes 208904 | tf_op jit(solution)/shard_map/ppermute | solution.py:25
  105.1 6.1 %collective-permute-start.26 = (s16[16,33,128]{2,0,1:T(8,128)(2,1)S(1)}, s16[16,33,128]{2,0,1:T(8,128)(2,1)S(1)}, u32[]{:S(2)}, u32[]{:S(2)}) collective-permute-start(s16[16,33,128]{2,0,1:T(8,128)(2,1)S(1)} %pad_add_fusion.7), channel_id=1, source_target_pairs={{0,16},{16,0},{1,17},{17,1},{2,18},{18,2},{3,19},{19,3},{4,20},{20... | collective-permute-start | bytes 405512 | tf_op jit(solution)/shard_map/ppermute | solution.py:196
  106.3 7.9 %collective-permute-start.23 = (s16[16,33,128]{2,0,1:T(8,128)(2,1)S(1)}, s16[16,33,128]{2,0,1:T(8,128)(2,1)S(1)}, u32[]{:S(2)}, u32[]{:S(2)}) collective-permute-start(s16[16,33,128]{2,0,1:T(8,128)(2,1)S(1)} %pad_add_fusion.6), channel_id=1, source_target_pairs={{0,16},{16,0},{1,17},{17,1},{2,18},{18,2},{3,19},{19,3},{4,20},{20... | collective-permute-start | bytes 405512 | tf_op jit(solution)/shard_map/ppermute | solution.py:196
  (13 other events, 41.8 us)

commit v10 on v8

--- a/solution.py
+++ b/solution.py
@@ -161,6 +161,7 @@
         out_specs=[VMEM] * 3,
     )(padded)
 
+    start = lax.optimization_barrier(start)
     joined = estimate
     for step in range(ITERS):
         wide = start

time: 104 us -> 104 us (level)
  no operation moved by 1% of the time
where the time goes in v10:
time: 104 us; the launch traced here: 103 us
  waiting for transfers between devices  44.3 us (43%)
  matrix products  22.6 us (22%)
  starting transfers between devices  21.4 us (21%)
  other arithmetic  6.82 us (7%)
  local copies, waits for them, and re-layouts  5.44 us (5%)
  Pallas kernels  1.66 us (2%)
    ppermute x8, waiting for transfers between devices, swap_edges(): second = lax.ppermute(jnp.where(even, to_below, to_above), axis, pairs(1))  28.6 us
    ppermute x8, starting transfers between devices, swap_edges(): second = lax.ppermute(jnp.where(even, to_below, to_above), axis, pairs(1))  16.6 us
    ppermute x2, waiting for transfers between devices, body(): moving = lax.ppermute(moving, 'view', swap)  8.65 us
    ppermute x8, waiting for transfers between devices, swap_edges(): first = lax.ppermute(jnp.where(even, to_above, to_below), axis, pairs(0))  6.98 us
    dot_general x2, matrix products, body(): field = jnp.einsum('gox,goyz->xyz', table_x, field, precision=exact)  5.58 us
    dot_general x2, matrix products, body(): field = jnp.einsum('goy,gxyz->gxoz', table_y, field, precision=exact)  5.48 us
    dot_general x2, matrix products, body(): field = jnp.einsum('goy,gxoz->gxyz', table_y, field, precision=exact)  2.88 us
    dot_general x1, matrix products, weight_of(): jnp.einsum('xym,mz->xyz', plane, sums_z.reshape(-1, depth), precision=lax...  2.78 us
  transfers between devices with their start and end apart: 19, of which 14 were waited for; matrix products, arithmetic and copies ran while one was open for 8% of the time, Pallas kernels for 2%

profile of v10, /device:TPU:20, one launch (start us, length us, event | category | flops | bytes accessed | tf_op | source)
XLA Modules:
  0.0 103.1 jit_solution(5444728290584108621)
XLA Ops:
  3.0 1.9 %collective-permute-start.1 = (bf16[32,16,128]{2,0,1:T(8,128)(2,1)S(1)}, bf16[32,16,128]{2,0,1:T(8,128)(2,1)S(1)}, u32[]{:S(2)}, u32[]{:S(2)}) collective-permute-start(bf16[32,16,128]{2,0,1:T(8,128)(2,1)S(1)} %get-tuple-element.66), channel_id=1, source_target_pairs={{1,2},{2,1},{5,6},{6,5},{9,10},{10,9},{13,14},{14,13},{17,18},{18,... | collective-permute-start | bytes 393224 | tf_op jit(solution)/shard_map/ppermute | solution.py:26
  6.7 3.2 %collective-permute-done.1 = bf16[32,16,128]{2,0,1:T(8,128)(2,1)S(1)} collective-permute-done((bf16[32,16,128]{2,0,1:T(8,128)(2,1)S(1)}, bf16[32,16,128]{2,0,1:T(8,128)(2,1)S(1)}, u32[]{:S(2)}, u32[]{:S(2)}) %collective-permute-start.1) | collective-permute-done | bytes 131104 | tf_op jit(solution)/shard_map/ppermute | solution.py:26
  10.0 1.9 %collective-permute-start.2 = (bf16[16,64,128]{2,0,1:T(8,128)(2,1)S(1)}, bf16[16,64,128]{2,0,1:T(8,128)(2,1)S(1)}, u32[]{:S(2)}, u32[]{:S(2)}) collective-permute-start(bf16[16,64,128]{2,0,1:T(8,128)(2,1)S(1)} %get-tuple-element.49), channel_id=1, source_target_pairs={{4,8},{8,4},{5,9},{9,5},{6,10},{10,6},{7,11},{11,7},{20,24},{24,20... | collective-permute-start | bytes 786440 | tf_op jit(solution)/shard_map/ppermute | solution.py:26
  14.4 3.3 %collective-permute-done.2 = bf16[16,64,128]{2,0,1:T(8,128)(2,1)S(1)} collective-permute-done((bf16[16,64,128]{2,0,1:T(8,128)(2,1)S(1)}, bf16[16,64,128]{2,0,1:T(8,128)(2,1)S(1)}, u32[]{:S(2)}, u32[]{:S(2)}) %collective-permute-start.2) | collective-permute-done | bytes 262176 | tf_op jit(solution)/shard_map/ppermute | solution.py:26
  18.9 2.7 %fusion.7 = f32[3,32,128,32]{2,3,1,0:T(8,128)S(1)} fusion(f32[3,32,64,128]{3,1,2,0:T(8,128)S(1)} %fusion.38, f32[3,32,64]{2,1,0:T(8,128)S(1)} %copy-done.1), kind=kOutput, calls=%fused_computation.7 | convolution fusion | flops 150994944 | bytes 4743168 | tf_op jit(solution)/shard_map/goy,gxyz->gxoz/dot_general | solution.py:173
  25.1 2.8 %fusion.11 = f32[64,64,128]{2,0,1:T(8,128)S(1)} fusion(f32[3,32,64,128]{3,2,1,0:T(8,128)S(1)} %convolution_bitcast_fusion.1, f32[3,32,64]{2,1,0:T(8,128)S(1)} %copy-done.3), kind=kOutput, calls=%fused_computation.15 | convolution fusion | flops 301989888 | bytes 5267456 | tf_op jit(solution)/shard_map/gox,goyz->xyz/dot_general | solution.py:178
  28.5 2.1 %collective-permute-start.4 = (s16[16,65,128]{2,0,1:T(8,128)(2,1)S(1)}, s16[16,65,128]{2,0,1:T(8,128)(2,1)S(1)}, u32[]{:S(2)}, u32[]{:S(2)}) collective-permute-start(s16[16,65,128]{2,0,1:T(8,128)(2,1)S(1)} %get-tuple-element.41), channel_id=1, source_target_pairs={{4,8},{8,4},{5,9},{9,5},{6,10},{10,6},{7,11},{11,7},{20,24},{24,20... | collective-permute-start | bytes 798728 | tf_op jit(solution)/shard_map/ppermute | solution.py:26
  31.0 5.2 %collective-permute-done.4 = s16[16,65,128]{2,0,1:T(8,128)(2,1)S(1)} collective-permute-done((s16[16,65,128]{2,0,1:T(8,128)(2,1)S(1)}, s16[16,65,128]{2,0,1:T(8,128)(2,1)S(1)}, u32[]{:S(2)}, u32[]{:S(2)}) %collective-permute-start.4) | collective-permute-done | bytes 266272 | tf_op jit(solution)/shard_map/ppermute | solution.py:26
  38.7 2.2 %collective-permute-start.7 = (s16[32,17,128]{2,0,1:T(8,128)(2,1)S(1)}, s16[32,17,128]{2,0,1:T(8,128)(2,1)S(1)}, u32[]{:S(2)}, u32[]{:S(2)}) collective-permute-start(s16[32,17,128]{2,0,1:T(8,128)(2,1)S(1)} %get-tuple-element.58), channel_id=1, source_target_pairs={{1,2},{2,1},{5,6},{6,5},{9,10},{10,9},{13,14},{14,13},{17,18},{18,... | collective-permute-start | bytes 417800 | tf_op jit(solution)/shard_map/ppermute | solution.py:26
  43.7 1.9 %collective-permute-done.7 = s16[32,17,128]{2,0,1:T(8,128)(2,1)S(1)} collective-permute-done((s16[32,17,128]{2,0,1:T(8,128)(2,1)S(1)}, s16[32,17,128]{2,0,1:T(8,128)(2,1)S(1)}, u32[]{:S(2)}, u32[]{:S(2)}) %collective-permute-start.7) | collective-permute-done | bytes 139296 | tf_op jit(solution)/shard_map/ppermute | solution.py:26
  47.1 2.8 %fusion.23 = f32[32,32,128]{2,1,0:T(8,128)S(1)} fusion(f32[32,6,4]{0,1,2:T(8,128)S(1)} %convolution_bitcast_fusion.2, f32[32,6,4]{1,0,2:T(8,128)S(1)} %copy.32, f32[6,4,4,128,1]{3,2,1,0,4:T(4,128)S(1)} %bitcast.120), kind=kOutput, calls=%fused_computation.24 | convolution fusion | flops 151093248 | bytes 579584 | tf_op jit(solution)/shard_map/xym,mz->xyz/dot_general | solution.py:112
  49.9 2.7 %collective-permute-done.8 = s16[32,33,128]{2,0,1:T(8,128)(2,1)S(1)} collective-permute-done((s16[32,33,128]{2,0,1:T(8,128)(2,1)S(1)}, s16[32,33,128]{2,0,1:T(8,128)(2,1)S(1)}, u32[]{:S(2)}, u32[]{:S(2)}) %collective-permute-start.8) | collective-permute-done | bytes 270368 | tf_op jit(solution)/shard_map/ppermute | solution.py:189
  53.5 2.2 %collective-permute-start.11 = (bf16[32,16,128]{2,0,1:T(8,128)(2,1)S(1)}, bf16[32,16,128]{2,0,1:T(8,128)(2,1)S(1)}, u32[]{:S(2)}, u32[]{:S(2)}) collective-permute-start(bf16[32,16,128]{2,0,1:T(8,128)(2,1)S(1)} %get-tuple-element.62), channel_id=1, source_target_pairs={{1,2},{2,1},{5,6},{6,5},{9,10},{10,9},{13,14},{14,13},{17,18},{18,... | collective-permute-start | bytes 393224 | tf_op jit(solution)/shard_map/ppermute | solution.py:26
  55.7 2.7 %collective-permute-done.10 = bf16[32,16,128]{2,0,1:T(8,128)(2,1)S(1)} collective-permute-done((bf16[32,16,128]{2,0,1:T(8,128)(2,1)S(1)}, bf16[32,16,128]{2,0,1:T(8,128)(2,1)S(1)}, u32[]{:S(2)}, u32[]{:S(2)}) %collective-permute-start.10) | collective-permute-done | bytes 131104 | tf_op jit(solution)/shard_map/ppermute | solution.py:25
  58.4 1.9 %collective-permute-done.11 = bf16[32,16,128]{2,0,1:T(8,128)(2,1)S(1)} collective-permute-done((bf16[32,16,128]{2,0,1:T(8,128)(2,1)S(1)}, bf16[32,16,128]{2,0,1:T(8,128)(2,1)S(1)}, u32[]{:S(2)}, u32[]{:S(2)}) %collective-permute-start.11) | collective-permute-done | bytes 131104 | tf_op jit(solution)/shard_map/ppermute | solution.py:26
  60.5 2.1 %collective-permute-start.12 = (bf16[16,64,128]{2,0,1:T(8,128)(2,1)S(1)}, bf16[16,64,128]{2,0,1:T(8,128)(2,1)S(1)}, u32[]{:S(2)}, u32[]{:S(2)}) collective-permute-start(bf16[16,64,128]{2,0,1:T(8,128)(2,1)S(1)} %get-tuple-element.45), channel_id=1, source_target_pairs={{4,8},{8,4},{5,9},{9,5},{6,10},{10,6},{7,11},{11,7},{20,24},{24,20... | collective-permute-start | bytes 786440 | tf_op jit(solution)/shard_map/ppermute | solution.py:26
  62.7 5.5 %collective-permute-done.12 = bf16[16,64,128]{2,0,1:T(8,128)(2,1)S(1)} collective-permute-done((bf16[16,64,128]{2,0,1:T(8,128)(2,1)S(1)}, bf16[16,64,128]{2,0,1:T(8,128)(2,1)S(1)}, u32[]{:S(2)}, u32[]{:S(2)}) %collective-permute-start.12) | collective-permute-done | bytes 262176 | tf_op jit(solution)/shard_map/ppermute | solution.py:26
  69.2 2.7 %fusion.3 = f32[3,32,128,32]{2,3,1,0:T(8,128)S(1)} fusion(f32[3,32,64,128]{3,1,2,0:T(8,128)S(1)} %fusion.29, f32[3,32,64]{2,1,0:T(8,128)S(1)} %copy-done.1), kind=kOutput, calls=%fused_computation.3 | convolution fusion | flops 150994944 | bytes 4743168 | tf_op jit(solution)/shard_map/goy,gxyz->gxoz/dot_general | solution.py:173
  75.4 2.8 %fusion.14 = f32[64,64,128]{2,0,1:T(8,128)S(1)} fusion(f32[3,32,64,128]{3,2,1,0:T(8,128)S(1)} %convolution_bitcast_fusion, f32[3,32,64]{2,1,0:T(8,128)S(1)} %copy-done.3), kind=kOutput, calls=%fused_computation.16 | convolution fusion | flops 301989888 | bytes 5267456 | tf_op jit(solution)/shard_map/gox,goyz->xyz/dot_general | solution.py:178
  78.6 1.9 %collective-permute-start.14 = (s16[16,65,128]{2,0,1:T(8,128)(2,1)S(1)}, s16[16,65,128]{2,0,1:T(8,128)(2,1)S(1)}, u32[]{:S(2)}, u32[]{:S(2)}) collective-permute-start(s16[16,65,128]{2,0,1:T(8,128)(2,1)S(1)} %get-tuple-element.37), channel_id=1, source_target_pairs={{4,8},{8,4},{5,9},{9,5},{6,10},{10,6},{7,11},{11,7},{20,24},{24,20... | collective-permute-start | bytes 798728 | tf_op jit(solution)/shard_map/ppermute | solution.py:26
  80.7 5.7 %collective-permute-done.14 = s16[16,65,128]{2,0,1:T(8,128)(2,1)S(1)} collective-permute-done((s16[16,65,128]{2,0,1:T(8,128)(2,1)S(1)}, s16[16,65,128]{2,0,1:T(8,128)(2,1)S(1)}, u32[]{:S(2)}, u32[]{:S(2)}) %collective-permute-start.14) | collective-permute-done | bytes 266272 | tf_op jit(solution)/shard_map/ppermute | solution.py:26
  87.2 2.2 %collective-permute-start.17 = (s16[32,17,128]{2,0,1:T(8,128)(2,1)S(1)}, s16[32,17,128]{2,0,1:T(8,128)(2,1)S(1)}, u32[]{:S(2)}, u32[]{:S(2)}) collective-permute-start(s16[32,17,128]{2,0,1:T(8,128)(2,1)S(1)} %get-tuple-element.54), channel_id=1, source_target_pairs={{1,2},{2,1},{5,6},{6,5},{9,10},{10,9},{13,14},{14,13},{17,18},{18,... | collective-permute-start | bytes 417800 | tf_op jit(solution)/shard_map/ppermute | solution.py:26
  89.4 2.8 %collective-permute-done.16 = s16[32,17,128]{2,0,1:T(8,128)(2,1)S(1)} collective-permute-done((s16[32,17,128]{2,0,1:T(8,128)(2,1)S(1)}, s16[32,17,128]{2,0,1:T(8,128)(2,1)S(1)}, u32[]{:S(2)}, u32[]{:S(2)}) %collective-permute-start.16) | collective-permute-done | bytes 139296 | tf_op jit(solution)/shard_map/ppermute | solution.py:25
  95.2 5.9 %collective-permute-done.18 = s16[32,33,128]{2,0,1:T(8,128)(2,1)S(1)} collective-permute-done((s16[32,33,128]{2,0,1:T(8,128)(2,1)S(1)}, s16[32,33,128]{2,0,1:T(8,128)(2,1)S(1)}, u32[]{:S(2)}, u32[]{:S(2)}) %collective-permute-start.18) | collective-permute-done | bytes 270368 | tf_op jit(solution)/shard_map/ppermute | solution.py:189
  (144 shorter events, 30.9 us)
Async XLA Ops:
  0.0 12.1 %copy-start.6 = (f32[3,3,31]{2,1,0:T(4,128)S(1)}, f32[3,3,31]{2,1,0:T(4,128)}, u32[]{:S(2)}) copy-start(f32[3,3,31]{2,1,0:T(4,128)} %param.7) | copy-start | bytes 3352
  1.4 5.3 %collective-permute-start = (bf16[32,16,128]{2,0,1:T(8,128)(2,1)S(1)}, bf16[32,16,128]{2,0,1:T(8,128)(2,1)S(1)}, u32[]{:S(2)}, u32[]{:S(2)}) collective-permute-start(bf16[32,16,128]{2,0,1:T(8,128)(2,1)S(1)} %get-tuple-element.65), channel_id=1, source_target_pairs={{0,1},{1,0},{2,3},{3,2},{4,5},{5,4},{6,7},{7,6},{8,9},{9,8},{10,11... | collective-permute-start | bytes 393224 | tf_op jit(solution)/shard_map/ppermute | solution.py:25
  3.0 6.8 %collective-permute-start.1 = (bf16[32,16,128]{2,0,1:T(8,128)(2,1)S(1)}, bf16[32,16,128]{2,0,1:T(8,128)(2,1)S(1)}, u32[]{:S(2)}, u32[]{:S(2)}) collective-permute-start(bf16[32,16,128]{2,0,1:T(8,128)(2,1)S(1)} %get-tuple-element.66), channel_id=1, source_target_pairs={{1,2},{2,1},{5,6},{6,5},{9,10},{10,9},{13,14},{14,13},{17,18},{18,... | collective-permute-start | bytes 393224 | tf_op jit(solution)/shard_map/ppermute | solution.py:26
  10.0 7.7 %collective-permute-start.2 = (bf16[16,64,128]{2,0,1:T(8,128)(2,1)S(1)}, bf16[16,64,128]{2,0,1:T(8,128)(2,1)S(1)}, u32[]{:S(2)}, u32[]{:S(2)}) collective-permute-start(bf16[16,64,128]{2,0,1:T(8,128)(2,1)S(1)} %get-tuple-element.49), channel_id=1, source_target_pairs={{4,8},{8,4},{5,9},{9,5},{6,10},{10,6},{7,11},{11,7},{20,24},{24,20... | collective-permute-start | bytes 786440 | tf_op jit(solution)/shard_map/ppermute | solution.py:26
  12.0 5.8 %collective-permute-start.3 = (bf16[16,64,128]{2,0,1:T(8,128)(2,1)S(1)}, bf16[16,64,128]{2,0,1:T(8,128)(2,1)S(1)}, u32[]{:S(2)}, u32[]{:S(2)}) collective-permute-start(bf16[16,64,128]{2,0,1:T(8,128)(2,1)S(1)} %get-tuple-element.50), channel_id=1, source_target_pairs={{0,4},{4,0},{8,12},{12,8},{1,5},{5,1},{9,13},{13,9},{2,6},{6,2},{1... | collective-permute-start | bytes 786440 | tf_op jit(solution)/shard_map/ppermute | solution.py:25
  14.3 3.6 %copy-start.3 = (f32[3,32,64]{2,1,0:T(8,128)S(1)}, f32[3,32,64]{2,1,0:T(8,128)}, u32[]{:S(2)}) copy-start(f32[3,32,64]{2,1,0:T(8,128)} %get-tuple-element.12) | copy-start | bytes 73732
  27.9 2.9 %copy-start.4 = (s32[3,4,4]{2,1,0:T(4,128)S(1)}, s32[3,4,4]{2,1,0:T(4,128)}, u32[]{:S(2)}) copy-start(s32[3,4,4]{2,1,0:T(4,128)} %param.8) | copy-start | bytes 580
  27.9 3.0 %copy-start.5 = (s32[3,4,4]{2,1,0:T(4,128)S(1)}, s32[3,4,4]{2,1,0:T(4,128)}, u32[]{:S(2)}) copy-start(s32[3,4,4]{2,1,0:T(4,128)} %param.9) | copy-start | bytes 580
  28.4 2.3 %collective-permute-start.5 = (s16[16,65,128]{2,0,1:T(8,128)(2,1)S(1)}, s16[16,65,128]{2,0,1:T(8,128)(2,1)S(1)}, u32[]{:S(2)}, u32[]{:S(2)}) collective-permute-start(s16[16,65,128]{2,0,1:T(8,128)(2,1)S(1)} %get-tuple-element.42), channel_id=1, source_target_pairs={{0,4},{4,0},{8,12},{12,8},{1,5},{5,1},{9,13},{13,9},{2,6},{6,2},{1... | collective-permute-start | bytes 798728 | tf_op jit(solution)/shard_map/ppermute | solution.py:25
  28.5 7.7 %collective-permute-start.4 = (s16[16,65,128]{2,0,1:T(8,128)(2,1)S(1)}, s16[16,65,128]{2,0,1:T(8,128)(2,1)S(1)}, u32[]{:S(2)}, u32[]{:S(2)}) collective-permute-start(s16[16,65,128]{2,0,1:T(8,128)(2,1)S(1)} %get-tuple-element.41), channel_id=1, source_target_pairs={{4,8},{8,4},{5,9},{9,5},{6,10},{10,6},{7,11},{11,7},{20,24},{24,20... | collective-permute-start | bytes 798728 | tf_op jit(solution)/shard_map/ppermute | solution.py:26
  36.5 4.4 %collective-permute-start.9 = (f32[375]{0:T(512)S(1)}, f32[375]{0:T(512)S(1)}, u32[]{:S(2)}, u32[]{:S(2)}) collective-permute-start(f32[375]{0:T(512)S(1)} %pad_maximum_fusion.3), channel_id=1, source_target_pairs={{0,16},{16,0},{1,17},{17,1},{2,18},{18,2},{3,19},{19,3},{4,20},{20... | collective-permute-start | bytes 4508 | tf_op jit(solution)/shard_map/ppermute | solution.py:124
  38.6 5.1 %collective-permute-start.6 = (s16[32,17,128]{2,0,1:T(8,128)(2,1)S(1)}, s16[32,17,128]{2,0,1:T(8,128)(2,1)S(1)}, u32[]{:S(2)}, u32[]{:S(2)}) collective-permute-start(s16[32,17,128]{2,0,1:T(8,128)(2,1)S(1)} %get-tuple-element.57), channel_id=1, source_target_pairs={{0,1},{1,0},{2,3},{3,2},{4,5},{5,4},{6,7},{7,6},{8,9},{9,8},{10,11... | collective-permute-start | bytes 417800 | tf_op jit(solution)/shard_map/ppermute | solution.py:25
  38.7 6.9 %collective-permute-start.7 = (s16[32,17,128]{2,0,1:T(8,128)(2,1)S(1)}, s16[32,17,128]{2,0,1:T(8,128)(2,1)S(1)}, u32[]{:S(2)}, u32[]{:S(2)}) collective-permute-start(s16[32,17,128]{2,0,1:T(8,128)(2,1)S(1)} %get-tuple-element.58), channel_id=1, source_target_pairs={{1,2},{2,1},{5,6},{6,5},{9,10},{10,9},{13,14},{14,13},{17,18},{18,... | collective-permute-start | bytes 417800 | tf_op jit(solution)/shard_map/ppermute | solution.py:26
  46.1 6.6 %copy-start = (f32[32,32,128]{2,1,0:T(8,128)S(1)}, f32[32,32,128]{2,1,0:T(8,128)}, u32[]{:S(2)}) copy-start(f32[32,32,128]{2,1,0:T(8,128)} %param.5) | copy-start | bytes 1572868
  46.1 6.5 %collective-permute-start.8 = (s16[32,33,128]{2,0,1:T(8,128)(2,1)S(1)}, s16[32,33,128]{2,0,1:T(8,128)(2,1)S(1)}, u32[]{:S(2)}, u32[]{:S(2)}) collective-permute-start(s16[32,33,128]{2,0,1:T(8,128)(2,1)S(1)} %pad_add_fusion), channel_id=1, source_target_pairs={{0,16},{16,0},{1,17},{17,1},{2,18},{18,2},{3,19},{19,3},{4,20},{20... | collective-permute-start | bytes 811016 | tf_op jit(solution)/shard_map/ppermute | solution.py:189
  53.4 5.0 %collective-permute-start.10 = (bf16[32,16,128]{2,0,1:T(8,128)(2,1)S(1)}, bf16[32,16,128]{2,0,1:T(8,128)(2,1)S(1)}, u32[]{:S(2)}, u32[]{:S(2)}) collective-permute-start(bf16[32,16,128]{2,0,1:T(8,128)(2,1)S(1)} %get-tuple-element.61), channel_id=1, source_target_pairs={{0,1},{1,0},{2,3},{3,2},{4,5},{5,4},{6,7},{7,6},{8,9},{9,8},{10,11... | collective-permute-start | bytes 393224 | tf_op jit(solution)/shard_map/ppermute | solution.py:25
  53.5 6.9 %collective-permute-start.11 = (bf16[32,16,128]{2,0,1:T(8,128)(2,1)S(1)}, bf16[32,16,128]{2,0,1:T(8,128)(2,1)S(1)}, u32[]{:S(2)}, u32[]{:S(2)}) collective-permute-start(bf16[32,16,128]{2,0,1:T(8,128)(2,1)S(1)} %get-tuple-element.62), channel_id=1, source_target_pairs={{1,2},{2,1},{5,6},{6,5},{9,10},{10,9},{13,14},{14,13},{17,18},{18,... | collective-permute-start | bytes 393224 | tf_op jit(solution)/shard_map/ppermute | solution.py:26
  60.5 7.7 %collective-permute-start.12 = (bf16[16,64,128]{2,0,1:T(8,128)(2,1)S(1)}, bf16[16,64,128]{2,0,1:T(8,128)(2,1)S(1)}, u32[]{:S(2)}, u32[]{:S(2)}) collective-permute-start(bf16[16,64,128]{2,0,1:T(8,128)(2,1)S(1)} %get-tuple-element.45), channel_id=1, source_target_pairs={{4,8},{8,4},{5,9},{9,5},{6,10},{10,6},{7,11},{11,7},{20,24},{24,20... | collective-permute-start | bytes 786440 | tf_op jit(solution)/shard_map/ppermute | solution.py:26
  62.6 5.5 %collective-permute-start.13 = (bf16[16,64,128]{2,0,1:T(8,128)(2,1)S(1)}, bf16[16,64,128]{2,0,1:T(8,128)(2,1)S(1)}, u32[]{:S(2)}, u32[]{:S(2)}) collective-permute-start(bf16[16,64,128]{2,0,1:T(8,128)(2,1)S(1)} %get-tuple-element.46), channel_id=1, source_target_pairs={{0,4},{4,0},{8,12},{12,8},{1,5},{5,1},{9,13},{13,9},{2,6},{6,2},{1... | collective-permute-start | bytes 786440 | tf_op jit(solution)/shard_map/ppermute | solution.py:25
  78.6 7.7 %collective-permute-start.14 = (s16[16,65,128]{2,0,1:T(8,128)(2,1)S(1)}, s16[16,65,128]{2,0,1:T(8,128)(2,1)S(1)}, u32[]{:S(2)}, u32[]{:S(2)}) collective-permute-start(s16[16,65,128]{2,0,1:T(8,128)(2,1)S(1)} %get-tuple-element.37), channel_id=1, source_target_pairs={{4,8},{8,4},{5,9},{9,5},{6,10},{10,6},{7,11},{11,7},{20,24},{24,20... | collective-permute-start | bytes 798728 | tf_op jit(solution)/shard_map/ppermute | solution.py:26
  80.6 5.8 %collective-permute-start.15 = (s16[16,65,128]{2,0,1:T(8,128)(2,1)S(1)}, s16[16,65,128]{2,0,1:T(8,128)(2,1)S(1)}, u32[]{:S(2)}, u32[]{:S(2)}) collective-permute-start(s16[16,65,128]{2,0,1:T(8,128)(2,1)S(1)} %get-tuple-element.38), channel_id=1, source_target_pairs={{0,4},{4,0},{8,12},{12,8},{1,5},{5,1},{9,13},{13,9},{2,6},{6,2},{1... | collective-permute-start | bytes 798728 | tf_op jit(solution)/shard_map/ppermute | solution.py:25
  87.1 5.1 %collective-permute-start.16 = (s16[32,17,128]{2,0,1:T(8,128)(2,1)S(1)}, s16[32,17,128]{2,0,1:T(8,128)(2,1)S(1)}, u32[]{:S(2)}, u32[]{:S(2)}) collective-permute-start(s16[32,17,128]{2,0,1:T(8,128)(2,1)S(1)} %get-tuple-element.53), channel_id=1, source_target_pairs={{0,1},{1,0},{2,3},{3,2},{4,5},{5,4},{6,7},{7,6},{8,9},{9,8},{10,11... | collective-permute-start | bytes 417800 | tf_op jit(solution)/shard_map/ppermute | solution.py:25
  87.2 6.9 %collective-permute-start.17 = (s16[32,17,128]{2,0,1:T(8,128)(2,1)S(1)}, s16[32,17,128]{2,0,1:T(8,128)(2,1)S(1)}, u32[]{:S(2)}, u32[]{:S(2)}) collective-permute-start(s16[32,17,128]{2,0,1:T(8,128)(2,1)S(1)} %get-tuple-element.54), channel_id=1, source_target_pairs={{1,2},{2,1},{5,6},{6,5},{9,10},{10,9},{13,14},{14,13},{17,18},{18,... | collective-permute-start | bytes 417800 | tf_op jit(solution)/shard_map/ppermute | solution.py:26
  94.6 6.5 %collective-permute-start.18 = (s16[32,33,128]{2,0,1:T(8,128)(2,1)S(1)}, s16[32,33,128]{2,0,1:T(8,128)(2,1)S(1)}, u32[]{:S(2)}, u32[]{:S(2)}) collective-permute-start(s16[32,33,128]{2,0,1:T(8,128)(2,1)S(1)} %pad_add_fusion.1), channel_id=1, source_target_pairs={{0,16},{16,0},{1,17},{17,1},{2,18},{18,2},{3,19},{19,3},{4,20},{20... | collective-permute-start | bytes 811016 | tf_op jit(solution)/shard_map/ppermute | solution.py:189
  (4 other events, 6.0 us)
